TPU v7x, 32 devices: a whole 2x2x4 slice. The times are simulated.
32 devices in a mesh: dp: 2 (over core), seq: 4 (over z), mp: 4 (over y, x).
Axes of the slice: x: 2, y: 2, z: 4, core: 2. Of those that a mesh axis runs over, the one named last changes fastest.
Arguments:
- tokens: bfloat16 [2, 4096, 2304], P('dp', 'seq'), may hold values from -27 to 27
- cotangent: bfloat16 [2, 4096, 2304], P('dp', 'seq'), may hold values from -6 to 6
- pre_attn_gain: bfloat16 [2304], P(('dp', 'seq')), may hold values from 0.099609375 to 1.8984375
- w_query: bfloat16 [2304, 2048], P(('dp', 'seq'), 'mp'), may hold values from -4 to 4
- w_key: bfloat16 [2304, 1024], P(('dp', 'seq')), may hold values from -2 to 2
- w_value: bfloat16 [2304, 1024], P(('dp', 'seq')), may hold values from -0.125 to 0.125
- w_out: bfloat16 [2048, 2304], P('mp', ('dp', 'seq')), may hold values from -0.375 to 0.375
- post_attn_gain: bfloat16 [2304], P(('dp', 'seq')), may hold values from 0.099609375 to 1.8984375
- pre_ffw_gain: bfloat16 [2304], P(('dp', 'seq')), may hold values from 0.099609375 to 1.8984375
- w_gate: bfloat16 [2304, 9216], P(('dp', 'seq'), 'mp'), may hold values from -0.125 to 0.125
- w_up: bfloat16 [2304, 9216], P(('dp', 'seq'), 'mp'), may hold values from -0.125 to 0.125
- w_down: bfloat16 [9216, 2304], P('mp', ('dp', 'seq')), may hold values from -0.0625 to 0.0625
- post_ffw_gain: bfloat16 [2304], P(('dp', 'seq')), may hold values from 0.099609375 to 1.8984375
Outputs:
- output: bfloat16 [2, 4096, 2304], P('dp', ('seq', 'mp'))
- tokens_grad: bfloat16 [2, 4096, 2304], P('dp', ('seq', 'mp'))
- pre_attn_gain_grad: float32 [2304], P(('dp', 'seq'))
- w_query_grad: float32 [2304, 2048], P(('dp', 'seq'), 'mp')
- w_key_grad: float32 [2304, 1024], P(('dp', 'seq'))
- w_value_grad: float32 [2304, 1024], P(('dp', 'seq'))
- w_out_grad: float32 [2048, 2304], P('mp', ('dp', 'seq'))
- post_attn_gain_grad: float32 [2304], P(('dp', 'seq'))
- pre_ffw_gain_grad: float32 [2304], P(('dp', 'seq'))
- w_gate_grad: float32 [2304, 9216], P(('dp', 'seq'), 'mp')
- w_up_grad: float32 [2304, 9216], P(('dp', 'seq'), 'mp')
- w_down_grad: float32 [9216, 2304], P('mp', ('dp', 'seq'))
- post_ffw_gain_grad: float32 [2304], P(('dp', 'seq'))
All inputs are finite; a program needn't handle non-finite values.
Results may differ from a plain program's by a relative error of at most 0.022.
The roundings to bfloat16 on the way count: a program that leaves them out, or rounds other values in their place, can miss the bound.
Values may be sent and summed in bfloat16 or wider, within the bound.
A program may use at most 256 MiB of HBM per device.

v0:
```python
import jax
import jax.numpy as jnp
from jax import lax
from jax.sharding import PartitionSpec as P

Q_HEADS = 8
KV_HEADS = 4
HEAD_DIM = 256
WINDOW = 4096


EPSILON = 1e-06
SOFT_CAP = 50.0
ROPE_BASE = 10000.0
MASKED = -1e30


def shifted(x, axis, by):
    devices = lax.axis_size(axis)
    pairs = [(i, i + by) for i in range(devices) if 0 <= i + by < devices]
    return lax.ppermute(x, axis, pairs)


def rms_scale(vector):
    return lax.rsqrt(jnp.mean(vector * vector, axis=-1, keepdims=True) + EPSILON)


def norm_back(grad_in, unit, scale, gain):
    gain_grad = jnp.sum(grad_in * unit, axis=0)
    unit_grad = grad_in * gain
    vector_grad = scale * (unit_grad - unit * jnp.mean(unit_grad * unit, axis=-1, keepdims=True))
    return (vector_grad, gain_grad)


def rotary(vector, cosine, sine, direction):
    half_dim = vector.shape[-1] // 2
    first_half = vector[..., :half_dim]
    second_half = vector[..., half_dim:]
    return jnp.concatenate(
        [
            first_half * cosine - direction * (second_half * sine),
            second_half * cosine + direction * (first_half * sine),
        ],
        axis=-1,
    )


def row_sum(term_fn, span_len):
    summed = lax.psum(term_fn(0, span_len), "mp")
    return summed


def row_share(rows_hand):
    share_len = rows_hand.shape[0] // lax.axis_size("mp")
    own_share = lax.dynamic_slice_in_dim(rows_hand, lax.axis_index("mp") * share_len, share_len, 0)
    return own_share


def shards(
    tokens,
    cotangent,
    pre_attn_gain,
    w_query,
    w_key,
    w_value,
    w_out,
    post_attn_gain,
    pre_ffw_gain,
    w_gate,
    w_up,
    w_down,
    post_ffw_gain,
):
    local_heads = w_query.shape[1] // HEAD_DIM
    group_size = Q_HEADS // KV_HEADS
    kv_heads_local = max(1, local_heads // group_size)
    repeat = local_heads // kv_heads_local
    kv_width = kv_heads_local * HEAD_DIM
    kv_first = lax.axis_index("mp") * local_heads // group_size
    key_part = lax.dynamic_slice_in_dim(w_key, kv_first * HEAD_DIM, kv_width, 1)
    value_part = lax.dynamic_slice_in_dim(w_value, kv_first * HEAD_DIM, kv_width, 1)
    attn_gathered = (
        lax.all_gather(pre_attn_gain, ("dp", "seq"), axis=0, tiled=True),
        lax.all_gather(w_query, ("dp", "seq"), axis=0, tiled=True),
        lax.all_gather(key_part, ("dp", "seq"), axis=0, tiled=True),
        lax.all_gather(value_part, ("dp", "seq"), axis=0, tiled=True),
        lax.all_gather(w_out, ("dp", "seq"), axis=1, tiled=True),
        lax.all_gather(post_attn_gain, ("dp", "seq"), axis=0, tiled=True),
    )
    gain_one = attn_gathered[0].astype(jnp.float32)
    query_w = attn_gathered[1]
    key_w = attn_gathered[2]
    value_w = attn_gathered[3]
    out_w = attn_gathered[4]
    gain_two = attn_gathered[5].astype(jnp.float32)
    inputs = tokens[0].astype(jnp.float32)
    span_len = inputs.shape[0]
    block_len = min(512, span_len)
    block_count = span_len // block_len
    seq_index = lax.axis_index("seq")
    positions = seq_index * span_len + jnp.arange(span_len, dtype=jnp.int32)
    half_dim = HEAD_DIM // 2
    frequency = ROPE_BASE ** (-jnp.arange(half_dim, dtype=jnp.float32) * 2.0 / HEAD_DIM)
    angles = positions.astype(jnp.float32)[:, None, None] * frequency
    cosine = jnp.cos(angles)
    sine = jnp.sin(angles)
    scale_one = rms_scale(inputs)
    unit_one = inputs * scale_one
    normed_one = (unit_one * gain_one).astype(jnp.bfloat16)
    query_lin = jnp.dot(normed_one, query_w, preferred_element_type=jnp.float32).reshape(
        span_len, local_heads, HEAD_DIM
    )
    queries = (rotary(query_lin, cosine, sine, 1.0) * HEAD_DIM ** (-0.5)).astype(jnp.bfloat16)
    key_lin = jnp.dot(normed_one, key_w, preferred_element_type=jnp.float32).reshape(
        span_len, kv_heads_local, HEAD_DIM
    )
    keys_own = rotary(key_lin, cosine, sine, 1.0).astype(jnp.bfloat16).reshape(span_len, kv_width)
    values_own = jnp.dot(normed_one, value_w, preferred_element_type=jnp.float32).astype(
        jnp.bfloat16
    )
    own_pair = jnp.stack([keys_own, values_own])
    hop_count = min(WINDOW // span_len, lax.axis_size("seq") - 1)
    arrived = [own_pair]
    for distance in range(1, hop_count + 1):
        arrived.insert(0, shifted(own_pair, "seq", distance))
    window_pair = jnp.concatenate(arrived, axis=1)
    key_count = (hop_count + 1) * span_len
    keys_all = window_pair[0].reshape(key_count, kv_heads_local, HEAD_DIM)
    values_all = window_pair[1].reshape(key_count, kv_heads_local, HEAD_DIM)
    key_pos = (seq_index - hop_count) * span_len + jnp.arange(key_count, dtype=jnp.int32)

    def scores_at(start):
        query_block = lax.dynamic_slice_in_dim(queries, start, block_len, 0).reshape(
            block_len, kv_heads_local, repeat, HEAD_DIM
        )
        raw_scores = jnp.einsum(
            "qgrd,kgd->grqk", query_block, keys_all, preferred_element_type=jnp.float32
        )
        bounded = jnp.tanh(raw_scores / SOFT_CAP)
        query_pos = seq_index * span_len + start + jnp.arange(block_len, dtype=jnp.int32)
        distance_grid = query_pos[:, None] - key_pos[None, :]
        inside = (distance_grid >= 0) & (distance_grid < WINDOW) & (key_pos[None, :] >= 0)
        masked_scores = jnp.where(inside, SOFT_CAP * bounded, MASKED)
        return (query_block, bounded, inside, masked_scores)

    def forward_block(start):
        query_block, bounded, inside, masked_scores = scores_at(start)
        top_score = jnp.max(masked_scores, axis=-1, keepdims=True)
        weights_exp = jnp.exp(masked_scores - top_score)
        row_total = jnp.sum(weights_exp, axis=-1, keepdims=True)
        probs_low = (weights_exp / row_total).astype(jnp.bfloat16)
        block_out = jnp.einsum(
            "grqk,kgd->qgrd", probs_low, values_all, preferred_element_type=jnp.float32
        )
        return (
            block_out.reshape(block_len, local_heads * HEAD_DIM).astype(jnp.bfloat16),
            top_score + jnp.log(row_total),
        )

    starts = jnp.arange(block_count, dtype=jnp.int32) * block_len
    out_blocks, kept_lse = lax.map(forward_block, starts)
    attn_o = out_blocks.reshape(span_len, local_heads * HEAD_DIM)

    def attn_term(start, count):
        return jnp.dot(attn_o, out_w, preferred_element_type=jnp.float32)

    attn = row_sum(attn_term, span_len)
    scale_two = rms_scale(attn)
    unit_two = attn * scale_two
    resid = inputs + unit_two * gain_two
    mlp_gathered = (
        lax.all_gather(pre_ffw_gain, ("dp", "seq"), axis=0, tiled=True),
        lax.all_gather(w_gate, ("dp", "seq"), axis=0, tiled=True),
        lax.all_gather(w_up, ("dp", "seq"), axis=0, tiled=True),
        lax.all_gather(w_down, ("dp", "seq"), axis=1, tiled=True),
        lax.all_gather(post_ffw_gain, ("dp", "seq"), axis=0, tiled=True),
    )
    gain_three = mlp_gathered[0].astype(jnp.float32)
    gate_w = mlp_gathered[1]
    up_w = mlp_gathered[2]
    down_w = mlp_gathered[3]
    gain_four = mlp_gathered[4].astype(jnp.float32)
    scale_three = rms_scale(resid)
    unit_three = resid * scale_three
    normed_two = (unit_three * gain_three).astype(jnp.bfloat16)
    gate_lin = jnp.dot(normed_two, gate_w, preferred_element_type=jnp.float32)
    up_lin = jnp.dot(normed_two, up_w, preferred_element_type=jnp.float32)
    gate_act, gelu_pull = jax.vjp(lambda gate_in: jax.nn.gelu(gate_in, approximate=True), gate_lin)
    hidden = (gate_act * up_lin).astype(jnp.bfloat16)

    def down_term(start, count):
        return jnp.dot(hidden, down_w, preferred_element_type=jnp.float32)

    mixed = row_sum(down_term, span_len)
    scale_four = rms_scale(mixed)
    unit_four = mixed * scale_four
    output = resid + unit_four * gain_four
    grad_out = cotangent[0].astype(jnp.float32)
    dmixed, grad_gain_four = norm_back(grad_out, unit_four, scale_four, gain_four)
    dmixed_low = dmixed.astype(jnp.bfloat16)
    gate_w, up_w, down_w = (
        lax.all_gather(w_gate, ("dp", "seq"), axis=0, tiled=True),
        lax.all_gather(w_up, ("dp", "seq"), axis=0, tiled=True),
        lax.all_gather(w_down, ("dp", "seq"), axis=1, tiled=True),
    )
    grad_down = jnp.einsum("tf,td->fd", hidden, dmixed_low, preferred_element_type=jnp.float32)
    dhidden = jnp.einsum("td,fd->tf", dmixed_low, down_w, preferred_element_type=jnp.float32)
    dgate_low = gelu_pull(dhidden * up_lin)[0].astype(jnp.bfloat16)
    dup_low = (dhidden * gate_act).astype(jnp.bfloat16)
    grad_gate = jnp.einsum("td,tf->df", normed_two, dgate_low, preferred_element_type=jnp.float32)
    grad_up = jnp.einsum("td,tf->df", normed_two, dup_low, preferred_element_type=jnp.float32)

    def ffw_term(start, count):
        return jnp.einsum(
            "tf,df->td", dgate_low, gate_w, preferred_element_type=jnp.float32
        ) + jnp.einsum("tf,df->td", dup_low, up_w, preferred_element_type=jnp.float32)

    dnormed_two = row_sum(ffw_term, span_len)
    dresid_norm, grad_gain_three = norm_back(dnormed_two, unit_three, scale_three, gain_three)
    dresid = grad_out + dresid_norm
    mlp_grads = (
        lax.psum_scatter(
            grad_gain_three.astype(jnp.bfloat16), ("dp", "seq"), scatter_dimension=0, tiled=True
        ).astype(jnp.float32),
        lax.psum_scatter(
            grad_gate.astype(jnp.bfloat16), ("dp", "seq"), scatter_dimension=0, tiled=True
        ).astype(jnp.float32),
        lax.psum_scatter(
            grad_up.astype(jnp.bfloat16), ("dp", "seq"), scatter_dimension=0, tiled=True
        ).astype(jnp.float32),
        lax.psum_scatter(
            grad_down.astype(jnp.bfloat16), ("dp", "seq"), scatter_dimension=1, tiled=True
        ).astype(jnp.float32),
        lax.psum_scatter(
            grad_gain_four.astype(jnp.bfloat16), ("dp", "seq"), scatter_dimension=0, tiled=True
        ).astype(jnp.float32),
    )
    dattn, grad_gain_two = norm_back(dresid, unit_two, scale_two, gain_two)
    dattn_low = dattn.astype(jnp.bfloat16)
    query_w, key_w, value_w, out_w = (
        lax.all_gather(w_query, ("dp", "seq"), axis=0, tiled=True),
        lax.all_gather(key_part, ("dp", "seq"), axis=0, tiled=True),
        lax.all_gather(value_part, ("dp", "seq"), axis=0, tiled=True),
        lax.all_gather(w_out, ("dp", "seq"), axis=1, tiled=True),
    )
    grad_out_w = jnp.einsum("tc,td->cd", attn_o, dattn_low, preferred_element_type=jnp.float32)
    dattn_o = jnp.einsum("td,cd->tc", dattn_low, out_w, preferred_element_type=jnp.float32).astype(
        jnp.bfloat16
    )

    def backward_block(carry, block_in):
        start, lse_block, dout_block = block_in
        query_block, bounded, inside, masked_scores = scores_at(start)
        probs = jnp.exp(masked_scores - lse_block)
        probs_low = probs.astype(jnp.bfloat16)
        dout_heads = dout_block.reshape(block_len, kv_heads_local, repeat, HEAD_DIM)
        dprobs = jnp.einsum(
            "qgrd,kgd->grqk", dout_heads, values_all, preferred_element_type=jnp.float32
        )
        dvalues = jnp.einsum(
            "grqk,qgrd->kgd", probs_low, dout_heads, preferred_element_type=jnp.float32
        )
        dmasked = probs * (dprobs - jnp.sum(probs * dprobs, axis=-1, keepdims=True))
        draw_low = (jnp.where(inside, dmasked, 0.0) * (1.0 - bounded * bounded)).astype(
            jnp.bfloat16
        )
        dquery = jnp.einsum(
            "grqk,kgd->qgrd", draw_low, keys_all, preferred_element_type=jnp.float32
        )
        dkeys = jnp.einsum(
            "grqk,qgrd->kgd", draw_low, query_block, preferred_element_type=jnp.float32
        )
        return ((carry[0] + dkeys, carry[1] + dvalues), dquery)

    dout_blocks = dattn_o.reshape(block_count, block_len, local_heads * HEAD_DIM)
    zero_grads = jnp.zeros((key_count, kv_heads_local, HEAD_DIM), jnp.float32)
    (dkeys_all, dvalues_all), dquery_blocks = lax.scan(
        backward_block, (zero_grads, zero_grads), (starts, kept_lse, dout_blocks)
    )
    pair_grads = jnp.stack(
        [dkeys_all.reshape(key_count, kv_width), dvalues_all.reshape(key_count, kv_width)]
    )
    own_grads = pair_grads[:, hop_count * span_len :]
    for distance in range(1, hop_count + 1):
        sent_piece = pair_grads[
            :, (hop_count - distance) * span_len : (hop_count - distance + 1) * span_len
        ]
        own_grads = own_grads + shifted(sent_piece.astype(jnp.bfloat16), "seq", -distance).astype(
            sent_piece.dtype
        )
    dkey_rot = own_grads[0].reshape(span_len, kv_heads_local, HEAD_DIM)
    dkey_low = rotary(dkey_rot, cosine, sine, -1.0).reshape(span_len, kv_width).astype(jnp.bfloat16)
    dvalue_low = own_grads[1].astype(jnp.bfloat16)
    dquery_all = dquery_blocks.reshape(span_len, local_heads, HEAD_DIM)
    dquery_low = (
        rotary(dquery_all * HEAD_DIM ** (-0.5), cosine, sine, -1.0)
        .reshape(span_len, local_heads * HEAD_DIM)
        .astype(jnp.bfloat16)
    )
    grad_query = jnp.einsum("td,tc->dc", normed_one, dquery_low, preferred_element_type=jnp.float32)
    grad_key = jnp.einsum("td,tc->dc", normed_one, dkey_low, preferred_element_type=jnp.float32)
    grad_value = jnp.einsum("td,tc->dc", normed_one, dvalue_low, preferred_element_type=jnp.float32)

    def input_term(start, count):
        partial_sum = jnp.einsum(
            "tc,dc->td", dquery_low, query_w, preferred_element_type=jnp.float32
        )
        partial_sum = partial_sum + jnp.einsum(
            "tc,dc->td", dkey_low, key_w, preferred_element_type=jnp.float32
        )
        return partial_sum + jnp.einsum(
            "tc,dc->td", dvalue_low, value_w, preferred_element_type=jnp.float32
        )

    dnormed_one = row_sum(input_term, span_len)
    dinput_norm, grad_gain_one = norm_back(dnormed_one, unit_one, scale_one, gain_one)
    tokens_grad = row_share((dresid + dinput_norm).astype(jnp.bfloat16))
    output_rows = row_share(output.astype(jnp.bfloat16))
    attn_grads = (
        lax.psum_scatter(
            grad_gain_one.astype(jnp.bfloat16), ("dp", "seq"), scatter_dimension=0, tiled=True
        ).astype(jnp.float32),
        lax.psum_scatter(
            grad_query.astype(jnp.bfloat16), ("dp", "seq"), scatter_dimension=0, tiled=True
        ).astype(jnp.float32),
        lax.psum_scatter(
            grad_key.astype(jnp.bfloat16), ("dp", "seq"), scatter_dimension=0, tiled=True
        ).astype(jnp.float32),
        lax.psum_scatter(
            grad_value.astype(jnp.bfloat16), ("dp", "seq"), scatter_dimension=0, tiled=True
        ).astype(jnp.float32),
        lax.psum_scatter(
            grad_out_w.astype(jnp.bfloat16), ("dp", "seq"), scatter_dimension=1, tiled=True
        ).astype(jnp.float32),
        lax.psum_scatter(
            grad_gain_two.astype(jnp.bfloat16), ("dp", "seq"), scatter_dimension=0, tiled=True
        ).astype(jnp.float32),
    )
    empty_columns = jnp.zeros((w_key.shape[0], w_key.shape[1]), jnp.float32)
    key_columns = lax.dynamic_update_slice_in_dim(
        empty_columns, attn_grads[2], kv_first * HEAD_DIM, 1
    )
    value_columns = lax.dynamic_update_slice_in_dim(
        empty_columns, attn_grads[3], kv_first * HEAD_DIM, 1
    )
    key_total, value_total = (
        lax.psum(key_columns.astype(jnp.bfloat16), "mp").astype(jnp.float32),
        lax.psum(value_columns.astype(jnp.bfloat16), "mp").astype(jnp.float32),
    )
    gain_one_grad = attn_grads[0]
    gain_two_grad = attn_grads[5]
    gain_three_grad = mlp_grads[0]
    gain_four_grad = mlp_grads[4]
    return (
        output_rows[None],
        tokens_grad[None],
        gain_one_grad,
        attn_grads[1],
        key_total,
        value_total,
        attn_grads[4],
        gain_two_grad,
        gain_three_grad,
        mlp_grads[1],
        mlp_grads[2],
        mlp_grads[3],
        gain_four_grad,
    )


def solution(mesh):
    in_specs = (
        P("dp", "seq", None),
        P("dp", "seq", None),
        P(("dp", "seq")),
        P(("dp", "seq"), "mp"),
        P(("dp", "seq"), None),
        P(("dp", "seq"), None),
        P("mp", ("dp", "seq")),
        P(("dp", "seq")),
        P(("dp", "seq")),
        P(("dp", "seq"), "mp"),
        P(("dp", "seq"), "mp"),
        P("mp", ("dp", "seq")),
        P(("dp", "seq")),
    )
    out_specs = (
        P("dp", ("seq", "mp"), None),
        P("dp", ("seq", "mp"), None),
        P(("dp", "seq")),
        P(("dp", "seq"), "mp"),
        P(("dp", "seq"), None),
        P(("dp", "seq"), None),
        P("mp", ("dp", "seq")),
        P(("dp", "seq")),
        P(("dp", "seq")),
        P(("dp", "seq"), "mp"),
        P(("dp", "seq"), "mp"),
        P("mp", ("dp", "seq")),
        P(("dp", "seq")),
    )
    return jax.shard_map(shards, mesh=mesh, in_specs=in_specs, out_specs=out_specs, check_vma=False)
```

profile of v0, /device:TPU:0, one launch (start us, length us, event | category | flops | bytes accessed | tf_op | source)
XLA Modules:
  0.0 2620.8 jit_solution(14063816057796629568)
XLA Ops:
  16.9 31.9 %all-reduce.9 = (bf16[2304]{0:T(1024)(128)(2,1)S(1)}, bf16[2304]{0:T(1024)(128)(2,1)}, bf16[2304]{0:T(1024)(128)(2,1)}, bf16[2304]{0:T(1024)(128)(2,1)}) all-reduce(bf16[2304]{0:T(1024)(128)(2,1)S(1)} %dynamic-update-slice, bf16[2304]{0:T(1024)(128)(2,1)S(1)} %dynamic-update-slice.1, ...), channel_id=1, replica_groups=mesh['dp'=2,'seq'=4,'mp'=4] {'dp','seq'}, use_global_device_ids=true, to_apply=%add | all-reduce | flops 9216 | bytes 36864
  76.8 33.9 %collective-permute-done.2 = bf16[2,1024,256]{1,2,0:T(8,128)(2,1)} collective-permute-done((bf16[2,1024,256]{1,2,0:T(8,128)(2,1)S(1)}, bf16[2,1024,256]{1,2,0:T(8,128)(2,1)}, u32[]{:S(2)}, u32[]{:S(2)}) %collective-permute-start.2) | collective-permute-done | bytes 1048608 | tf_op jit(solution)/shard_map/ppermute | solution.py:21
  110.7 36.4 %collective-permute-done.1 = bf16[2,1024,256]{1,2,0:T(8,128)(2,1)} collective-permute-done((bf16[2,1024,256]{1,2,0:T(8,128)(2,1)S(1)}, bf16[2,1024,256]{1,2,0:T(8,128)(2,1)}, u32[]{:S(2)}, u32[]{:S(2)}) %collective-permute-start.1) | collective-permute-done | bytes 1048608 | tf_op jit(solution)/shard_map/ppermute | solution.py:21
  147.1 26.8 %collective-permute-done = bf16[2,1024,256]{1,2,0:T(8,128)(2,1)} collective-permute-done((bf16[2,1024,256]{1,2,0:T(8,128)(2,1)S(1)}, bf16[2,1024,256]{1,2,0:T(8,128)(2,1)}, u32[]{:S(2)}, u32[]{:S(2)}) %collective-permute-start) | collective-permute-done | bytes 1048608 | tf_op jit(solution)/shard_map/ppermute | solution.py:21
  173.9 7.7 maximum_maximum_fusion
  190.0 5.7 fusion.94
  197.7 52.9 %while.32 = (s32[]{:T(128)}, bf16[2,512,512]{2,1,0:T(8,128)(2,1)}, f32[2,1,2,512,1]{3,2,4,1,0:T(2,128)S(1)}, s32[2]{0:T(128)S(1)}, s32[]{:T(128)}, /*index=5*/bf...) while((s32[]{:T(128)}, bf16[2,512,512]{2,1,0:T(8,128)(2,1)}, ...), condition=%wide.region_4.5_spmd.clone, body=%wide.region_1.4_spmd.clone.sunk | while | flops 4368641536 | bytes 74526952 | solution.py:161
  203.7 7.1 fusion.226
  210.8 5.9 fusion.227
  216.7 6.6 fusion.228
  229.9 7.1 fusion.226
  237.1 5.9 fusion.227
  243.0 6.6 fusion.228
  250.6 8.2 fusion.162
  261.1 210.7 %all-reduce.17.cloned.1.call-done = f32[1024,2304]{1,0:T(8,128)} async-done(((f32[1024,2304]{1,0:T(8,128)}), f32[1024,2304]{1,0:T(8,128)}) %all-reduce.17.cloned.1.call-update) | async-done | bytes 9437200 | tf_op jit(solution)/shard_map/psum | solution.py:49
  476.2 11.1 multiply_reduce_fusion.7
  487.4 6.8 multiply_convert_fusion.3
  494.2 79.6 %all-gather.16.cloned.1.call-done = bf16[2304,2304]{1,0:T(8,128)(2,1)} async-done(((bf16[288,2304]{1,0:T(8,128)(2,1)}), bf16[2304,2304]{1,0:T(8,128)(2,1)}) %all-gather.16.cloned.1.call-update) | async-done | bytes 10616848 | tf_op jit(solution)/shard_map/all_gather | solution.py:173
  573.8 16.9 fusion.163
  590.7 83.6 %all-gather.18.cloned.1.call-done = bf16[2304,2304]{1,0:T(8,128)(2,1)} async-done(((bf16[288,2304]{1,0:T(8,128)(2,1)}), bf16[2304,2304]{1,0:T(8,128)(2,1)}) %all-gather.18.cloned.1.call-update) | async-done | bytes 10616848 | tf_op jit(solution)/shard_map/all_gather | solution.py:174
  674.3 21.5 multiply_convert_fusion.2
  695.8 79.0 %all-gather.20.cloned.1.call-done = bf16[2304,2304]{0,1:T(8,128)(2,1)} async-done(((bf16[2304,288]{0,1:T(8,128)(2,1)}), bf16[2304,2304]{0,1:T(8,128)(2,1)}) %all-gather.20.cloned.1.call-update) | async-done | bytes 10616848 | tf_op jit(solution)/shard_map/all_gather | solution.py:175
  774.7 16.7 fusion.164
  792.1 186.5 %all-reduce.19.cloned.1.call-done = f32[1024,2304]{1,0:T(8,128)} async-done(((f32[1024,2304]{1,0:T(8,128)}), f32[1024,2304]{1,0:T(8,128)}) %all-reduce.19.cloned.1.call-update) | async-done | bytes 9437200 | tf_op jit(solution)/shard_map/psum | solution.py:49
  983.2 9.3 fusion.92
  992.5 7.7 fusion.81
  1000.2 27.9 %multiply_convert_fusion.1 = (bf16[1024,2304]{1,0:T(8,128)(2,1)}, bf16[1024,2304]{1,0:T(8,128)(2,1)}) fusion(f32[1024,2304]{1,0:T(8,128)} %fusion.163, f32[1024,2304]{1,0:T(8,128)} %get-tuple-element.480, bf16[1024,2304]{1,0:T(8,128)(2,1)} %fusion.81, bf16[2304,2304]{0,1:T(8,128)(2,1)} %all-gather.20.cloned.1.call-done), kind=kOutput, calls=%fused_computation.113 | convolution fusion | flops 10928259072 | bytes 43646976 | tf_op jit(solution)/shard_map/td,fd->tf/dot_general | solution.py:207
  1028.1 17.1 fusion.165
  1045.2 19.7 convolution_add_fusion
  1069.0 184.8 %all-reduce.21.cloned.1.call-done = f32[1024,2304]{1,0:T(8,128)} async-done(((f32[1024,2304]{1,0:T(8,128)}), f32[1024,2304]{1,0:T(8,128)}) %all-reduce.21.cloned.1.call-update) | async-done | bytes 9437200 | tf_op jit(solution)/shard_map/psum | solution.py:49
  1253.8 8.4 multiply_reduce_fusion
  1262.9 12.5 multiply_reduce_fusion.1
  1283.0 149.9 %while.33 = (s32[]{:T(128)}, f32[4096,1,256]{0,2,1:T(8,128)}, f32[4096,1,256]{0,2,1:T(8,128)}, f32[2,512,1,2,256]{4,1,3,2,0:T(8,128)}, s32[2]{0:T(128)S(1)}, /*i...) while((s32[]{:T(128)}, f32[4096,1,256]{0,2,1:T(8,128)}, ...), condition=%wide.region_16.17_spmd.clone, body=%wide.region_14.16_spmd.clone.sunk | while | flops 10844385280 | bytes 246489552 | solution.py:277
  1285.8 9.2 fusion.238
  1299.4 15.7 fusion.240
  1315.1 16.5 fusion.241
  1331.6 8.2 fusion.242
  1339.8 10.6 fusion.243
  1350.5 5.5 fusion.244
  1359.8 9.2 fusion.238
  1373.4 15.7 fusion.240
  1389.1 16.5 fusion.241
  1405.7 9.4 fusion.242
  1415.1 10.6 fusion.243
  1425.7 5.5 fusion.244
  1442.0 25.7 collective-permute-done.5
  1467.6 43.8 %collective-permute-done.4 = bf16[2,1024,256]{1,2,0:T(8,128)(2,1)S(1)} collective-permute-done((bf16[2,1024,256]{1,2,0:T(8,128)(2,1)S(1)}, bf16[2,1024,256]{1,2,0:T(8,128)(2,1)S(1)}, u32[]{:S(2)}, u32[]{:S(2)}) %collective-permute-start.4) | collective-permute-done | bytes 1048608 | tf_op jit(solution)/shard_map/ppermute | solution.py:21
  1517.7 5.1 fusion.105
  1522.9 50.8 %reduce-scatter.10.cloned.1.call-done = bf16[288,256]{1,0:T(8,128)(2,1)} async-done(((bf16[2304,256]{1,0:T(8,128)(2,1)}), bf16[288,256]{1,0:T(8,128)(2,1)}) %reduce-scatter.10.cloned.1.call-update) | async-done | bytes 147472 | tf_op jit(solution)/shard_map/reduce_scatter | solution.py:326
  1574.6 37.4 %reduce-scatter.12.cloned.1.call-done = bf16[288,256]{1,0:T(8,128)(2,1)} async-done(((bf16[2304,256]{1,0:T(8,128)(2,1)}), bf16[288,256]{1,0:T(8,128)(2,1)}) %reduce-scatter.12.cloned.1.call-update) | async-done | bytes 147472 | tf_op jit(solution)/shard_map/reduce_scatter | solution.py:329
  1622.6 6.9 fusion.102
  1629.8 6.9 convolution_convert_fusion.3
  1643.6 6.5 add_add_fusion
  1650.4 16.9 convolution_convert_fusion.2
  1667.4 16.9 convolution_convert_fusion.1
  1684.6 16.9 convolution_convert_fusion
  1710.4 16.4 reduce-scatter.8.cloned.1.call-done
  1728.6 54.2 %reduce-scatter.14.cloned.1.call-done = bf16[512,288]{0,1:T(8,128)(2,1)} async-done(((bf16[512,2304]{0,1:T(8,128)(2,1)}), bf16[512,288]{0,1:T(8,128)(2,1)}) %reduce-scatter.14.cloned.1.call-update) | async-done | bytes 294928 | tf_op jit(solution)/shard_map/reduce_scatter | solution.py:332
  1784.7 189.8 %all-reduce.23.cloned.1.call-done = f32[1024,2304]{1,0:T(8,128)} async-done(((f32[1024,2304]{1,0:T(8,128)}), f32[1024,2304]{1,0:T(8,128)}) %all-reduce.23.cloned.1.call-update) | async-done | bytes 9437200 | tf_op jit(solution)/shard_map/psum | solution.py:49
  1974.5 11.2 multiply_reduce_fusion.2
  1985.8 32.9 %all-reduce.8 = (bf16[2304]{0:T(1024)(128)(2,1)S(1)}, bf16[2304]{0:T(1024)(128)(2,1)S(1)}, bf16[2304]{0:T(1024)(128)(2,1)S(1)}, bf16[2304]{0:T(1024)(128)(2,1)S(1)}) all-reduce(bf16[2304]{0:T(1024)(128)(2,1)S(1)} %get-tuple-element.396, ...), channel_id=2, replica_groups=mesh['dp'=2,'seq'=4,'mp'=4] {'dp','seq'}, use_global_device_ids=true, to_apply=%region_20.21.clone | all-reduce | flops 9216 | bytes 36864
  2024.7 161.9 %reduce-scatter.16.cloned.1.call-done = bf16[288,2304]{1,0:T(8,128)(2,1)} async-done(((bf16[2304,2304]{1,0:T(8,128)(2,1)}), bf16[288,2304]{1,0:T(8,128)(2,1)}) %reduce-scatter.16.cloned.1.call-update) | async-done | bytes 1327120 | tf_op jit(solution)/shard_map/reduce_scatter | solution.py:225
  2189.6 209.0 %reduce-scatter.18.cloned.1.call-done = bf16[288,2304]{1,0:T(8,128)(2,1)} async-done(((bf16[2304,2304]{1,0:T(8,128)(2,1)}), bf16[288,2304]{1,0:T(8,128)(2,1)}) %reduce-scatter.18.cloned.1.call-update) | async-done | bytes 1327120 | tf_op jit(solution)/shard_map/reduce_scatter | solution.py:228
  2401.6 209.2 %reduce-scatter.20.cloned.1.call-done = bf16[2304,288]{0,1:T(8,128)(2,1)} async-done(((bf16[2304,2304]{0,1:T(8,128)(2,1)}), bf16[2304,288]{0,1:T(8,128)(2,1)}) %reduce-scatter.20.cloned.1.call-update) | async-done | bytes 1327120 | tf_op jit(solution)/shard_map/reduce_scatter | solution.py:231
  (311 shorter events, 151.7 us)
Async XLA Ops:
  7.2 45.1 %all-gather.10.cloned.1.call-start = ((), (), s32[]{:S(2)}) async-start(), calls=%async_computation.8 | async-start | bytes 1327104 | tf_op jit(solution)/shard_map/all_gather | solution.py:85
  9.0 51.5 %all-gather.12.cloned.1.call-start = ((), (), s32[]{:S(2)}) async-start(), calls=%async_computation.9 | async-start | bytes 1327104 | tf_op jit(solution)/shard_map/all_gather | solution.py:86
  10.6 175.2 %all-gather.8.cloned.1.call-start = ((), (), s32[]{:S(2)}) async-start(), calls=%async_computation.7 | async-start | bytes 2654208 | tf_op jit(solution)/shard_map/all_gather | solution.py:84
  11.4 239.3 %all-gather.14.cloned.1.call-start = ((), (), s32[]{:S(2)}) async-start(), calls=%async_computation.10 | async-start | bytes 2654208 | tf_op jit(solution)/shard_map/all_gather | solution.py:87
  48.8 141.2 %copy-start.41 = (f32[2304]{0:T(1024)}, f32[2304]{0:T(1024)S(1)}, u32[]{:S(2)}) copy-start(f32[2304]{0:T(1024)S(1)} %convert_element_type.251) | copy-start | bytes 27652
  48.8 26.0 copy-start.51
  48.8 26.0 copy-start.33
  52.2 137.8 %copy-start.46 = (f32[1024]{0:T(1024)}, f32[1024]{0:T(1024)S(1)}, u32[]{:S(2)}) copy-start(f32[1024]{0:T(1024)S(1)} %add_rsqrt_fusion.3) | copy-start | bytes 12292
  64.8 45.8 %collective-permute-start.2 = (bf16[2,1024,256]{1,2,0:T(8,128)(2,1)S(1)}, bf16[2,1024,256]{1,2,0:T(8,128)(2,1)}, u32[]{:S(2)}, u32[]{:S(2)}) collective-permute-start(bf16[2,1024,256]{1,2,0:T(8,128)(2,1)S(1)} %pad_maximum_fusion.1), channel_id=1, source_target_pairs={{0,4},{4,8},{8,12},{1,5},{5,9},{9,13},{2,6},{6,10},{10,14},{3,7},{... | collective-permute-start | bytes 3145736 | tf_op jit(solution)/shard_map/ppermute | solution.py:21
  69.2 77.9 %collective-permute-start.1 = (bf16[2,1024,256]{1,2,0:T(8,128)(2,1)S(1)}, bf16[2,1024,256]{1,2,0:T(8,128)(2,1)}, u32[]{:S(2)}, u32[]{:S(2)}) collective-permute-start(bf16[2,1024,256]{1,2,0:T(8,128)(2,1)S(1)} %pad_maximum_fusion.1), channel_id=1, source_target_pairs={{0,8},{4,12},{1,9},{5,13},{2,10},{6,14},{3,11},{7,15},{16,24},{20,... | collective-permute-start | bytes 3145736 | tf_op jit(solution)/shard_map/ppermute | solution.py:21
  72.2 101.7 %collective-permute-start = (bf16[2,1024,256]{1,2,0:T(8,128)(2,1)S(1)}, bf16[2,1024,256]{1,2,0:T(8,128)(2,1)}, u32[]{:S(2)}, u32[]{:S(2)}) collective-permute-start(bf16[2,1024,256]{1,2,0:T(8,128)(2,1)S(1)} %pad_maximum_fusion.1), channel_id=1, source_target_pairs={{0,12},{1,13},{2,14},{3,15},{16,28},{17,29},{18,30},{19,31}} | collective-permute-start | bytes 3145736 | tf_op jit(solution)/shard_map/ppermute | solution.py:21
  74.5 397.3 %all-reduce.17.cloned.1.call-start = ((), (), s32[]{:S(2)}) async-start(), calls=%async_computation.11 | async-start | bytes 18874368 | tf_op jit(solution)/shard_map/psum | solution.py:49
  76.7 119.0 %copy-start.15 = (f32[1024,128]{0,1:T(8,128)}, f32[1024,128]{0,1:T(8,128)S(1)}, u32[]{:S(2)}) copy-start(f32[1024,128]{0,1:T(8,128)S(1)} %get-tuple-element.475) | copy-start | bytes 1572868
  76.7 119.0 %copy-start.17 = (f32[1024,128]{0,1:T(8,128)}, f32[1024,128]{0,1:T(8,128)S(1)}, u32[]{:S(2)}) copy-start(f32[1024,128]{0,1:T(8,128)S(1)} %get-tuple-element.476) | copy-start | bytes 1572868
  258.9 314.9 %all-gather.16.cloned.1.call-start = ((), (), s32[]{:S(2)}) async-start(), calls=%async_computation.12 | async-start | bytes 11943936 | tf_op jit(solution)/shard_map/all_gather | solution.py:173
  259.5 414.8 %all-gather.18.cloned.1.call-start = ((), (), s32[]{:S(2)}) async-start(), calls=%async_computation.13 | async-start | bytes 11943936 | tf_op jit(solution)/shard_map/all_gather | solution.py:174
  260.2 514.5 %all-gather.20.cloned.1.call-start = ((), (), s32[]{:S(2)}) async-start(), calls=%async_computation.14 | async-start | bytes 11943936 | tf_op jit(solution)/shard_map/all_gather | solution.py:175
  261.0 717.7 %all-reduce.19.cloned.1.call-start = ((), (), s32[]{:S(2)}) async-start(), calls=%async_computation.15 | async-start | bytes 18874368 | tf_op jit(solution)/shard_map/psum | solution.py:49
  261.0 226.3 %copy-start.27 = (f32[2304]{0:T(1024)}, f32[2304]{0:T(1024)S(1)}, u32[]{:S(2)}) copy-start(f32[2304]{0:T(1024)S(1)} %convert_element_type.258) | copy-start | bytes 27652
  261.1 226.3 %copy-start.31 = (f32[2304]{0:T(1024)}, f32[2304]{0:T(1024)S(1)}, u32[]{:S(2)}) copy-start(f32[2304]{0:T(1024)S(1)} %convert_element_type.259) | copy-start | bytes 27652
  476.2 11.2 copy-start.35
  487.3 103.3 %copy-start.37 = (f32[1024]{0:T(1024)}, f32[1024]{0:T(1024)S(1)}, u32[]{:S(2)}) copy-start(f32[1024]{0:T(1024)S(1)} %add_rsqrt_fusion.1) | copy-start | bytes 12292
  791.5 462.3 %all-reduce.21.cloned.1.call-start = ((), (), s32[]{:S(2)}) async-start(), calls=%async_computation.16 | async-start | bytes 18874368 | tf_op jit(solution)/shard_map/psum | solution.py:49
  792.1 200.4 %copy-start.29 = (f32[2304]{0:T(1024)}, f32[2304]{0:T(1024)S(1)}, u32[]{:S(2)}) copy-start(f32[2304]{0:T(1024)S(1)} %convert_element_type.262) | copy-start | bytes 27652
  978.7 13.9 slice-start.7
  1064.9 188.8 %copy-start.32 = (f32[2304]{0:T(1024)S(1)}, f32[2304]{0:T(1024)}, u32[]{:S(2)}) copy-start(f32[2304]{0:T(1024)} %copy-done.31) | copy-start | bytes 27652
  1064.9 188.8 %copy-start.38 = (f32[1024]{0:T(1024)S(1)}, f32[1024]{0:T(1024)}, u32[]{:S(2)}) copy-start(f32[1024]{0:T(1024)} %copy-done.37) | copy-start | bytes 12292
  1065.0 508.7 %reduce-scatter.10.cloned.1.call-start = ((), (), s32[]{:S(2)}) async-start(), calls=%async_computation.19 | async-start | bytes 1327104 | tf_op jit(solution)/shard_map/reduce_scatter | solution.py:326
  1068.9 193.2 %copy-start.28 = (f32[2304]{0:T(1024)S(1)}, f32[2304]{0:T(1024)}, u32[]{:S(2)}) copy-start(f32[2304]{0:T(1024)} %copy-done.27) | copy-start | bytes 27652
  1068.9 193.2 %copy-start.36 = (f32[1024]{0:T(1024)S(1)}, f32[1024]{0:T(1024)}, u32[]{:S(2)}) copy-start(f32[1024]{0:T(1024)} %copy-done.35) | copy-start | bytes 12292
  1253.8 21.7 slice-start.2
  1262.9 12.6 slice-start.3
  1262.9 12.6 slice-start.4
  1331.6 18.8 slice-start
  1339.8 10.6 copy-start.22
  1405.7 20.0 slice-start
  1415.1 10.6 slice-start.1
  1415.1 10.6 copy-start.22
  1433.0 78.5 %copy-start.2 = (f32[4096,1,256]{0,2,1:T(8,128)S(1)}, f32[4096,1,256]{0,2,1:T(8,128)}, u32[]{:S(2)}) copy-start(f32[4096,1,256]{0,2,1:T(8,128)} %get-tuple-element.727) | copy-start | bytes 12582916
  1433.0 78.5 %copy-start.9 = (f32[4096,1,256]{0,2,1:T(8,128)S(1)}, f32[4096,1,256]{0,2,1:T(8,128)}, u32[]{:S(2)}) copy-start(f32[4096,1,256]{0,2,1:T(8,128)} %get-tuple-element.728) | copy-start | bytes 12582916
  1437.6 74.6 %copy-start.34 = (f32[1024]{0:T(1024)S(1)}, f32[1024]{0:T(1024)}, u32[]{:S(2)}) copy-start(f32[1024]{0:T(1024)} %copy-done.33) | copy-start | bytes 12292
  1437.6 74.6 %copy-start.52 = (f32[128]{0:T(128)S(1)}, f32[128]{0:T(128)}, u32[]{:S(2)}) copy-start(f32[128]{0:T(128)} %copy-done.51) | copy-start | bytes 1540
  1437.6 30.0 %collective-permute-start.5 = (bf16[2,1024,256]{1,2,0:T(8,128)(2,1)S(1)}, bf16[2,1024,256]{1,2,0:T(8,128)(2,1)S(1)}, u32[]{:S(2)}, u32[]{:S(2)}) collective-permute-start(bf16[2,1024,256]{1,2,0:T(8,128)(2,1)S(1)} %get-tuple-element.463), channel_id=1, source_target_pairs={{12,0},{13,1},{14,2},{15,3},{28,16},{29,17},{30,18},{31,19}} | collective-permute-start | bytes 3145736 | tf_op jit(solution)/shard_map/ppermute | solution.py:21
  1439.1 72.4 %collective-permute-start.4 = (bf16[2,1024,256]{1,2,0:T(8,128)(2,1)S(1)}, bf16[2,1024,256]{1,2,0:T(8,128)(2,1)S(1)}, u32[]{:S(2)}, u32[]{:S(2)}) collective-permute-start(bf16[2,1024,256]{1,2,0:T(8,128)(2,1)S(1)} %get-tuple-element.464), channel_id=1, source_target_pairs={{8,0},{12,4},{9,1},{13,5},{10,2},{14,6},{11,3},{15,7},{24,16},{28,... | collective-permute-start | bytes 3145736 | tf_op jit(solution)/shard_map/ppermute | solution.py:21
  1440.4 74.2 %slice-start.5 = ((s8[4718592]{0:T(1024)(128)(4,1)}), s8[4194304]{0:T(1024)(128)(4,1)S(1)}, s32[]{:S(2)}) async-start(s8[4718592]{0:T(1024)(128)(4,1)} %bitcast.336), calls=%async_computation.31 | async-start | bytes 8388608
  1440.4 74.2 %slice-start.6 = ((s8[4718592]{0:T(1024)(128)(4,1)}), s8[524288]{0:T(1024)(128)(4,1)S(1)}, s32[]{:S(2)}) async-start(s8[4718592]{0:T(1024)(128)(4,1)} %bitcast.336), calls=%async_computation.32 | async-start | bytes 1048576
  1440.4 74.2 %copy-start.42 = (f32[2304]{0:T(1024)S(1)}, f32[2304]{0:T(1024)}, u32[]{:S(2)}) copy-start(f32[2304]{0:T(1024)} %copy-done.41) | copy-start | bytes 27652
  1440.4 74.2 %copy-start.47 = (f32[1024]{0:T(1024)S(1)}, f32[1024]{0:T(1024)}, u32[]{:S(2)}) copy-start(f32[1024]{0:T(1024)} %copy-done.46) | copy-start | bytes 12292
  1440.4 71.0 %collective-permute-start.3 = (bf16[2,1024,256]{1,2,0:T(8,128)(2,1)S(1)}, bf16[2,1024,256]{1,2,0:T(8,128)(2,1)S(1)}, u32[]{:S(2)}, u32[]{:S(2)}) collective-permute-start(bf16[2,1024,256]{1,2,0:T(8,128)(2,1)S(1)} %get-tuple-element.462), channel_id=1, source_target_pairs={{4,0},{8,4},{12,8},{5,1},{9,5},{13,9},{6,2},{10,6},{14,10},{7,3},{... | collective-permute-start | bytes 3145736 | tf_op jit(solution)/shard_map/ppermute | solution.py:21
  1517.6 94.5 %reduce-scatter.12.cloned.1.call-start = ((), (), s32[]{:S(2)}) async-start(), calls=%async_computation.20 | async-start | bytes 1327104 | tf_op jit(solution)/shard_map/reduce_scatter | solution.py:329
  1522.8 98.4 %copy-start.16 = (f32[1024,128]{0,1:T(8,128)S(1)}, f32[1024,128]{0,1:T(8,128)}, u32[]{:S(2)}) copy-start(f32[1024,128]{0,1:T(8,128)} %copy-done.15) | copy-start | bytes 1572868
  1522.8 98.4 %copy-start.18 = (f32[1024,128]{0,1:T(8,128)S(1)}, f32[1024,128]{0,1:T(8,128)}, u32[]{:S(2)}) copy-start(f32[1024,128]{0,1:T(8,128)} %copy-done.17) | copy-start | bytes 1572868
  1522.8 183.1 %all-reduce.25.cloned.1.call-start = ((), (), s32[]{:S(2)}) async-start(), calls=%async_computation.25 | async-start | bytes 2359296 | tf_op jit(solution)/shard_map/psum | solution.py:347
  1574.6 38.5 %copy-start.21 = (bf16[288,1024]{1,0:T(8,128)(2,1)}, bf16[288,1024]{1,0:T(8,128)(2,1)S(1)}, u32[]{:S(2)}) copy-start(bf16[288,1024]{1,0:T(8,128)(2,1)S(1)} %convert_dynamic-update-slice_fusion.1) | copy-start | bytes 1769476
  1613.9 112.9 %reduce-scatter.8.cloned.1.call-start = ((), (), s32[]{:S(2)}) async-start(), calls=%async_computation.18 | async-start | bytes 2654208 | tf_op jit(solution)/shard_map/reduce_scatter | solution.py:323
  1629.6 153.3 %reduce-scatter.14.cloned.1.call-start = ((), (), s32[]{:S(2)}) async-start(), calls=%async_computation.21 | async-start | bytes 2654208 | tf_op jit(solution)/shard_map/reduce_scatter | solution.py:332
  1636.7 337.8 %all-reduce.23.cloned.1.call-start = ((), (), s32[]{:S(2)}) async-start(), calls=%async_computation.17 | async-start | bytes 18874368 | tf_op jit(solution)/shard_map/psum | solution.py:49
  1650.1 536.4 %reduce-scatter.16.cloned.1.call-start = ((), (), s32[]{:S(2)}) async-start(), calls=%async_computation.22 | async-start | bytes 11943936 | tf_op jit(solution)/shard_map/reduce_scatter | solution.py:225
  1667.3 731.2 %reduce-scatter.18.cloned.1.call-start = ((), (), s32[]{:S(2)}) async-start(), calls=%async_computation.23 | async-start | bytes 11943936 | tf_op jit(solution)/shard_map/reduce_scatter | solution.py:228
  1684.3 926.5 %reduce-scatter.20.cloned.1.call-start = ((), (), s32[]{:S(2)}) async-start(), calls=%async_computation.24 | async-start | bytes 11943936 | tf_op jit(solution)/shard_map/reduce_scatter | solution.py:231
  1784.7 201.1 %copy-start.43 = (bf16[2304]{0:T(1024)(128)(2,1)S(1)}, bf16[2304]{0:T(1024)(128)(2,1)}, u32[]{:S(2)}) copy-start(bf16[2304]{0:T(1024)(128)(2,1)} %get-tuple-element.394) | copy-start | bytes 13828
  1784.7 201.1 %copy-start.44 = (bf16[2304]{0:T(1024)(128)(2,1)S(1)}, bf16[2304]{0:T(1024)(128)(2,1)}, u32[]{:S(2)}) copy-start(bf16[2304]{0:T(1024)(128)(2,1)} %get-tuple-element.390) | copy-start | bytes 13828
  1784.7 201.1 %copy-start.45 = (bf16[2304]{0:T(1024)(128)(2,1)S(1)}, bf16[2304]{0:T(1024)(128)(2,1)}, u32[]{:S(2)}) copy-start(bf16[2304]{0:T(1024)(128)(2,1)} %get-tuple-element.392) | copy-start | bytes 13828
  2020.0 593.9 %copy-start.1 = (bf16[288,1024]{1,0:T(8,128)(2,1)S(1)}, bf16[288,1024]{1,0:T(8,128)(2,1)}, u32[]{:S(2)}) copy-start(bf16[288,1024]{1,0:T(8,128)(2,1)} %param.21) | copy-start | bytes 1769476
  (34 other events, 163.1 us)
Sparse Core Ops, SparseCore 0:
  10.2 25.8 all-gather.9
  38.2 22.1 all-gather.11
  62.0 45.8 all-gather.7
  109.4 48.1 all-gather.13
  259.0 212.7 all-reduce.16
  473.3 100.4 all-gather.15
  575.4 98.8 all-gather.17
  675.8 98.8 all-gather.19
  791.6 187.0 all-reduce.18
  1065.1 188.6 all-reduce.20
  1517.8 55.8 reduce-scatter.9
  1576.3 35.6 reduce-scatter.11
  1615.8 54.0 all-reduce.24
  1672.8 53.9 reduce-scatter.7
  1729.6 53.1 reduce-scatter.13
  1786.6 187.8 all-reduce.22
  1976.7 209.7 reduce-scatter.15
  2188.7 209.7 reduce-scatter.17
  2401.0 209.7 reduce-scatter.19
where the time goes:
time: 2630 us; the launch traced here: 2620 us
  waiting for transfers between devices  1920 us (73%)
  matrix products  359 us (14%)
  other arithmetic  187 us (7%)
  blocking collectives  64.8 us (2%)
  local copies, waits for them, and re-layouts  42.7 us (2%)
    psum x4, waiting for transfers between devices, row_sum(): summed = lax.psum(term_fn(0, span_len), 'mp')  772 us
    reduce_scatter x1, waiting for transfers between devices, shards(): lax.psum_scatter(grad_down.astype(jnp.bfloat16), ('dp', 'seq'), scatter_d...  209 us
    reduce_scatter x1, waiting for transfers between devices, shards(): lax.psum_scatter(grad_up.astype(jnp.bfloat16), ('dp', 'seq'), scatter_dim...  209 us
    ppermute x6, waiting for transfers between devices, shifted(): return lax.ppermute(x, axis, pairs)  167 us
    reduce_scatter x1, waiting for transfers between devices, shards(): lax.psum_scatter(grad_gate.astype(jnp.bfloat16), ('dp', 'seq'), scatter_d...  162 us
    all_gather x1, waiting for transfers between devices, shards(): lax.all_gather(w_up, ('dp', 'seq'), axis=0, tiled=True)  83.6 us
    all_gather x1, waiting for transfers between devices, shards(): lax.all_gather(w_gate, ('dp', 'seq'), axis=0, tiled=True)  79.6 us
    all_gather x1, waiting for transfers between devices, shards(): lax.all_gather(w_down, ('dp', 'seq'), axis=1, tiled=True)  79 us
  transfers between devices with their start and end apart: 25, of which 20 were waited for; matrix products, arithmetic and copies ran while one was open for 11% of the time, Pallas kernels for 0%

commit v1 on v0

v1 whole, which is shorter than its diff:
```python
import functools

import jax
import jax.numpy as jnp
from jax import lax
from jax.experimental import pallas as pl
from jax.experimental.pallas import tpu as pltpu
from jax.sharding import PartitionSpec as P

Q_HEADS = 8
KV_HEADS = 4
HEAD_DIM = 256
WINDOW = 4096

EPSILON = 1e-06
SOFT_CAP = 50.0
ROPE_BASE = 10000.0
MESH = pl.DeviceIdType.MESH
VMEM_LIMIT = 56 * 1024 * 1024
LANES = 128
BF16 = jnp.bfloat16
F32 = jnp.float32


def after(value, *earlier):
    return lax.optimization_barrier((value, *earlier))[0]


def dot_nn(left, right):
    return lax.dot_general(left, right, (((1,), (0,)), ((), ())), preferred_element_type=F32)


def dot_nt(left, right):
    return lax.dot_general(left, right, (((1,), (1,)), ((), ())), preferred_element_type=F32)


def dot_tn(left, right):
    return lax.dot_general(left, right, (((0,), (0,)), ((), ())), preferred_element_type=F32)


def rms_scale(vector):
    return lax.rsqrt(jnp.mean(vector * vector, axis=-1, keepdims=True) + EPSILON)


def norm_back(grad_in, unit, scale, gain):
    gain_grad = jnp.sum(grad_in * unit, axis=0)
    unit_grad = grad_in * gain
    vector_grad = scale * (unit_grad - unit * jnp.mean(unit_grad * unit, axis=-1, keepdims=True))
    return (vector_grad, gain_grad)


def rotary(vector, cosine, sine, direction):
    half_dim = vector.shape[-1] // 2
    first_half = vector[..., :half_dim]
    second_half = vector[..., half_dim:]
    return jnp.concatenate(
        [
            first_half * cosine - direction * (second_half * sine),
            second_half * cosine + direction * (first_half * sine),
        ],
        axis=-1,
    )


def gather_kernel(sizes, x_ref, o_ref, send_sem, recv_sem):
    dp_size, seq_size = sizes
    count = dp_size * seq_size
    dp, seq, mp = lax.axis_index("dp"), lax.axis_index("seq"), lax.axis_index("mp")
    rank = dp * seq_size + seq

    def peer(k):
        other = lax.rem(rank + k, count)
        return (other // seq_size, lax.rem(other, seq_size), mp)

    barrier = pltpu.get_barrier_semaphore()
    for k in range(1, count):
        pl.semaphore_signal(barrier, inc=1, device_id=peer(k), device_id_type=MESH)
    pl.semaphore_wait(barrier, count - 1)
    copies = []
    for k in range(1, count):
        copies.append(
            pltpu.make_async_remote_copy(
                src_ref=x_ref,
                dst_ref=o_ref.at[rank],
                send_sem=send_sem.at[k],
                recv_sem=recv_sem.at[k],
                device_id=peer(k),
                device_id_type=MESH,
            )
        )
        copies[-1].start()
    o_ref[pl.ds(rank, 1)] = x_ref[...][None]
    for copy in copies:
        copy.wait()


def gather_gains(gains, dp_size, seq_size):
    count = dp_size * seq_size
    local = gains[0].shape[0]
    width = -(-local // LANES) * LANES
    block = jnp.stack([gain.astype(F32) for gain in gains])
    block = jnp.pad(block, ((0, 8 - len(gains)), (0, width - local)))
    full = pl.pallas_call(
        functools.partial(gather_kernel, (dp_size, seq_size)),
        out_shape=jax.ShapeDtypeStruct((count, 8, width), F32),
        in_specs=[pl.BlockSpec(memory_space=pltpu.VMEM)],
        out_specs=pl.BlockSpec(memory_space=pltpu.VMEM),
        scratch_shapes=[
            pltpu.SemaphoreType.DMA((count,)),
            pltpu.SemaphoreType.DMA((count,)),
        ],
        compiler_params=pltpu.CompilerParams(collective_id=1, has_side_effects=True),
    )(block)
    full = jnp.transpose(full[:, : len(gains), :local], (1, 0, 2)).reshape(len(gains), -1)
    return [full[i] for i in range(len(gains))]


def reduce_kernel(sizes, x_ref, o_ref, mine, from_mp, from_ws, sems):
    dp_size, seq_size, mp_size = sizes
    count = dp_size * seq_size
    dp, seq, mp = lax.axis_index("dp"), lax.axis_index("seq"), lax.axis_index("mp")
    rank = dp * seq_size + seq

    def mp_peer(k):
        return (dp, seq, lax.rem(mp + k, mp_size))

    def ws_rank(k):
        return lax.rem(rank + k, count)

    def ws_peer(k):
        other = ws_rank(k)
        return (other // seq_size, lax.rem(other, seq_size), mp)

    barrier = pltpu.get_barrier_semaphore()
    for k in range(1, mp_size):
        pl.semaphore_signal(barrier, inc=1, device_id=mp_peer(k), device_id_type=MESH)
    for k in range(1, count):
        pl.semaphore_signal(barrier, inc=1, device_id=ws_peer(k), device_id_type=MESH)
    pl.semaphore_wait(barrier, mp_size - 1 + count - 1)
    copies = []
    for k in range(1, mp_size):
        copies.append(
            pltpu.make_async_remote_copy(
                src_ref=x_ref,
                dst_ref=from_mp.at[k],
                send_sem=sems.at[0, k],
                recv_sem=sems.at[1, k],
                device_id=mp_peer(k),
                device_id_type=MESH,
            )
        )
        copies[-1].start()
    for copy in copies:
        copy.wait()
    total = x_ref[...]
    for k in range(1, mp_size):
        total = total + from_mp[k]
    mine[...] = total
    copies = []
    for k in range(1, count):
        copies.append(
            pltpu.make_async_remote_copy(
                src_ref=mine.at[ws_rank(k)],
                dst_ref=from_ws.at[k],
                send_sem=sems.at[2, k],
                recv_sem=sems.at[3, k],
                device_id=ws_peer(k),
                device_id_type=MESH,
            )
        )
        copies[-1].start()
    for copy in copies:
        copy.wait()
    own = mine[pl.ds(rank, 1)][0]
    for k in range(1, count):
        own = own + from_ws[k]
    o_ref[...] = own


def reduce_gains(grads, dp_size, seq_size, mp_size):
    count = dp_size * seq_size
    local = grads[0].shape[0] // count
    width = -(-local // LANES) * LANES
    block = jnp.transpose(jnp.stack(grads).reshape(len(grads), count, local), (1, 0, 2))
    block = jnp.pad(block, ((0, 0), (0, 8 - len(grads)), (0, width - local)))
    most = max(count, mp_size)
    total = pl.pallas_call(
        functools.partial(reduce_kernel, (dp_size, seq_size, mp_size)),
        out_shape=jax.ShapeDtypeStruct((8, width), F32),
        in_specs=[pl.BlockSpec(memory_space=pltpu.VMEM)],
        out_specs=pl.BlockSpec(memory_space=pltpu.VMEM),
        scratch_shapes=[
            pltpu.VMEM((count, 8, width), F32),
            pltpu.VMEM((mp_size, count, 8, width), F32),
            pltpu.VMEM((count, 8, width), F32),
            pltpu.SemaphoreType.DMA((4, most)),
        ],
        compiler_params=pltpu.CompilerParams(collective_id=2, has_side_effects=True),
    )(block)
    return [total[i, :local] for i in range(len(grads))]


def key_mask(shape, first_key, first_query, tile, far):
    key = first_key + lax.broadcasted_iota(jnp.int32, shape, 0)
    query = first_query + lax.rem(lax.broadcasted_iota(jnp.int32, shape, 1), tile)
    return key > query if far else key <= query


def for_key_tiles(tile_fn, index, tile, span, step, blocks, windowed):
    seq = lax.axis_index("seq")
    per_block = span // step
    low = jnp.maximum(seq - blocks, 0)
    if windowed:
        @pl.when(seq >= blocks)
        def _():
            tile_fn(seq - blocks, 0, span, "far")

        low = jnp.maximum(seq - blocks + 1, 0)

    def past(t, carry):
        tile_fn(lax.div(t, per_block), pl.multiple_of(lax.rem(t, per_block) * step, step), step, "")
        return carry

    lax.fori_loop(low * per_block, seq * per_block, past, 0)
    tile_fn(seq, 0, (index + 1) * tile, "near")


def attend_kernel(plan, q_ref, kv_ref, o_ref, of_ref, lse_ref, acc, total):
    tile, span, step, blocks, windowed = plan
    for i in range(q_ref.shape[0]):
        query = q_ref[i]
        rows = query.shape[0]
        acc[...] = jnp.zeros_like(acc)
        total[...] = jnp.zeros_like(total)

        def tile_fn(block, first, count, mask, i=i, query=query, rows=rows):
            key = kv_ref[block, 0, pl.ds(first, count), :]
            value = kv_ref[block, 1, pl.ds(first, count), :]
            raw = dot_nt(key, query)
            weight = jnp.exp(SOFT_CAP * jnp.tanh(raw * (1.0 / SOFT_CAP)))
            if mask:
                inside = key_mask(weight.shape, first, i * tile, tile, mask == "far")
                weight = jnp.where(inside, weight, 0.0)
            total[...] += jnp.sum(weight.reshape(count // 8, 8, rows), axis=0)
            acc[...] += dot_tn(value, weight.astype(BF16))

        for_key_tiles(tile_fn, i, tile, span, step, blocks, windowed)
        row_total = jnp.sum(total[...], axis=0, keepdims=True)
        out = (acc[...] / row_total).T
        o_ref[i] = out.astype(BF16)
        of_ref[i] = out
        lse_ref[i] = jnp.log(row_total)


def attend_back_kernel(plan, q_ref, do_ref, lse_ref, delta_ref, kv_ref, dq_ref, dkv_ref, grads, acc):
    tile, span, step, blocks, windowed = plan
    grads[...] = jnp.zeros_like(grads)
    for i in range(q_ref.shape[0]):
        query = q_ref[i]
        dout = do_ref[i]
        lse = lse_ref[i]
        delta = delta_ref[i]
        acc[...] = jnp.zeros_like(acc)

        def tile_fn(block, first, count, mask, i=i, query=query, dout=dout, lse=lse, delta=delta):
            key = kv_ref[block, 0, pl.ds(first, count), :]
            value = kv_ref[block, 1, pl.ds(first, count), :]
            bounded = jnp.tanh(dot_nt(key, query) * (1.0 / SOFT_CAP))
            prob = jnp.exp(SOFT_CAP * bounded - lse)
            if mask:
                inside = key_mask(prob.shape, first, i * tile, tile, mask == "far")
                prob = jnp.where(inside, prob, 0.0)
            dprob = dot_nt(value, dout)
            draw = (prob * (dprob - delta) * (1.0 - bounded * bounded)).astype(BF16)
            grads[block, 1, pl.ds(first, count), :] += dot_nn(prob.astype(BF16), dout)
            grads[block, 0, pl.ds(first, count), :] += dot_nn(draw, query)
            acc[...] += dot_tn(key, draw)

        for_key_tiles(tile_fn, i, tile, span, step, blocks, windowed)
        dq_ref[i] = acc[...].T
    dkv_ref[...] = grads[...].astype(BF16)


def attention_plan(span, seq_size):
    blocks = WINDOW // span
    return (min(256, span), span, min(512, span), blocks, seq_size > blocks)


def attend(queries, pairs, plan):
    tiles, rows, width = queries.shape
    return pl.pallas_call(
        functools.partial(attend_kernel, plan),
        out_shape=(
            jax.ShapeDtypeStruct(queries.shape, BF16),
            jax.ShapeDtypeStruct(queries.shape, F32),
            jax.ShapeDtypeStruct((tiles, 1, rows), F32),
        ),
        in_specs=[pl.BlockSpec(memory_space=pltpu.VMEM)] * 2,
        out_specs=(pl.BlockSpec(memory_space=pltpu.VMEM),) * 3,
        scratch_shapes=[pltpu.VMEM((width, rows), F32), pltpu.VMEM((8, rows), F32)],
        compiler_params=pltpu.CompilerParams(vmem_limit_bytes=VMEM_LIMIT),
        cost_estimate=pl.CostEstimate(
            flops=4 * tiles * rows * width * plan[1] * 3,
            bytes_accessed=4 * queries.size * 2,
            transcendentals=0,
        ),
    )(queries, pairs)


def attend_back(queries, dout, lse, delta, pairs, plan):
    tiles, rows, width = queries.shape
    return pl.pallas_call(
        functools.partial(attend_back_kernel, plan),
        out_shape=(
            jax.ShapeDtypeStruct(queries.shape, F32),
            jax.ShapeDtypeStruct(pairs.shape, BF16),
        ),
        in_specs=[pl.BlockSpec(memory_space=pltpu.VMEM)] * 5,
        out_specs=(pl.BlockSpec(memory_space=pltpu.VMEM),) * 2,
        scratch_shapes=[pltpu.VMEM(pairs.shape, F32), pltpu.VMEM((width, rows), F32)],
        compiler_params=pltpu.CompilerParams(vmem_limit_bytes=VMEM_LIMIT),
        cost_estimate=pl.CostEstimate(
            flops=10 * tiles * rows * width * plan[1] * 3,
            bytes_accessed=4 * queries.size * 2,
            transcendentals=0,
        ),
    )(queries, dout, lse, delta, pairs)


def swapped(x, axis, k):
    return lax.ppermute(x, axis, [(i, i ^ k) for i in range(lax.axis_size(axis))])


def shards(
    tokens,
    cotangent,
    pre_attn_gain,
    w_query,
    w_key,
    w_value,
    w_out,
    post_attn_gain,
    pre_ffw_gain,
    w_gate,
    w_up,
    w_down,
    post_ffw_gain,
):
    dp_size, seq_size, mp_size = (lax.axis_size(axis) for axis in ("dp", "seq", "mp"))
    dp, seq, mp = lax.axis_index("dp"), lax.axis_index("seq"), lax.axis_index("mp")
    both = ("dp", "seq")
    heads = w_query.shape[1] // HEAD_DIM
    group = Q_HEADS // KV_HEADS
    kv_first = mp * heads // group
    q_width = heads * HEAD_DIM
    span = tokens.shape[1]
    width = tokens.shape[2]
    share = span // mp_size
    plan = attention_plan(span, seq_size)
    tile = plan[0]
    tiles = span // tile

    def gather_weight(x):
        return lax.all_gather(x, both, axis=0, tiled=True)

    w_qkv_own = jnp.concatenate(
        [
            w_query,
            lax.dynamic_slice_in_dim(w_key, kv_first * HEAD_DIM, HEAD_DIM, 1),
            lax.dynamic_slice_in_dim(w_value, kv_first * HEAD_DIM, HEAD_DIM, 1),
        ],
        axis=1,
    )
    w_qkv = gather_weight(w_qkv_own)
    w_out_t = gather_weight(after(w_out.T, w_qkv))
    gain_one, gain_two, gain_three, gain_four = gather_gains(
        [pre_attn_gain, post_attn_gain, pre_ffw_gain, post_ffw_gain], dp_size, seq_size
    )

    inputs = tokens[0].astype(F32)
    positions = seq * span + jnp.arange(span, dtype=jnp.int32)
    half_dim = HEAD_DIM // 2
    frequency = ROPE_BASE ** (-jnp.arange(half_dim, dtype=F32) * 2.0 / HEAD_DIM)
    angles = positions.astype(F32)[:, None, None] * frequency
    cosine = jnp.cos(angles)
    sine = jnp.sin(angles)
    scale_one = rms_scale(inputs)
    normed_one = (inputs * scale_one * gain_one).astype(BF16)
    key_lin = dot_nn(normed_one, w_qkv[:, q_width : q_width + HEAD_DIM])
    keys_own = rotary(key_lin, cosine[:, 0], sine[:, 0], 1.0).astype(BF16)
    values_own = dot_nn(normed_one, w_qkv[:, q_width + HEAD_DIM :]).astype(BF16)
    pairs = lax.all_gather(jnp.stack([keys_own, values_own]), "seq", axis=0)
    query_lin = dot_nn(normed_one, w_qkv[:, :q_width]).reshape(span, heads, HEAD_DIM)
    queries = (rotary(query_lin, cosine, sine, 1.0) * HEAD_DIM ** (-0.5)).astype(BF16)

    def to_tiles(x):
        x = x.reshape(tiles, tile, heads, -1)
        return jnp.transpose(x, (0, 2, 1, 3)).reshape(tiles, heads * tile, -1)

    def from_tiles(x):
        x = x.reshape(tiles, heads, tile, -1)
        return jnp.transpose(x, (0, 2, 1, 3)).reshape(span, -1)

    queries = to_tiles(queries)
    gate_w = gather_weight(after(w_gate, pairs))
    up_w = gather_weight(after(w_up, gate_w))
    down_wt = gather_weight(after(w_down.T, up_w))

    attn_tiles, attn_exact, lse = attend(queries, pairs, plan)
    attn_o = from_tiles(attn_tiles)

    def owner_rows(x, k):
        return lax.dynamic_slice_in_dim(x, (mp ^ k) * share, share, 0)

    def by_owner(x):
        return jnp.concatenate([owner_rows(x, k) for k in range(mp_size)], axis=0)

    def in_place(x):
        return jnp.concatenate(
            [lax.dynamic_slice_in_dim(x, (mp ^ k) * share, share, 0) for k in range(mp_size)], axis=0
        )

    def row_total(part_fn):
        arrived = [swapped(part_fn(k).astype(BF16), "mp", k) for k in reversed(range(1, mp_size))]
        total = part_fn(0)
        for part in arrived:
            total = total + part.astype(F32)
        return total

    def row_gather(rows):
        return jnp.concatenate(
            [rows] + [swapped(rows, "mp", k) for k in range(1, mp_size)], axis=0
        )

    def group_of(x, k):
        return x[k * share : (k + 1) * share]

    attn_o = by_owner(attn_o)
    inputs_own = owner_rows(tokens[0], 0).astype(F32)
    grad_out = owner_rows(cotangent[0], 0).astype(F32)

    attn = row_total(lambda k: dot_nt(group_of(attn_o, k), w_out_t))
    scale_two = rms_scale(attn)
    unit_two = attn * scale_two
    resid = inputs_own + unit_two * gain_two
    scale_three = rms_scale(resid)
    unit_three = resid * scale_three
    normed_two = row_gather((unit_three * gain_three).astype(BF16))

    gate_lin = dot_nn(normed_two, gate_w)
    up_lin = dot_nn(normed_two, up_w)
    gate_act, gelu_pull = jax.vjp(lambda gate_in: jax.nn.gelu(gate_in, approximate=True), gate_lin)
    hidden = (gate_act * up_lin).astype(BF16)
    mixed = row_total(lambda k: dot_nt(group_of(hidden, k), down_wt))
    scale_four = rms_scale(mixed)
    unit_four = mixed * scale_four
    output = resid + unit_four * gain_four
    dmixed, grad_gain_four = norm_back(grad_out, unit_four, scale_four, gain_four)
    dmixed_low = row_gather(dmixed.astype(BF16))

    half = width // dp_size

    def weight_grad(left, right):
        parts = []
        for k in reversed(range(dp_size)):
            columns = lax.dynamic_slice_in_dim(left, (dp ^ k) * half, half, 1)
            part = dot_tn(columns, right)
            if k:
                parts.append(swapped(part.astype(BF16), "dp", k).astype(F32))
            else:
                total = part
        for part in parts:
            total = total + part
        return total.astype(BF16)

    def spread(x):
        return lax.psum_scatter(x, "seq", scatter_dimension=0, tiled=True)

    dhidden = dot_nn(dmixed_low, down_wt)
    dgate_low = gelu_pull(dhidden * up_lin)[0].astype(BF16)
    dup_low = (dhidden * gate_act).astype(BF16)
    grad_down_t = spread(weight_grad(dmixed_low, hidden))
    dnormed_two = row_total(
        lambda k: dot_nt(group_of(dgate_low, k), gate_w) + dot_nt(group_of(dup_low, k), up_w)
    )
    dresid_norm, grad_gain_three = norm_back(dnormed_two, unit_three, scale_three, gain_three)
    dresid = grad_out + dresid_norm
    dattn, grad_gain_two = norm_back(dresid, unit_two, scale_two, gain_two)
    dattn_low = row_gather(dattn.astype(BF16))
    grad_gate = spread(weight_grad(normed_two, dgate_low))
    grad_up = spread(weight_grad(normed_two, dup_low))

    dattn_o = in_place(dot_nn(dattn_low, w_out_t)).astype(BF16)
    dattn_tiles = to_tiles(dattn_o)
    delta = jnp.sum(dattn_tiles.astype(F32) * attn_exact, axis=-1)[:, None, :]
    dquery_tiles, dpairs = attend_back(queries, dattn_tiles, lse, delta, pairs, plan)
    own_grads = lax.psum_scatter(dpairs, "seq", scatter_dimension=0, tiled=False).astype(F32)
    dquery = from_tiles(dquery_tiles).reshape(span, heads, HEAD_DIM)
    dquery_low = (
        rotary(dquery * HEAD_DIM ** (-0.5), cosine, sine, -1.0).reshape(span, q_width).astype(BF16)
    )
    dkey_low = rotary(own_grads[0], cosine[:, 0], sine[:, 0], -1.0).astype(BF16)
    dvalue_low = own_grads[1].astype(BF16)
    dqkv_low = jnp.concatenate([dquery_low, dkey_low, dvalue_low], axis=1)
    dnormed_one = row_total(lambda k: dot_nt(owner_rows(dqkv_low, k), w_qkv))
    grad_out_wt = spread(weight_grad(dattn_low, attn_o))
    grad_qkv = spread(weight_grad(normed_one, dqkv_low))

    scale_own = owner_rows(scale_one, 0)
    unit_one = inputs_own * scale_own
    dinput_norm, grad_gain_one = norm_back(dnormed_one, unit_one, scale_own, gain_one)
    tokens_grad = (dresid + dinput_norm).astype(BF16)

    kv_grad = grad_qkv[:, q_width:]
    empty = jnp.zeros((2, w_key.shape[0], w_key.shape[1]), F32)
    kv_total = empty
    for k in range(mp_size):
        piece = (swapped(kv_grad, "mp", k) if k else kv_grad).astype(F32)
        first = (mp ^ k) * heads // group * HEAD_DIM
        piece = jnp.stack([piece[:, :HEAD_DIM], piece[:, HEAD_DIM:]])
        before = lax.dynamic_slice_in_dim(kv_total, first, HEAD_DIM, 2)
        kv_total = lax.dynamic_update_slice_in_dim(kv_total, before + piece, first, 2)

    gain_grads = reduce_gains(
        [grad_gain_one, grad_gain_two, grad_gain_three, grad_gain_four], dp_size, seq_size, mp_size
    )
    return (
        output.astype(BF16)[None],
        tokens_grad[None],
        gain_grads[0],
        grad_qkv[:, :q_width].astype(F32),
        kv_total[0],
        kv_total[1],
        grad_out_wt.astype(F32).T,
        gain_grads[1],
        gain_grads[2],
        grad_gate.astype(F32),
        grad_up.astype(F32),
        grad_down_t.astype(F32).T,
        gain_grads[3],
    )


def solution(mesh):
    weight = P(("dp", "seq"), "mp")
    whole_rows = P(("dp", "seq"), None)
    columns = P("mp", ("dp", "seq"))
    gain = P(("dp", "seq"))
    tokens = P("dp", "seq", None)
    rows = P("dp", ("seq", "mp"), None)
    in_specs = (
        tokens,
        tokens,
        gain,
        weight,
        whole_rows,
        whole_rows,
        columns,
        gain,
        gain,
        weight,
        weight,
        columns,
        gain,
    )
    out_specs = (
        rows,
        rows,
        gain,
        weight,
        whole_rows,
        whole_rows,
        columns,
        gain,
        gain,
        weight,
        weight,
        columns,
        gain,
    )
    return jax.shard_map(shards, mesh=mesh, in_specs=in_specs, out_specs=out_specs, check_vma=False)
```

time: 2630 us -> 1410 us (0.54)
  waiting for transfers between devices: 1920 us -> 906 us
  other arithmetic: 187 us -> 55.1 us
  matrix products: 359 us -> 284 us
  Pallas kernels: 0 us -> 71.1 us
  blocking collectives: 64.8 us -> 0 us
    psum x5 -> x0, waiting for transfers between devices: 772 us -> none  [the longest x4 772 us: row_sum(): summed = lax.psum(term_fn(0, span_len), 'mp')]
    reduce_scatter x7 -> x6, waiting for transfers between devices: 739 us -> 232 us  [the longest x5 224 us: spread(): return lax.psum_scatter(x, 'seq', scatter_dimension=0, tiled=True)]
    ppermute x6 -> x29, waiting for transfers between devices: 167 us -> 351 us  [swapped(): lax.ppermute(x, axis, [(i, i ^ k) for i in range(lax.axis_size(axis))])]
    all_gather x7 -> x6, waiting for transfers between devices: 244 us -> 323 us  [the longest x5 244 us: gather_weight(): return lax.all_gather(x, both, axis=0, tiled=True)]
    dot_general x35 -> x37, matrix products: 359 us -> 284 us  [the longest x20 122 us: dot_nt(): lax.dot_general(left, right, (((1,), (1,)), ((), ())), preferred_element_...]
    pallas_call x0 -> x4, Pallas kernels: none -> 71.1 us  [the longest x1 40.4 us: reduce_gains(): pl.pallas_call(functools.partial(reduce_kernel, (dp_size, seq_size, mp_si...]
    unnamed x2 -> x0, blocking collectives: 64.8 us -> none
    convert_element_type x21 -> x11, other arithmetic: 68.4 us -> 14.7 us  [the longest x1 3.29 us: shards(): normed_one = (inputs * scale_one * gain_one).astype(BF16)]
  transfers between devices with their start and end apart: 25 -> 41, of which waited for: 20 -> 27; matrix products, arithmetic and copies ran while one was open for 11% -> 18% of each run, Pallas kernels for 0% -> 4%
where the time goes in v1:
time: 1410 us; the launch traced here: 1400 us
  waiting for transfers between devices  906 us (64%)
  matrix products  284 us (20%)
  Pallas kernels  71.1 us (5%)
  other arithmetic  55.1 us (4%)
  local copies, waits for them, and re-layouts  36.3 us (3%)
  starting transfers between devices  29.7 us (2%)
  between operations  15.8 us (1%)
    ppermute x29, waiting for transfers between devices, swapped(): lax.ppermute(x, axis, [(i, i ^ k) for i in range(lax.axis_size(axis))])  351 us
    all_gather x5, waiting for transfers between devices, gather_weight(): return lax.all_gather(x, both, axis=0, tiled=True)  244 us
    reduce_scatter x5, waiting for transfers between devices, spread(): return lax.psum_scatter(x, 'seq', scatter_dimension=0, tiled=True)  224 us
    dot_general x20, matrix products, dot_nt(): lax.dot_general(left, right, (((1,), (1,)), ((), ())), preferred_element_...  122 us
    dot_general x7, matrix products, dot_nn(): lax.dot_general(left, right, (((1,), (0,)), ((), ())), preferred_element_...  84.7 us
    all_gather x1, waiting for transfers between devices, shards(): pairs = lax.all_gather(jnp.stack([keys_own, values_own]), 'seq', axis=0)  79.7 us
    dot_general x10, matrix products, dot_tn(): lax.dot_general(left, right, (((0,), (0,)), ((), ())), preferred_element_...  77.3 us
    pallas_call x1, Pallas kernels, reduce_gains(): pl.pallas_call(functools.partial(reduce_kernel, (dp_size, seq_size, mp_si...  40.4 us
  transfers between devices with their start and end apart: 41, of which 27 were waited for; matrix products, arithmetic and copies ran while one was open for 18% of the time, Pallas kernels for 4%

profile of v1, /device:TPU:0, one launch (start us, length us, event | category | flops | bytes accessed | tf_op | source)
XLA Modules:
  0.0 1398.7 jit_solution(2668868226721619463)
XLA Ops:
  10.9 10.0 shard_map.228
  29.7 35.0 %all-gather.8.cloned.1.call-done = bf16[2304,1024]{1,0:T(8,128)(2,1)} async-done(((bf16[288,1024]{1,0:T(8,128)(2,1)}), bf16[2304,1024]{1,0:T(8,128)(2,1)}) %all-gather.8.cloned.1.call-update) | async-done | bytes 4718608 | tf_op jit(solution)/shard_map/all_gather | solution.py:364
  64.7 4.2 fusion.80
  75.5 79.7 %all-gather.18.cloned.1.call-done = bf16[8,1024,256]{2,1,0:T(8,128)(2,1)} async-done(((bf16[2,1024,256]{2,1,0:T(8,128)(2,1)}), bf16[8,1024,256]{2,1,0:T(8,128)(2,1)}) %all-gather.18.cloned.1.call-update) | async-done | bytes 4194320 | tf_op jit(solution)/shard_map/all_gather | solution.py:392
  155.3 100.6 %all-gather.12.cloned.1.call-done = bf16[2304,2304]{1,0:T(8,128)(2,1)} async-done(((bf16[288,2304]{1,0:T(8,128)(2,1)}), bf16[2304,2304]{1,0:T(8,128)(2,1)}) %all-gather.12.cloned.1.call-update) | async-done | bytes 10616848 | tf_op jit(solution)/shard_map/all_gather | solution.py:364
  256.5 99.7 %all-gather.14.cloned.1.call-done = bf16[2304,2304]{1,0:T(8,128)(2,1)} async-done(((bf16[288,2304]{1,0:T(8,128)(2,1)}), bf16[2304,2304]{1,0:T(8,128)(2,1)}) %all-gather.14.cloned.1.call-update) | async-done | bytes 10616848 | tf_op jit(solution)/shard_map/all_gather | solution.py:364
  360.5 5.5 fusion.18
  367.5 8.3 shard_map.229
  379.3 8.3 all-gather.10.cloned.1.call-done
  387.7 3.6 convolution_convert_fusion.9
  400.6 19.7 %collective-permute-done.2 = bf16[256,2304]{1,0:T(8,128)(2,1)S(1)} collective-permute-done((bf16[256,2304]{1,0:T(8,128)(2,1)}, bf16[256,2304]{1,0:T(8,128)(2,1)S(1)}, u32[]{:S(2)}, u32[]{:S(2)}) %collective-permute-start.2) | collective-permute-done | bytes 1179680 | tf_op jit(solution)/shard_map/ppermute | solution.py:331
  420.3 27.7 %collective-permute-done.1 = bf16[256,2304]{1,0:T(8,128)(2,1)} collective-permute-done((bf16[256,2304]{1,0:T(8,128)(2,1)}, bf16[256,2304]{1,0:T(8,128)(2,1)}, u32[]{:S(2)}, u32[]{:S(2)}) %collective-permute-start.1) | collective-permute-done | bytes 1179680 | tf_op jit(solution)/shard_map/ppermute | solution.py:331
  457.5 26.3 %collective-permute-done.5 = bf16[256,2304]{1,0:T(8,128)(2,1)S(1)} collective-permute-done((bf16[256,2304]{1,0:T(8,128)(2,1)S(1)}, bf16[256,2304]{1,0:T(8,128)(2,1)S(1)}, u32[]{:S(2)}, u32[]{:S(2)}) %collective-permute-start.5) | collective-permute-done | bytes 1179680 | tf_op jit(solution)/shard_map/ppermute | solution.py:331
  483.9 23.3 %collective-permute-done.4 = bf16[256,2304]{1,0:T(8,128)(2,1)S(1)} collective-permute-done((bf16[256,2304]{1,0:T(8,128)(2,1)S(1)}, bf16[256,2304]{1,0:T(8,128)(2,1)S(1)}, u32[]{:S(2)}, u32[]{:S(2)}) %collective-permute-start.4) | collective-permute-done | bytes 1179680 | tf_op jit(solution)/shard_map/ppermute | solution.py:331
  509.3 17.5 %fusion.144 = f32[1024,2304]{1,0:T(8,128)} fusion(bf16[2304,2304]{1,0:T(8,128)(2,1)} %all-gather.12.cloned.1.call-done, bf16[256,2304]{1,0:T(8,128)(2,1)S(1)} %collective-permute-done.5, bf16[256,2304]{1,0:T(8,128)(2,1)S(1)} %collective-permute-done.4, bf16[256,2304]{1,0:T(8,128)(2,1)S(1)} %collective-permute-done.3, ...), kind=kOutput, calls=%fused_computation.257 | convolution fusion | flops 10890510336 | bytes 24772608 | tf_op jit(solution)/shard_map/dot_general | solution.py:30
  526.7 23.4 %multiply_convert_fusion.1 = (bf16[1024,2304]{1,0:T(8,128)(2,1)}, f32[1024,2304]{1,0:T(8,128)}) fusion(f32[1024,2304]{1,0:T(8,128)} %fusion.144, bf16[2304,2304]{1,0:T(8,128)(2,1)} %all-gather.14.cloned.1.call-done, bf16[256,2304]{1,0:T(8,128)(2,1)} %copy-done.27, bf16[256,2304]{1,0:T(8,128)(2,1)} %copy-done.29, bf16[256,2304]{1,0:T(8,128)(2,1)} %copy-done.30, ...), kind=kOutput, calls=%fused_computation.28 | convolution fusion | flops 10914103296 | bytes 38928384 | tf_op jit(solution)/shard_map/dot_general | solution.py:30
  550.2 8.5 convolution_convert_fusion.3
  559.3 4.0 convolution_convert_fusion.4
  564.7 4.0 convolution_convert_fusion.5
  570.2 17.7 %collective-permute-done.8 = bf16[256,2304]{1,0:T(8,128)(2,1)} collective-permute-done((bf16[256,2304]{1,0:T(8,128)(2,1)}, bf16[256,2304]{1,0:T(8,128)(2,1)}, u32[]{:S(2)}, u32[]{:S(2)}) %collective-permute-start.8) | collective-permute-done | bytes 1179680 | tf_op jit(solution)/shard_map/ppermute | solution.py:331
  587.8 28.9 %collective-permute-done.7 = bf16[256,2304]{1,0:T(8,128)(2,1)} collective-permute-done((bf16[256,2304]{1,0:T(8,128)(2,1)}, bf16[256,2304]{1,0:T(8,128)(2,1)}, u32[]{:S(2)}, u32[]{:S(2)}) %collective-permute-start.7) | collective-permute-done | bytes 1179680 | tf_op jit(solution)/shard_map/ppermute | solution.py:331
  616.8 8.4 multiply_reduce_fusion.4
  634.7 26.3 %collective-permute-done.11 = bf16[256,2304]{1,0:T(8,128)(2,1)S(1)} collective-permute-done((bf16[256,2304]{1,0:T(8,128)(2,1)S(1)}, bf16[256,2304]{1,0:T(8,128)(2,1)S(1)}, u32[]{:S(2)}, u32[]{:S(2)}) %collective-permute-start.11) | collective-permute-done | bytes 1179680 | tf_op jit(solution)/shard_map/ppermute | solution.py:331
  661.0 23.4 %collective-permute-done.10 = bf16[256,2304]{1,0:T(8,128)(2,1)S(1)} collective-permute-done((bf16[256,2304]{1,0:T(8,128)(2,1)S(1)}, bf16[256,2304]{1,0:T(8,128)(2,1)S(1)}, u32[]{:S(2)}, u32[]{:S(2)}) %collective-permute-start.10) | collective-permute-done | bytes 1179680 | tf_op jit(solution)/shard_map/ppermute | solution.py:331
  686.5 28.5 %multiply_convert_fusion = (bf16[1024,2304]{1,0:T(8,128)(2,1)}, bf16[1024,2304]{1,0:T(8,128)(2,1)}) fusion(f32[1024,2304]{1,0:T(8,128)} %fusion.144, f32[1024,2304]{1,0:T(8,128)} %get-tuple-element.90, bf16[2304,2304]{1,0:T(8,128)(2,1)} %all-gather.16.cloned.1.call-done, bf16[256,2304]{1,0:T(8,128)(2,1)} %copy-done.22, bf16[256,2304]{1,0:T(8,128)(2,1)} %copy-done.24, ...), kind=kOutput, calls=%fused_computation.27 | convolution fusion | flops 10947133440 | bytes 43646976 | tf_op jit(solution)/shard_map/dot_general | solution.py:30
  715.0 6.5 fusion.59
  721.5 8.5 fusion.24
  730.8 8.7 fusion.62
  739.6 6.1 fusion.23
  746.8 8.7 fusion.65
  755.5 6.0 fusion.22
  763.2 9.0 fusion.70
  772.1 26.9 %collective-permute-done.13 = bf16[256,2304]{1,0:T(8,128)(2,1)} collective-permute-done((bf16[256,2304]{1,0:T(8,128)(2,1)}, bf16[256,2304]{1,0:T(8,128)(2,1)}, u32[]{:S(2)}, u32[]{:S(2)}) %collective-permute-start.13) | collective-permute-done | bytes 1179680 | tf_op jit(solution)/shard_map/ppermute | solution.py:331
  799.1 10.9 multiply_reduce_fusion
  810.0 4.0 multiply_reduce_fusion.1
  818.8 26.3 %collective-permute-done.17 = bf16[256,2304]{1,0:T(8,128)(2,1)S(1)} collective-permute-done((bf16[256,2304]{1,0:T(8,128)(2,1)S(1)}, bf16[256,2304]{1,0:T(8,128)(2,1)S(1)}, u32[]{:S(2)}, u32[]{:S(2)}) %collective-permute-start.17) | collective-permute-done | bytes 1179680 | tf_op jit(solution)/shard_map/ppermute | solution.py:331
  845.2 23.2 %collective-permute-done.16 = bf16[256,2304]{1,0:T(8,128)(2,1)S(1)} collective-permute-done((bf16[256,2304]{1,0:T(8,128)(2,1)S(1)}, bf16[256,2304]{1,0:T(8,128)(2,1)S(1)}, u32[]{:S(2)}, u32[]{:S(2)}) %collective-permute-start.16) | collective-permute-done | bytes 1179680 | tf_op jit(solution)/shard_map/ppermute | solution.py:331
  874.8 12.5 shard_map.230
  890.9 11.5 convolution_convert_fusion.2
  905.4 7.7 collective-permute-done.25
  913.1 4.2 fusion.25
  917.5 11.4 fusion.2
  929.1 9.0 convolution_convert_fusion.1
  938.2 8.6 collective-permute-done.27
  946.9 10.7 fusion.3
  960.8 8.6 convolution_convert_fusion
  969.7 8.6 collective-permute-done.28
  978.3 7.5 fusion.4
  989.8 7.0 reduce-scatter.7.cloned.1.call-done
  1003.5 6.2 convolution_convert_fusion.12
  1010.0 5.6 convolution_convert_fusion.6
  1017.1 5.7 add_convert_fusion
  1024.4 4.8 convolution_convert_fusion.7
  1030.8 4.8 convolution_convert_fusion.8
  1039.0 5.7 collective-permute-done.20
  1044.7 38.3 %collective-permute-done.19 = bf16[256,2304]{1,0:T(8,128)(2,1)} collective-permute-done((bf16[256,2304]{1,0:T(8,128)(2,1)}, bf16[256,2304]{1,0:T(8,128)(2,1)}, u32[]{:S(2)}, u32[]{:S(2)}) %collective-permute-start.19) | collective-permute-done | bytes 1179680 | tf_op jit(solution)/shard_map/ppermute | solution.py:331
  1083.0 7.6 fusion.39
  1091.4 40.4 %shard_map.231 = f32[8,384]{1,0:T(8,128)} custom-call(f32[8,8,384]{2,1,0:T(8,128)} %pad.12.x_ref), custom_call_target="tpu_custom_call" | custom-call | tf_op jit(solution)/shard_map/pallas_call | solution.py:187
  1133.3 4.3 fusion.57
  1140.6 82.0 %reduce-scatter.15.cloned.1.call-done = bf16[288,2304]{1,0:T(8,128)(2,1)} async-done(((bf16[1152,2304]{1,0:T(8,128)(2,1)}), bf16[288,2304]{1,0:T(8,128)(2,1)}) %reduce-scatter.15.cloned.1.call-update) | async-done | bytes 1327120 | tf_op jit(solution)/shard_map/reduce_scatter | solution.py:477
  1225.5 94.8 %reduce-scatter.17.cloned.1.call-done = bf16[288,2304]{1,0:T(8,128)(2,1)} async-done(((bf16[1152,2304]{1,0:T(8,128)(2,1)}), bf16[288,2304]{1,0:T(8,128)(2,1)}) %reduce-scatter.17.cloned.1.call-update) | async-done | bytes 1327120 | tf_op jit(solution)/shard_map/reduce_scatter | solution.py:477
  1323.3 47.7 %reduce-scatter.9.cloned.1.call-done = bf16[288,1024]{1,0:T(8,128)(2,1)} async-done(((bf16[1152,1024]{1,0:T(8,128)(2,1)}), bf16[288,1024]{1,0:T(8,128)(2,1)}) %reduce-scatter.9.cloned.1.call-update) | async-done | bytes 589840 | tf_op jit(solution)/shard_map/reduce_scatter | solution.py:477
  1377.0 6.0 collective-permute-done.22
  1383.1 6.1 collective-permute-done.23
  (300 shorter events, 128.2 us)
Async XLA Ops:
  7.2 57.5 %all-gather.8.cloned.1.call-start = ((), (), s32[]{:S(2)}) async-start(), calls=%async_computation.6 | async-start | bytes 5308416 | tf_op jit(solution)/shard_map/all_gather | solution.py:364
  10.2 145.0 %all-gather.18.cloned.1.call-start = ((), (), s32[]{:S(2)}) async-start(), calls=%async_computation.17 | async-start | bytes 5242880 | tf_op jit(solution)/shard_map/all_gather | solution.py:392
  22.6 338.0 %copy-start.38 = (f32[2304]{0:T(1024)}, f32[2304]{0:T(1024)S(1)}, u32[]{:S(2)}) copy-start(f32[2304]{0:T(1024)S(1)} %mul.465) | copy-start | bytes 27652
  22.6 46.4 %copy-start.52 = (f32[128]{0:T(128)}, f32[128]{0:T(128)S(1)}, u32[]{:S(2)}) copy-start(f32[128]{0:T(128)S(1)} %multiply_power_fusion) | copy-start | bytes 1540
  22.6 46.4 %copy-start.46 = (f32[1024]{0:T(1024)}, f32[1024]{0:T(1024)S(1)}, u32[]{:S(2)}) copy-start(f32[1024]{0:T(1024)S(1)} %add_convert_fusion.3) | copy-start | bytes 12292
  26.4 334.1 %copy-start.48 = (f32[1024]{0:T(1024)}, f32[1024]{0:T(1024)S(1)}, u32[]{:S(2)}) copy-start(f32[1024]{0:T(1024)S(1)} %add_rsqrt_fusion) | copy-start | bytes 12292
  71.3 294.7 %copy-start.12 = (f32[1024,128]{1,0:T(8,128)}, f32[1024,128]{1,0:T(8,128)S(1)}, u32[]{:S(2)}) copy-start(f32[1024,128]{1,0:T(8,128)S(1)} %get-tuple-element.87) | copy-start | bytes 1572868
  71.3 294.7 %copy-start.14 = (f32[1024,128]{1,0:T(8,128)}, f32[1024,128]{1,0:T(8,128)S(1)}, u32[]{:S(2)}) copy-start(f32[1024,128]{1,0:T(8,128)S(1)} %get-tuple-element.88) | copy-start | bytes 1572868
  75.5 180.4 %all-gather.12.cloned.1.call-start = ((), (), s32[]{:S(2)}) async-start(), calls=%async_computation.8 | async-start | bytes 11943936 | tf_op jit(solution)/shard_map/all_gather | solution.py:364
  155.2 201.0 %all-gather.14.cloned.1.call-start = ((), (), s32[]{:S(2)}) async-start(), calls=%async_computation.9 | async-start | bytes 11943936 | tf_op jit(solution)/shard_map/all_gather | solution.py:364
  255.9 131.8 %all-gather.10.cloned.1.call-start = ((), (), s32[]{:S(2)}) async-start(), calls=%async_computation.7 | async-start | bytes 2654208 | tf_op jit(solution)/shard_map/all_gather | solution.py:364
  256.5 293.7 %all-gather.16.cloned.1.call-start = ((), (), s32[]{:S(2)}) async-start(), calls=%async_computation.10 | async-start | bytes 11943936 | tf_op jit(solution)/shard_map/all_gather | solution.py:364
  356.2 640.6 %reduce-scatter.7.cloned.1.call-start = ((), (), s32[]{:S(2)}) async-start(), calls=%async_computation.11 | async-start | bytes 5242880 | tf_op jit(solution)/shard_map/reduce_scatter | solution.py:497
  391.3 29.0 %collective-permute-start.2 = (bf16[256,2304]{1,0:T(8,128)(2,1)}, bf16[256,2304]{1,0:T(8,128)(2,1)S(1)}, u32[]{:S(2)}, u32[]{:S(2)}) collective-permute-start(bf16[256,2304]{1,0:T(8,128)(2,1)} %convolution_convert_fusion.9), channel_id=1, source_target_pairs={{0,1},{1,0},{2,3},{3,2},{4,5},{5,4},{6,7},{7,6},{8,9},{9,8},{10,11... | collective-permute-start | bytes 3538952 | tf_op jit(solution)/shard_map/ppermute | solution.py:331
  394.6 53.4 %collective-permute-start.1 = (bf16[256,2304]{1,0:T(8,128)(2,1)}, bf16[256,2304]{1,0:T(8,128)(2,1)}, u32[]{:S(2)}, u32[]{:S(2)}) collective-permute-start(bf16[256,2304]{1,0:T(8,128)(2,1)} %convolution_convert_fusion.10), channel_id=1, source_target_pairs={{0,2},{1,3},{2,0},{3,1},{4,6},{5,7},{6,4},{7,5},{8,10},{9,11},{10,... | collective-permute-start | bytes 3538952 | tf_op jit(solution)/shard_map/ppermute | solution.py:331
  397.9 50.2 %collective-permute-start = (bf16[256,2304]{1,0:T(8,128)(2,1)}, bf16[256,2304]{1,0:T(8,128)(2,1)}, u32[]{:S(2)}, u32[]{:S(2)}) collective-permute-start(bf16[256,2304]{1,0:T(8,128)(2,1)} %convolution_convert_fusion.11), channel_id=1, source_target_pairs={{0,3},{1,2},{2,1},{3,0},{4,7},{5,6},{6,5},{7,4},{8,11},{9,10},{10,... | collective-permute-start | bytes 3538952 | tf_op jit(solution)/shard_map/ppermute | solution.py:331
  453.7 53.5 %copy-start.50 = (f32[256]{0:T(256)}, f32[256]{0:T(256)S(1)}, u32[]{:S(2)}) copy-start(f32[256]{0:T(256)S(1)} %add_rsqrt_fusion.2) | copy-start | bytes 3076
  454.0 72.7 %copy-start.7 = (bf16[256,2304]{1,0:T(8,128)(2,1)}, bf16[256,2304]{1,0:T(8,128)(2,1)S(1)}, u32[]{:S(2)}) copy-start(bf16[256,2304]{1,0:T(8,128)(2,1)S(1)} %multiply_convert_fusion.3) | copy-start | bytes 3538948
  454.0 29.9 %collective-permute-start.5 = (bf16[256,2304]{1,0:T(8,128)(2,1)S(1)}, bf16[256,2304]{1,0:T(8,128)(2,1)S(1)}, u32[]{:S(2)}, u32[]{:S(2)}) collective-permute-start(bf16[256,2304]{1,0:T(8,128)(2,1)S(1)} %multiply_convert_fusion.3), channel_id=1, source_target_pairs={{0,3},{1,2},{2,1},{3,0},{4,7},{5,6},{6,5},{7,4},{8,11},{9,10},{10,... | collective-permute-start | bytes 3538952 | tf_op jit(solution)/shard_map/ppermute | solution.py:331
  455.5 51.7 %collective-permute-start.4 = (bf16[256,2304]{1,0:T(8,128)(2,1)S(1)}, bf16[256,2304]{1,0:T(8,128)(2,1)S(1)}, u32[]{:S(2)}, u32[]{:S(2)}) collective-permute-start(bf16[256,2304]{1,0:T(8,128)(2,1)S(1)} %multiply_convert_fusion.3), channel_id=1, source_target_pairs={{0,2},{1,3},{2,0},{3,1},{4,6},{5,7},{6,4},{7,5},{8,10},{9,11},{10,... | collective-permute-start | bytes 3538952 | tf_op jit(solution)/shard_map/ppermute | solution.py:331
  456.0 51.2 %collective-permute-start.3 = (bf16[256,2304]{1,0:T(8,128)(2,1)S(1)}, bf16[256,2304]{1,0:T(8,128)(2,1)S(1)}, u32[]{:S(2)}, u32[]{:S(2)}) collective-permute-start(bf16[256,2304]{1,0:T(8,128)(2,1)S(1)} %multiply_convert_fusion.3), channel_id=1, source_target_pairs={{0,1},{1,0},{2,3},{3,2},{4,5},{5,4},{6,7},{7,6},{8,9},{9,8},{10,11... | collective-permute-start | bytes 3538952 | tf_op jit(solution)/shard_map/ppermute | solution.py:331
  483.9 23.3 %copy-start.27 = (bf16[256,2304]{1,0:T(8,128)(2,1)}, bf16[256,2304]{1,0:T(8,128)(2,1)S(1)}, u32[]{:S(2)}) copy-start(bf16[256,2304]{1,0:T(8,128)(2,1)S(1)} %collective-permute-done.5) | copy-start | bytes 3538948
  558.7 29.2 %collective-permute-start.8 = (bf16[256,2304]{1,0:T(8,128)(2,1)}, bf16[256,2304]{1,0:T(8,128)(2,1)}, u32[]{:S(2)}, u32[]{:S(2)}) collective-permute-start(bf16[256,2304]{1,0:T(8,128)(2,1)} %convolution_convert_fusion.3), channel_id=1, source_target_pairs={{0,1},{1,0},{2,3},{3,2},{4,5},{5,4},{6,7},{7,6},{8,9},{9,8},{10,11... | collective-permute-start | bytes 3538952 | tf_op jit(solution)/shard_map/ppermute | solution.py:331
  563.3 53.5 %collective-permute-start.7 = (bf16[256,2304]{1,0:T(8,128)(2,1)}, bf16[256,2304]{1,0:T(8,128)(2,1)}, u32[]{:S(2)}, u32[]{:S(2)}) collective-permute-start(bf16[256,2304]{1,0:T(8,128)(2,1)} %convolution_convert_fusion.4), channel_id=1, source_target_pairs={{0,2},{1,3},{2,0},{3,1},{4,6},{5,7},{6,4},{7,5},{8,10},{9,11},{10,... | collective-permute-start | bytes 3538952 | tf_op jit(solution)/shard_map/ppermute | solution.py:331
  568.6 48.1 %collective-permute-start.6 = (bf16[256,2304]{1,0:T(8,128)(2,1)}, bf16[256,2304]{1,0:T(8,128)(2,1)}, u32[]{:S(2)}, u32[]{:S(2)}) collective-permute-start(bf16[256,2304]{1,0:T(8,128)(2,1)} %convolution_convert_fusion.5), channel_id=1, source_target_pairs={{0,3},{1,2},{2,1},{3,0},{4,7},{5,6},{6,5},{7,4},{8,11},{9,10},{10,... | collective-permute-start | bytes 3538952 | tf_op jit(solution)/shard_map/ppermute | solution.py:331
  570.2 55.0 %copy-start.42 = (f32[2304]{0:T(1024)}, f32[2304]{0:T(1024)S(1)}, u32[]{:S(2)}) copy-start(f32[2304]{0:T(1024)S(1)} %mul.512) | copy-start | bytes 27652
  631.2 29.8 %collective-permute-start.11 = (bf16[256,2304]{1,0:T(8,128)(2,1)S(1)}, bf16[256,2304]{1,0:T(8,128)(2,1)S(1)}, u32[]{:S(2)}, u32[]{:S(2)}) collective-permute-start(bf16[256,2304]{1,0:T(8,128)(2,1)S(1)} %get-tuple-element.58), channel_id=1, source_target_pairs={{0,3},{1,2},{2,1},{3,0},{4,7},{5,6},{6,5},{7,4},{8,11},{9,10},{10,... | collective-permute-start | bytes 3538952 | tf_op jit(solution)/shard_map/ppermute | solution.py:331
  632.7 51.7 %collective-permute-start.10 = (bf16[256,2304]{1,0:T(8,128)(2,1)S(1)}, bf16[256,2304]{1,0:T(8,128)(2,1)S(1)}, u32[]{:S(2)}, u32[]{:S(2)}) collective-permute-start(bf16[256,2304]{1,0:T(8,128)(2,1)S(1)} %get-tuple-element.58), channel_id=1, source_target_pairs={{0,2},{1,3},{2,0},{3,1},{4,6},{5,7},{6,4},{7,5},{8,10},{9,11},{10,... | collective-permute-start | bytes 3538952 | tf_op jit(solution)/shard_map/ppermute | solution.py:331
  633.8 50.6 %collective-permute-start.9 = (bf16[256,2304]{1,0:T(8,128)(2,1)S(1)}, bf16[256,2304]{1,0:T(8,128)(2,1)S(1)}, u32[]{:S(2)}, u32[]{:S(2)}) collective-permute-start(bf16[256,2304]{1,0:T(8,128)(2,1)S(1)} %get-tuple-element.58), channel_id=1, source_target_pairs={{0,1},{1,0},{2,3},{3,2},{4,5},{5,4},{6,7},{7,6},{8,9},{9,8},{10,11... | collective-permute-start | bytes 3538952 | tf_op jit(solution)/shard_map/ppermute | solution.py:331
  661.0 23.4 %copy-start.22 = (bf16[256,2304]{1,0:T(8,128)(2,1)}, bf16[256,2304]{1,0:T(8,128)(2,1)S(1)}, u32[]{:S(2)}) copy-start(bf16[256,2304]{1,0:T(8,128)(2,1)S(1)} %collective-permute-done.11) | copy-start | bytes 3538948
  721.5 18.1 %slice-start.4 = ((s8[10616832]{0:T(1024)(128)(4,1)}), s8[4194304]{0:T(1024)(128)(4,1)S(1)}, s32[]{:S(2)}) async-start(s8[10616832]{0:T(1024)(128)(4,1)} %bitcast.158), calls=%async_computation.22 | async-start | bytes 8388608
  721.5 18.1 %slice-start.5 = ((s8[10616832]{0:T(1024)(128)(4,1)}), s8[4194304]{0:T(1024)(128)(4,1)S(1)}, s32[]{:S(2)}) async-start(s8[10616832]{0:T(1024)(128)(4,1)} %bitcast.158), calls=%async_computation.23 | async-start | bytes 8388608
  730.1 42.1 %collective-permute-start.14 = (bf16[256,2304]{1,0:T(8,128)(2,1)}, bf16[256,2304]{1,0:T(8,128)(2,1)S(1)}, u32[]{:S(2)}, u32[]{:S(2)}) collective-permute-start(bf16[256,2304]{1,0:T(8,128)(2,1)} %fusion.24), channel_id=1, source_target_pairs={{0,1},{1,0},{2,3},{3,2},{4,5},{5,4},{6,7},{7,6},{8,9},{9,8},{10,11... | collective-permute-start | bytes 3538952 | tf_op jit(solution)/shard_map/ppermute | solution.py:331
  745.7 53.4 %collective-permute-start.13 = (bf16[256,2304]{1,0:T(8,128)(2,1)}, bf16[256,2304]{1,0:T(8,128)(2,1)}, u32[]{:S(2)}, u32[]{:S(2)}) collective-permute-start(bf16[256,2304]{1,0:T(8,128)(2,1)} %fusion.23), channel_id=1, source_target_pairs={{0,2},{1,3},{2,0},{3,1},{4,6},{5,7},{6,4},{7,5},{8,10},{9,11},{10,... | collective-permute-start | bytes 3538952 | tf_op jit(solution)/shard_map/ppermute | solution.py:331
  761.5 37.6 %copy-start.41 = (f32[2304]{0:T(1024)S(1)}, f32[2304]{0:T(1024)}, u32[]{:S(2)}) copy-start(f32[2304]{0:T(1024)} %mul.501) | copy-start | bytes 27652
  761.5 37.6 %copy-start.51 = (f32[256]{0:T(256)S(1)}, f32[256]{0:T(256)}, u32[]{:S(2)}) copy-start(f32[256]{0:T(256)} %copy-done.50) | copy-start | bytes 3076
  761.5 37.6 %collective-permute-start.12 = (bf16[256,2304]{1,0:T(8,128)(2,1)}, bf16[256,2304]{1,0:T(8,128)(2,1)S(1)}, u32[]{:S(2)}, u32[]{:S(2)}) collective-permute-start(bf16[256,2304]{1,0:T(8,128)(2,1)} %fusion.22), channel_id=1, source_target_pairs={{0,3},{1,2},{2,1},{3,0},{4,7},{5,6},{6,5},{7,4},{8,11},{9,10},{10,... | collective-permute-start | bytes 3538952 | tf_op jit(solution)/shard_map/ppermute | solution.py:331
  772.1 37.9 %copy-start.3 = (f32[256,2304]{1,0:T(8,128)S(1)}, f32[256,2304]{1,0:T(8,128)}, u32[]{:S(2)}) copy-start(f32[256,2304]{1,0:T(8,128)} %copy-done.2) | copy-start | bytes 7077892
  815.3 53.4 %copy-start.1 = (bf16[2304,512]{1,0:T(8,128)(2,1)S(1)}, bf16[2304,512]{1,0:T(8,128)(2,1)}, u32[]{:S(2)}) copy-start(bf16[2304,512]{1,0:T(8,128)(2,1)} %all-gather.10.cloned.1.call-done) | copy-start | bytes 7077892
  815.4 29.8 %collective-permute-start.17 = (bf16[256,2304]{1,0:T(8,128)(2,1)S(1)}, bf16[256,2304]{1,0:T(8,128)(2,1)S(1)}, u32[]{:S(2)}, u32[]{:S(2)}) collective-permute-start(bf16[256,2304]{1,0:T(8,128)(2,1)S(1)} %multiply_convert_fusion.2), channel_id=1, source_target_pairs={{0,3},{1,2},{2,1},{3,0},{4,7},{5,6},{6,5},{7,4},{8,11},{9,10},{10,... | collective-permute-start | bytes 3538952 | tf_op jit(solution)/shard_map/ppermute | solution.py:331
  816.7 51.7 %collective-permute-start.16 = (bf16[256,2304]{1,0:T(8,128)(2,1)S(1)}, bf16[256,2304]{1,0:T(8,128)(2,1)S(1)}, u32[]{:S(2)}, u32[]{:S(2)}) collective-permute-start(bf16[256,2304]{1,0:T(8,128)(2,1)S(1)} %multiply_convert_fusion.2), channel_id=1, source_target_pairs={{0,2},{1,3},{2,0},{3,1},{4,6},{5,7},{6,4},{7,5},{8,10},{9,11},{10,... | collective-permute-start | bytes 3538952 | tf_op jit(solution)/shard_map/ppermute | solution.py:331
  817.9 50.5 %collective-permute-start.15 = (bf16[256,2304]{1,0:T(8,128)(2,1)S(1)}, bf16[256,2304]{1,0:T(8,128)(2,1)S(1)}, u32[]{:S(2)}, u32[]{:S(2)}) collective-permute-start(bf16[256,2304]{1,0:T(8,128)(2,1)S(1)} %multiply_convert_fusion.2), channel_id=1, source_target_pairs={{0,1},{1,0},{2,3},{3,2},{4,5},{5,4},{6,7},{7,6},{8,9},{9,8},{10,11... | collective-permute-start | bytes 3538952 | tf_op jit(solution)/shard_map/ppermute | solution.py:331
  887.3 149.9 %reduce-scatter.11.cloned.1.call-start = ((), (), s32[]{:S(2)}) async-start(), calls=%async_computation.13 | async-start | bytes 1474560 | tf_op jit(solution)/shard_map/reduce_scatter | solution.py:477
  902.5 15.1 %collective-permute-start.26 = (bf16[1152,2304]{1,0:T(8,128)(2,1)}, bf16[1152,2304]{1,0:T(8,128)(2,1)}, u32[]{:S(2)}, u32[]{:S(2)}) collective-permute-start(bf16[1152,2304]{1,0:T(8,128)(2,1)} %convolution_convert_fusion.2), channel_id=1, source_target_pairs={{0,16},{16,0},{1,17},{17,1},{2,18},{18,2},{3,19},{19,3},{4,20},{20... | collective-permute-start | bytes 15925256 | tf_op jit(solution)/shard_map/ppermute | solution.py:331
  905.0 8.1 collective-permute-start.25
  917.3 220.3 %reduce-scatter.13.cloned.1.call-start = ((), (), s32[]{:S(2)}) async-start(), calls=%async_computation.14 | async-start | bytes 6635520 | tf_op jit(solution)/shard_map/reduce_scatter | solution.py:477
  929.0 293.5 %reduce-scatter.15.cloned.1.call-start = ((), (), s32[]{:S(2)}) async-start(), calls=%async_computation.15 | async-start | bytes 6635520 | tf_op jit(solution)/shard_map/reduce_scatter | solution.py:477
  938.0 8.8 collective-permute-start.27
  957.6 362.7 %reduce-scatter.17.cloned.1.call-start = ((), (), s32[]{:S(2)}) async-start(), calls=%async_computation.16 | async-start | bytes 6635520 | tf_op jit(solution)/shard_map/reduce_scatter | solution.py:477
  959.2 19.1 %slice-start.7 = ((s8[4718592]{0:T(1024)(128)(4,1)}), s8[4194304]{0:T(1024)(128)(4,1)S(1)}, s32[]{:S(2)}) async-start(s8[4718592]{0:T(1024)(128)(4,1)} %bitcast.162), calls=%async_computation.25 | async-start | bytes 8388608
  960.8 17.5 %slice-start.8 = ((s8[4718592]{0:T(1024)(128)(4,1)}), s8[524288]{0:T(1024)(128)(4,1)S(1)}, s32[]{:S(2)}) async-start(s8[4718592]{0:T(1024)(128)(4,1)} %bitcast.162), calls=%async_computation.26 | async-start | bytes 1048576
  969.5 8.8 collective-permute-start.28
  985.8 385.2 %reduce-scatter.9.cloned.1.call-start = ((), (), s32[]{:S(2)}) async-start(), calls=%async_computation.12 | async-start | bytes 2949120 | tf_op jit(solution)/shard_map/reduce_scatter | solution.py:477
  996.9 20.2 %slice-start = ((s8[4718592]{0:T(1024)(128)(4,1)}), s8[524288]{0:T(1024)(128)(4,1)S(1)}, s32[]{:S(2)}) async-start(s8[4718592]{0:T(1024)(128)(4,1)} %bitcast.140), calls=%async_computation.18 | async-start | bytes 1048576
  1003.5 13.6 slice-start.1
  1009.7 7.3 collective-permute-start.21
  1015.6 29.1 %collective-permute-start.20 = (bf16[256,2304]{1,0:T(8,128)(2,1)}, bf16[256,2304]{1,0:T(8,128)(2,1)}, u32[]{:S(2)}, u32[]{:S(2)}) collective-permute-start(bf16[256,2304]{1,0:T(8,128)(2,1)} %convolution_convert_fusion.6), channel_id=1, source_target_pairs={{0,1},{1,0},{2,3},{3,2},{4,5},{5,4},{6,7},{7,6},{8,9},{9,8},{10,11... | collective-permute-start | bytes 3538952 | tf_op jit(solution)/shard_map/ppermute | solution.py:331
  1029.2 53.8 %copy-start.39 = (f32[2304]{0:T(1024)S(1)}, f32[2304]{0:T(1024)}, u32[]{:S(2)}) copy-start(f32[2304]{0:T(1024)} %copy-done.38) | copy-start | bytes 27652
  1029.2 53.8 %collective-permute-start.19 = (bf16[256,2304]{1,0:T(8,128)(2,1)}, bf16[256,2304]{1,0:T(8,128)(2,1)}, u32[]{:S(2)}, u32[]{:S(2)}) collective-permute-start(bf16[256,2304]{1,0:T(8,128)(2,1)} %convolution_convert_fusion.7), channel_id=1, source_target_pairs={{0,2},{1,3},{2,0},{3,1},{4,6},{5,7},{6,4},{7,5},{8,10},{9,11},{10,... | collective-permute-start | bytes 3538952 | tf_op jit(solution)/shard_map/ppermute | solution.py:331
  1035.6 47.5 %collective-permute-start.18 = (bf16[256,2304]{1,0:T(8,128)(2,1)}, bf16[256,2304]{1,0:T(8,128)(2,1)}, u32[]{:S(2)}, u32[]{:S(2)}) collective-permute-start(bf16[256,2304]{1,0:T(8,128)(2,1)} %convolution_convert_fusion.8), channel_id=1, source_target_pairs={{0,3},{1,2},{2,1},{3,0},{4,7},{5,6},{6,5},{7,4},{8,11},{9,10},{10,... | collective-permute-start | bytes 3538952 | tf_op jit(solution)/shard_map/ppermute | solution.py:331
  1039.0 94.2 %copy-start.6 = (f32[256,2304]{1,0:T(8,128)S(1)}, f32[256,2304]{1,0:T(8,128)}, u32[]{:S(2)}) copy-start(f32[256,2304]{1,0:T(8,128)} %copy-done.5) | copy-start | bytes 7077892
  1373.1 9.9 collective-permute-start.22
  1374.5 14.6 %collective-permute-start.23 = (bf16[288,512]{1,0:T(8,128)(2,1)S(1)}, bf16[288,512]{1,0:T(8,128)(2,1)S(1)}, u32[]{:S(2)}, u32[]{:S(2)}) collective-permute-start(bf16[288,512]{1,0:T(8,128)(2,1)S(1)} %get-tuple-element.82), channel_id=1, source_target_pairs={{0,2},{1,3},{2,0},{3,1},{4,6},{5,7},{6,4},{7,5},{8,10},{9,11},{10,... | collective-permute-start | bytes 884744 | tf_op jit(solution)/shard_map/ppermute | solution.py:331
  1376.0 13.3 collective-permute-start.24
  (46 other events, 245.2 us)
Sparse Core Ops, SparseCore 0:
  10.3 54.3 all-gather.7
  75.6 79.5 all-gather.17
  156.8 99.0 all-gather.11
  257.3 98.8 all-gather.13
  357.6 29.9 all-gather.9
  389.1 99.5 all-gather.15
  887.4 109.3 reduce-scatter.6
  999.3 29.6 reduce-scatter.10
  1031.4 93.5 reduce-scatter.12
  1127.1 95.3 reduce-scatter.14
  1224.9 95.3 reduce-scatter.16
  1322.4 48.5 reduce-scatter.8

commit v2 on v1

v2 whole, which is shorter than its diff:
```python
import functools

import jax
import jax.numpy as jnp
from jax import lax
from jax.experimental import pallas as pl
from jax.experimental.pallas import tpu as pltpu
from jax.sharding import PartitionSpec as P

Q_HEADS = 8
KV_HEADS = 4
HEAD_DIM = 256
WINDOW = 4096

EPSILON = 1e-06
SOFT_CAP = 50.0
ROPE_BASE = 10000.0
MESH = pl.DeviceIdType.MESH
VMEM_LIMIT = 56 * 1024 * 1024
LANES = 128
BF16 = jnp.bfloat16
F32 = jnp.float32


def after(value, *earlier):
    return lax.optimization_barrier((value, *earlier))[0]


def dot_nn(left, right):
    return lax.dot_general(left, right, (((1,), (0,)), ((), ())), preferred_element_type=F32)


def dot_nt(left, right):
    return lax.dot_general(left, right, (((1,), (1,)), ((), ())), preferred_element_type=F32)


def dot_tn(left, right):
    return lax.dot_general(left, right, (((0,), (0,)), ((), ())), preferred_element_type=F32)


def rms_scale(vector):
    return lax.rsqrt(jnp.mean(vector * vector, axis=-1, keepdims=True) + EPSILON)


def rotary(vector, cosine, sine, direction):
    half_dim = vector.shape[-1] // 2
    first_half = vector[..., :half_dim]
    second_half = vector[..., half_dim:]
    return jnp.concatenate(
        [
            first_half * cosine - direction * (second_half * sine),
            second_half * cosine + direction * (first_half * sine),
        ],
        axis=-1,
    )


def gather_kernel(sizes, x_ref, o_ref, send_sem, recv_sem):
    dp_size, seq_size = sizes
    count = dp_size * seq_size
    dp, seq, mp = lax.axis_index("dp"), lax.axis_index("seq"), lax.axis_index("mp")
    rank = dp * seq_size + seq

    def peer(k):
        other = lax.rem(rank + k, count)
        return (other // seq_size, lax.rem(other, seq_size), mp)

    barrier = pltpu.get_barrier_semaphore()
    for k in range(1, count):
        pl.semaphore_signal(barrier, inc=1, device_id=peer(k), device_id_type=MESH)
    pl.semaphore_wait(barrier, count - 1)
    copies = []
    for k in range(1, count):
        copies.append(
            pltpu.make_async_remote_copy(
                src_ref=x_ref,
                dst_ref=o_ref.at[rank],
                send_sem=send_sem.at[k],
                recv_sem=recv_sem.at[k],
                device_id=peer(k),
                device_id_type=MESH,
            )
        )
        copies[-1].start()
    o_ref[pl.ds(rank, 1)] = x_ref[...][None]
    for copy in copies:
        copy.wait()


def gather_gains(gains, dp_size, seq_size):
    count = dp_size * seq_size
    local = gains[0].shape[0]
    width = -(-local // LANES) * LANES
    block = jnp.stack([gain.astype(F32) for gain in gains])
    block = jnp.pad(block, ((0, 8 - len(gains)), (0, width - local)))
    full = pl.pallas_call(
        functools.partial(gather_kernel, (dp_size, seq_size)),
        out_shape=jax.ShapeDtypeStruct((count, 8, width), F32),
        in_specs=[pl.BlockSpec(memory_space=pltpu.VMEM)],
        out_specs=pl.BlockSpec(memory_space=pltpu.VMEM),
        scratch_shapes=[
            pltpu.SemaphoreType.DMA((count,)),
            pltpu.SemaphoreType.DMA((count,)),
        ],
        compiler_params=pltpu.CompilerParams(collective_id=1, has_side_effects=True),
    )(block)
    full = jnp.transpose(full[:, : len(gains), :local], (1, 0, 2)).reshape(len(gains), -1)
    return [full[i : i + 1] for i in range(len(gains))]


def flipped(index, k):
    result, bit = index, 1
    while bit <= k:
        if k & bit:
            result = result + bit * (1 - 2 * lax.rem(index // bit, 2))
        bit *= 2
    return result


def last_kernel(sizes, heads, x_ref, kv_ref, o_ref, key_ref, value_ref, mine, from_mp, from_ws, kv_from, sems):
    dp_size, seq_size, mp_size = sizes
    count = dp_size * seq_size
    dp, seq, mp = lax.axis_index("dp"), lax.axis_index("seq"), lax.axis_index("mp")
    rank = dp * seq_size + seq

    def mp_peer(k):
        return (dp, seq, flipped(mp, k))

    def ws_rank(k):
        return lax.rem(rank + k, count)

    def ws_peer(k):
        other = ws_rank(k)
        return (other // seq_size, lax.rem(other, seq_size), mp)

    def remote(src, dst, kind, k, device):
        copy = pltpu.make_async_remote_copy(
            src_ref=src,
            dst_ref=dst,
            send_sem=sems.at[kind, 0, k],
            recv_sem=sems.at[kind, 1, k],
            device_id=device,
            device_id_type=MESH,
        )
        copy.start()
        return copy

    barrier = pltpu.get_barrier_semaphore()
    for k in range(1, mp_size):
        pl.semaphore_signal(barrier, inc=1, device_id=mp_peer(k), device_id_type=MESH)
    for k in range(1, count):
        pl.semaphore_signal(barrier, inc=1, device_id=ws_peer(k), device_id_type=MESH)
    pl.semaphore_wait(barrier, mp_size - 1 + count - 1)
    copies = [remote(x_ref, from_mp.at[k], 0, k, mp_peer(k)) for k in range(1, mp_size)]
    kv_copies = [remote(kv_ref, kv_from.at[k], 1, k, mp_peer(k)) for k in range(1, mp_size)]
    for copy in copies:
        copy.wait()
    total = x_ref[...]
    for k in range(1, mp_size):
        total = total + from_mp[k]
    mine[...] = total
    copies = [remote(mine.at[ws_rank(k)], from_ws.at[k], 2, k, ws_peer(k)) for k in range(1, count)]
    key_ref[...] = jnp.zeros_like(key_ref)
    value_ref[...] = jnp.zeros_like(value_ref)
    for k in range(mp_size):
        if k:
            kv_copies[k - 1].wait()
        piece = (kv_from[k] if k else kv_ref[...]).astype(F32)
        head = flipped(mp, k) * heads // (Q_HEADS // KV_HEADS)
        columns = pl.ds(pl.multiple_of(head * HEAD_DIM, HEAD_DIM), HEAD_DIM)
        key_ref[:, columns] += piece[:, :HEAD_DIM]
        value_ref[:, columns] += piece[:, HEAD_DIM:]
    for copy in copies:
        copy.wait()
    own = mine[pl.ds(rank, 1)][0]
    for k in range(1, count):
        own = own + from_ws[k]
    o_ref[...] = own


def last_sums(grads, kv, kv_width, heads, sizes):
    dp_size, seq_size, mp_size = sizes
    count = dp_size * seq_size
    local = grads[0].shape[0] // count
    width = -(-local // LANES) * LANES
    block = jnp.transpose(jnp.stack(grads).reshape(len(grads), count, local), (1, 0, 2))
    block = jnp.pad(block, ((0, 0), (0, 8 - len(grads)), (0, width - local)))
    kv_out = jax.ShapeDtypeStruct((kv.shape[0], kv_width), F32)
    total, key, value = pl.pallas_call(
        functools.partial(last_kernel, sizes, heads),
        out_shape=(jax.ShapeDtypeStruct((8, width), F32), kv_out, kv_out),
        in_specs=[pl.BlockSpec(memory_space=pltpu.VMEM)] * 2,
        out_specs=(pl.BlockSpec(memory_space=pltpu.VMEM),) * 3,
        scratch_shapes=[
            pltpu.VMEM((count, 8, width), F32),
            pltpu.VMEM((mp_size, count, 8, width), F32),
            pltpu.VMEM((count, 8, width), F32),
            pltpu.VMEM((mp_size, *kv.shape), BF16),
            pltpu.SemaphoreType.DMA((3, 2, max(count, mp_size))),
        ],
        compiler_params=pltpu.CompilerParams(
            collective_id=2, has_side_effects=True, vmem_limit_bytes=VMEM_LIMIT
        ),
    )(block, kv)
    return [total[i, :local] for i in range(len(grads))], key, value


def key_mask(shape, first_key, first_query, tile, far):
    key = first_key + lax.broadcasted_iota(jnp.int32, shape, 0)
    query = first_query + lax.rem(lax.broadcasted_iota(jnp.int32, shape, 1), tile)
    return key > query if far else key <= query


def for_key_tiles(tile_fn, index, tile, span, step, hops, windowed):
    seq = lax.axis_index("seq")
    per_block = span // step
    last = jnp.minimum(seq, hops)
    if windowed:
        @pl.when(seq >= hops)
        def _():
            tile_fn(pl.multiple_of((seq - hops) * span, span), span, "far")

        last = jnp.minimum(seq, hops - 1)

    def past(t, carry):
        tile_fn(pl.multiple_of(t * step, step), step, "")
        return carry

    lax.fori_loop((seq - last) * per_block, seq * per_block, past, 0)
    tile_fn(pl.multiple_of(seq * span, span), (index + 1) * tile, "near")


def head_rows(ref, index, tile):
    block = ref[pl.ds(index * tile, tile), :]
    return jnp.concatenate(
        [block[:, h * HEAD_DIM : (h + 1) * HEAD_DIM] for h in range(ref.shape[1] // HEAD_DIM)], axis=0
    )


def put_head_rows(ref, index, tile, rows):
    for h in range(ref.shape[1] // HEAD_DIM):
        ref[pl.ds(index * tile, tile), h * HEAD_DIM : (h + 1) * HEAD_DIM] = rows[
            h * tile : (h + 1) * tile
        ].astype(ref.dtype)


def attend_kernel(plan, q_ref, kv_ref, o_ref, of_ref, lse_ref, acc, total):
    tile, span, step, hops, windowed = plan
    for i in range(span // tile):
        query = head_rows(q_ref, i, tile)
        rows = query.shape[0]
        acc[...] = jnp.zeros_like(acc)
        total[...] = jnp.zeros_like(total)

        def tile_fn(first, count, mask, i=i, query=query, rows=rows):
            key = kv_ref[pl.ds(first, count), :HEAD_DIM]
            value = kv_ref[pl.ds(first, count), HEAD_DIM:]
            raw = dot_nt(key, query)
            weight = jnp.exp(SOFT_CAP * jnp.tanh(raw * (1.0 / SOFT_CAP)))
            if mask:
                inside = key_mask(weight.shape, 0, i * tile, tile, mask == "far")
                weight = jnp.where(inside, weight, 0.0)
            total[...] += jnp.sum(weight.reshape(count // 8, 8, rows), axis=0)
            acc[...] += dot_tn(value, weight.astype(BF16))

        for_key_tiles(tile_fn, i, tile, span, step, hops, windowed)
        row_total = jnp.sum(total[...], axis=0, keepdims=True)
        out = (acc[...] / row_total).T
        put_head_rows(o_ref, i, tile, out)
        put_head_rows(of_ref, i, tile, out)
        lse_ref[i] = jnp.log(row_total)


def attend_back_kernel(plan, q_ref, do_ref, of_ref, lse_ref, kv_ref, dq_ref, dkv_ref, grads, acc):
    tile, span, step, hops, windowed = plan
    grads[...] = jnp.zeros_like(grads)
    for i in range(span // tile):
        query = head_rows(q_ref, i, tile)
        dout = head_rows(do_ref, i, tile)
        lse = lse_ref[i]
        delta = jnp.sum(dout.astype(F32) * head_rows(of_ref, i, tile), axis=-1, keepdims=True)
        delta = jnp.broadcast_to(delta, (delta.shape[0], LANES)).T[:1]
        acc[...] = jnp.zeros_like(acc)

        def tile_fn(first, count, mask, i=i, query=query, dout=dout, lse=lse, delta=delta):
            key = kv_ref[pl.ds(first, count), :HEAD_DIM]
            value = kv_ref[pl.ds(first, count), HEAD_DIM:]
            bounded = jnp.tanh(dot_nt(key, query) * (1.0 / SOFT_CAP))
            prob = jnp.exp(SOFT_CAP * bounded - lse)
            if mask:
                inside = key_mask(prob.shape, 0, i * tile, tile, mask == "far")
                prob = jnp.where(inside, prob, 0.0)
            dprob = dot_nt(value, dout)
            draw = (prob * (dprob - delta) * (1.0 - bounded * bounded)).astype(BF16)
            grads[pl.ds(first, count), HEAD_DIM:] += dot_nn(prob.astype(BF16), dout)
            grads[pl.ds(first, count), :HEAD_DIM] += dot_nn(draw, query)
            acc[...] += dot_tn(key, draw)

        for_key_tiles(tile_fn, i, tile, span, step, hops, windowed)
        put_head_rows(dq_ref, i, tile, acc[...].T)
    dkv_ref[...] = grads[...].astype(BF16)


def attention_plan(span, seq_size):
    hops = min(WINDOW // span, seq_size - 1)
    return (min(256, span), span, min(512, span), hops, seq_size * span > WINDOW)


def attend(queries, pairs, plan):
    tile, span = plan[:2]
    heads = queries.shape[1] // HEAD_DIM
    rows = heads * tile
    return pl.pallas_call(
        functools.partial(attend_kernel, plan),
        out_shape=(
            jax.ShapeDtypeStruct(queries.shape, BF16),
            jax.ShapeDtypeStruct(queries.shape, F32),
            jax.ShapeDtypeStruct((span // tile, 1, rows), F32),
        ),
        in_specs=[pl.BlockSpec(memory_space=pltpu.VMEM)] * 2,
        out_specs=(pl.BlockSpec(memory_space=pltpu.VMEM),) * 3,
        scratch_shapes=[pltpu.VMEM((HEAD_DIM, rows), F32), pltpu.VMEM((8, rows), F32)],
        compiler_params=pltpu.CompilerParams(vmem_limit_bytes=VMEM_LIMIT),
        cost_estimate=pl.CostEstimate(
            flops=12 * queries.size * span, bytes_accessed=8 * queries.size, transcendentals=0
        ),
    )(queries, pairs)


def attend_back(queries, dout, exact, lse, pairs, plan):
    tile, span = plan[:2]
    rows = queries.shape[1] // HEAD_DIM * tile
    return pl.pallas_call(
        functools.partial(attend_back_kernel, plan),
        out_shape=(
            jax.ShapeDtypeStruct(queries.shape, F32),
            jax.ShapeDtypeStruct(pairs.shape, BF16),
        ),
        in_specs=[pl.BlockSpec(memory_space=pltpu.VMEM)] * 5,
        out_specs=(pl.BlockSpec(memory_space=pltpu.VMEM),) * 2,
        scratch_shapes=[pltpu.VMEM(pairs.shape, F32), pltpu.VMEM((HEAD_DIM, rows), F32)],
        compiler_params=pltpu.CompilerParams(vmem_limit_bytes=VMEM_LIMIT),
        cost_estimate=pl.CostEstimate(
            flops=30 * queries.size * span, bytes_accessed=8 * queries.size, transcendentals=0
        ),
    )(queries, dout, exact, lse, pairs)


def remote_copy(src, dst, sems, index, device):
    copy = pltpu.make_async_remote_copy(
        src_ref=src,
        dst_ref=dst,
        send_sem=sems.at[(0, *index)],
        recv_sem=sems.at[(1, *index)],
        device_id=device,
        device_id_type=MESH,
    )
    copy.start()
    return copy


def sum_direct(parts_at, steps, step, mp_size, peer, total, sent, arrived, sems):
    copies = []
    for t in range(steps):
        for k in range(mp_size - 1, -1, -1):
            part = parts_at(t, k)
            if k == 0:
                total[:, t * step : (t + 1) * step] = part
            else:
                sent[t, k - 1] = part.astype(BF16)
                copies.append(
                    remote_copy(sent.at[t, k - 1], arrived.at[t, k - 1], sems, (t, k - 1), peer(k))
                )
    for t in range(steps):
        for k in range(1, mp_size):
            copies[t * (mp_size - 1) + mp_size - 1 - k].wait_recv()
            total[:, t * step : (t + 1) * step] += arrived[t, k - 1].astype(F32)
    return copies


def sum_square(parts_at, steps, step, peer, total, kept, sent, arrived, sems):
    half = step // 2
    copies, second = [], []
    for t in range(steps):
        first = t * step
        far = parts_at(t, 3)
        sent[t, 0, 1] = far[:, :half].astype(BF16)
        sent[t, 1, 1] = far[:, half:].astype(BF16)
        part = parts_at(t, 1)
        sent[t, 0, 0] = part[:, :half].astype(BF16)
        kept[t, 0] = part[:, half:]
        copies.append(
            remote_copy(sent.at[t, 0, pl.ds(0, 2)], arrived.at[t, 0, pl.ds(0, 2)], sems, (t, 0), peer(1))
        )
        part = parts_at(t, 2)
        sent[t, 1, 0] = part[:, half:].astype(BF16)
        kept[t, 1] = part[:, :half]
        copies.append(
            remote_copy(sent.at[t, 1, pl.ds(0, 2)], arrived.at[t, 1, pl.ds(0, 2)], sems, (t, 1), peer(2))
        )
        total[:, first : first + step] = parts_at(t, 0)
    for t in range(steps):
        copies[2 * t].wait_recv()
        sent[t, 1, 2] = (kept[t, 1] + arrived[t, 0, 1].astype(F32)).astype(BF16)
        second.append(remote_copy(sent.at[t, 1, 2], arrived.at[t, 1, 2], sems, (t, 2), peer(2)))
        copies[2 * t + 1].wait_recv()
        sent[t, 0, 2] = (kept[t, 0] + arrived[t, 1, 1].astype(F32)).astype(BF16)
        second.append(remote_copy(sent.at[t, 0, 2], arrived.at[t, 0, 2], sems, (t, 3), peer(1)))
    for t in range(steps):
        first = t * step
        second[2 * t].wait_recv()
        total[:, first : first + half] += arrived[t, 0, 0].astype(F32) + arrived[t, 1, 2].astype(F32)
        second[2 * t + 1].wait_recv()
        total[:, first + half : first + step] += arrived[t, 1, 0].astype(F32) + arrived[t, 0, 2].astype(
            F32
        )
    return copies + second


def gather_direct(own, gathered, share, mp_size, peer, sems):
    copies = [
        remote_copy(own, gathered.at[pl.ds(k * share, share)], sems, (k,), peer(k))
        for k in range(mp_size - 1, 0, -1)
    ]
    for copy in copies:
        copy.wait()


def gather_square(own, gathered, share, peer, sems):
    half = share // 2

    def place(k, lower):
        return gathered.at[pl.ds(k * share + lower * half, half)]

    upper, lower = own.at[pl.ds(0, half)], own.at[pl.ds(half, half)]
    to_one = remote_copy(upper, place(1, 0), sems, (0,), peer(1))
    to_two = remote_copy(lower, place(2, 1), sems, (1,), peer(2))
    copies = [
        remote_copy(upper, place(2, 0), sems, (2,), peer(2)),
        remote_copy(lower, place(1, 1), sems, (3,), peer(1)),
    ]
    to_one.wait_recv()
    copies.append(remote_copy(place(1, 0), place(3, 0), sems, (4,), peer(2)))
    to_two.wait_recv()
    copies.append(remote_copy(place(2, 1), place(3, 1), sems, (5,), peer(1)))
    to_one.wait_send()
    to_two.wait_send()
    for copy in copies:
        copy.wait()


def rows_kernel(plan, rows_fn, *refs):
    mp_size, share, step, row_step, natural, n_left, n_aux, n_out, gather = plan
    lefts, weight_ref, refs = refs[:n_left], refs[n_left], refs[n_left + 1 :]
    aux, refs = refs[:n_aux], refs[n_aux:]
    outs, refs = refs[:n_out], refs[n_out:]
    if gather:
        gathered, refs = refs[0], refs[1:]
    left, weight, kept, sent, arrived, total, own, in_sem, sum_sem, row_sem = refs
    steps = total.shape[1] // step
    dp, seq, mp = lax.axis_index("dp"), lax.axis_index("seq"), lax.axis_index("mp")

    def peer(k):
        return (dp, seq, flipped(mp, k))

    left_copies, weight_copies = {}, []
    for k in range(mp_size):
        first = (flipped(mp, k) if natural else k) * share
        left_copies[k] = []
        column = 0
        for i, ref in enumerate(lefts):
            depth = ref.shape[1]
            left_copies[k].append(
                pltpu.make_async_copy(
                    ref.at[pl.ds(first, share)],
                    left.at[k, :, pl.ds(column, depth)],
                    in_sem.at[2 + k * n_left + i],
                )
            )
            column += depth
    for t in range(steps):
        weight_copies.append(
            pltpu.make_async_copy(
                weight_ref.at[pl.ds(t * step, step)], weight.at[t % 2], in_sem.at[t % 2]
            )
        )
    weight_copies[0].start()
    for k in range(mp_size - 1, -1, -1):
        for copy in left_copies[k]:
            copy.start()

    barrier = pltpu.get_barrier_semaphore()
    for k in range(1, mp_size):
        pl.semaphore_signal(barrier, inc=1, device_id=peer(k), device_id_type=MESH)
    pl.semaphore_wait(barrier, mp_size - 1)

    def parts_at(t, k):
        if k == mp_size - 1:
            weight_copies[t].wait()
            if t + 1 < steps:
                weight_copies[t + 1].start()
        if t == 0:
            for copy in left_copies[k]:
                copy.wait()
        return dot_nt(left[k], weight[t % 2])

    if mp_size == 4:
        sums = sum_square(parts_at, steps, step, peer, total, kept, sent, arrived, sum_sem)
    else:
        sums = sum_direct(parts_at, steps, step, mp_size, peer, total, sent, arrived, sum_sem)

    def rows_at(r, carry):
        rows = pl.ds(pl.multiple_of(r * row_step, row_step), row_step)
        result = rows_fn(total[rows, :], rows, aux, outs)
        if gather:
            own[rows, :] = result.astype(BF16)
        return carry

    for ref in outs:
        if ref.shape[0] == 8:
            ref[...] = jnp.zeros_like(ref)
    lax.fori_loop(0, share // row_step, rows_at, 0)
    if gather:
        keep = pltpu.make_async_copy(own, gathered.at[pl.ds(0, share)], in_sem.at[0])
        keep.start()
        if mp_size == 4:
            gather_square(own, gathered, share, peer, row_sem)
        else:
            gather_direct(own, gathered, share, mp_size, peer, row_sem)
        keep.wait()
    for copy in sums:
        copy.wait_send()


def sum_rows(lefts, weight, rows_fn, aux, outs, gather, natural, mp_size, collective_id):
    span = lefts[0].shape[0]
    width, depth = weight.shape
    share = span // mp_size
    step = 768 if width % 768 == 0 else width
    row_step = min(32, share)
    steps = width // step
    plan = (mp_size, share, step, row_step, natural, len(lefts), len(aux), len(outs), gather)
    out_shape = [jax.ShapeDtypeStruct((rows, width), dtype) for rows, dtype in outs]
    out_specs = [pl.BlockSpec(memory_space=pltpu.VMEM)] * len(outs)
    if gather:
        out_shape.append(jax.ShapeDtypeStruct((span, width), BF16))
        out_specs.append(pl.BlockSpec(memory_space=pl.ANY))
    if mp_size == 4:
        pieces, kept = (steps, 2, 3, share, step // 2), (steps, 2, share, step // 2)
    else:
        pieces, kept = (steps, mp_size - 1, share, step), (8, LANES)
    return pl.pallas_call(
        functools.partial(rows_kernel, plan, rows_fn),
        out_shape=out_shape,
        in_specs=[pl.BlockSpec(memory_space=pl.ANY)] * (len(lefts) + 1)
        + [pl.BlockSpec(memory_space=pltpu.VMEM)] * len(aux),
        out_specs=out_specs,
        scratch_shapes=[
            pltpu.VMEM((mp_size, share, depth), BF16),
            pltpu.VMEM((2, step, depth), BF16),
            pltpu.VMEM(kept, F32),
            pltpu.VMEM(pieces, BF16),
            pltpu.VMEM(pieces, BF16),
            pltpu.VMEM((share, width), F32),
            pltpu.VMEM((share, width), BF16),
            pltpu.SemaphoreType.DMA((2 + mp_size * len(lefts),)),
            pltpu.SemaphoreType.DMA((2, steps, max(4, mp_size - 1))),
            pltpu.SemaphoreType.DMA((2, max(6, mp_size))),
        ],
        compiler_params=pltpu.CompilerParams(
            collective_id=collective_id, has_side_effects=True, vmem_limit_bytes=VMEM_LIMIT
        ),
    )(*lefts, weight, *aux)


def weight_grad_kernel(plan, *refs):
    n_right, tile, half = plan
    left_ref, rights, out_ref = refs[0], refs[1 : 1 + n_right], refs[1 + n_right]
    left, right, sent, arrived, own, result, in_sem, swap_sem, out_sem = refs[2 + n_right :]
    dp, seq, mp = lax.axis_index("dp"), lax.axis_index("seq"), lax.axis_index("mp")
    other = (1 - dp, seq, mp)
    lefts = []
    for i, side in enumerate((1 - dp, dp)):
        columns = pl.ds(pl.multiple_of(side * half, LANES), half)
        lefts.append(pltpu.make_async_copy(left_ref.at[:, columns], left.at[i], in_sem.at[2 + i]))
        lefts[i].start()
    sources = []
    for ref in rights:
        for first in range(0, ref.shape[1], tile):
            sources.append(ref.at[:, pl.ds(first, tile)])
    tiles = len(sources)
    loads = [
        pltpu.make_async_copy(source, right.at[t % 2], in_sem.at[t % 2])
        for t, source in enumerate(sources)
    ]
    loads[0].start()
    barrier = pltpu.get_barrier_semaphore()
    pl.semaphore_signal(barrier, inc=1, device_id=other, device_id_type=MESH)
    pl.semaphore_wait(barrier, 1)
    swaps, stores = [], []

    def finish(t):
        swaps[t].wait_recv()
        if t >= 2:
            stores[t - 2].wait()
        result[t % 2] = (own[t % 2] + arrived[t].astype(F32)).astype(BF16)
        stores.append(
            pltpu.make_async_copy(
                result.at[t % 2], out_ref.at[:, pl.ds(t * tile, tile)], out_sem.at[t % 2]
            )
        )
        stores[t].start()

    for t in range(tiles):
        loads[t].wait()
        if t + 1 < tiles:
            loads[t + 1].start()
        if t == 0:
            lefts[0].wait()
        sent[t] = dot_tn(left[0], right[t % 2]).astype(BF16)
        swaps.append(remote_copy(sent.at[t], arrived.at[t], swap_sem, (t,), other))
        if t == 0:
            lefts[1].wait()
        own[t % 2] = dot_tn(left[1], right[t % 2])
        if t >= 1:
            finish(t - 1)
    finish(tiles - 1)
    for store in stores[-2:]:
        store.wait()
    for swap in swaps:
        swap.wait_send()


def weight_grad(left, rights, collective_id):
    rows, width = left.shape
    half = width // 2
    total = sum(right.shape[1] for right in rights)
    tile = min(768 if rights[0].shape[1] % 768 == 0 else 384, rights[0].shape[1])
    tile = next(t for t in (tile, 256, LANES) if all(right.shape[1] % t == 0 for right in rights))
    tiles = total // tile
    return pl.pallas_call(
        functools.partial(weight_grad_kernel, (len(rights), tile, half)),
        out_shape=jax.ShapeDtypeStruct((half, total), BF16),
        in_specs=[pl.BlockSpec(memory_space=pl.ANY)] * (1 + len(rights)),
        out_specs=pl.BlockSpec(memory_space=pl.ANY),
        scratch_shapes=[
            pltpu.VMEM((2, rows, half), BF16),
            pltpu.VMEM((2, rows, tile), BF16),
            pltpu.VMEM((tiles, half, tile), BF16),
            pltpu.VMEM((tiles, half, tile), BF16),
            pltpu.VMEM((2, half, tile), F32),
            pltpu.VMEM((2, half, tile), BF16),
            pltpu.SemaphoreType.DMA((4,)),
            pltpu.SemaphoreType.DMA((2, tiles)),
            pltpu.SemaphoreType.DMA((2,)),
        ],
        compiler_params=pltpu.CompilerParams(
            collective_id=collective_id, has_side_effects=True, vmem_limit_bytes=VMEM_LIMIT
        ),
    )(left, *rights)


def hidden_back_kernel(dmixed_ref, down_ref, act_ref, slope_ref, dgate_ref, dup_ref):
    dhidden = dot_nn(dmixed_ref[...], down_ref[...])
    dgate_ref[...] = (dhidden * slope_ref[...].astype(F32)).astype(BF16)
    dup_ref[...] = (dhidden * act_ref[...].astype(F32)).astype(BF16)


def hidden_back(dmixed, down_wt, act, slope):
    rows, width = dmixed.shape
    units = down_wt.shape[1]
    tile = 256 if units % 256 == 0 else units
    columns = pl.BlockSpec((rows, tile), lambda i: (0, i))
    return pl.pallas_call(
        hidden_back_kernel,
        grid=(units // tile,),
        out_shape=(jax.ShapeDtypeStruct((rows, units), BF16),) * 2,
        in_specs=[
            pl.BlockSpec((rows, width), lambda i: (0, 0)),
            pl.BlockSpec((width, tile), lambda i: (0, i)),
            columns,
            columns,
        ],
        out_specs=(columns, columns),
        compiler_params=pltpu.CompilerParams(vmem_limit_bytes=VMEM_LIMIT),
    )(dmixed, down_wt, act, slope)


def fold_rows(x):
    return jnp.sum(x.reshape(x.shape[0] // 8, 8, x.shape[1]), axis=0)


def after_attention(attn, rows, aux, outs):
    tokens, gain_two, gain_three = aux
    attn_out, resid_out = outs
    resid = tokens[rows, :].astype(F32) + attn * rms_scale(attn) * gain_two[...]
    attn_out[rows, :] = attn
    resid_out[rows, :] = resid
    return resid * rms_scale(resid) * gain_three[...]


def after_ffw(mixed, rows, aux, outs):
    resid, cotangent, gain_four = aux
    output, gain_grad = outs
    scale = rms_scale(mixed)
    unit = mixed * scale
    grad_out = cotangent[rows, :].astype(F32)
    output[rows, :] = (resid[rows, :] + unit * gain_four[...]).astype(BF16)
    gain_grad[...] += fold_rows(grad_out * unit)
    return vector_back(grad_out, unit, scale, gain_four[...])


def vector_back(grad_in, unit, scale, gain):
    unit_grad = grad_in * gain
    return scale * (unit_grad - unit * jnp.mean(unit_grad * unit, axis=-1, keepdims=True))


def before_ffw(dnormed_two, rows, aux, outs):
    resid, attn, cotangent, gain_two, gain_three = aux
    dresid_out, gain_two_grad, gain_three_grad = outs
    scale = rms_scale(resid[rows, :])
    unit = resid[rows, :] * scale
    gain_three_grad[...] += fold_rows(dnormed_two * unit)
    dresid = cotangent[rows, :].astype(F32) + vector_back(dnormed_two, unit, scale, gain_three[...])
    dresid_out[rows, :] = dresid
    scale = rms_scale(attn[rows, :])
    unit = attn[rows, :] * scale
    gain_two_grad[...] += fold_rows(dresid * unit)
    return vector_back(dresid, unit, scale, gain_two[...])


def before_attention(dnormed_one, rows, aux, outs):
    tokens, dresid, gain_one = aux
    tokens_grad, gain_grad = outs
    vector = tokens[rows, :].astype(F32)
    scale = rms_scale(vector)
    unit = vector * scale
    gain_grad[...] += fold_rows(dnormed_one * unit)
    back = vector_back(dnormed_one, unit, scale, gain_one[...])
    tokens_grad[rows, :] = (dresid[rows, :] + back).astype(BF16)


def swapped(x, axis, k):
    return lax.ppermute(x, axis, [(i, i ^ k) for i in range(lax.axis_size(axis))])


def shards(
    tokens,
    cotangent,
    pre_attn_gain,
    w_query,
    w_key,
    w_value,
    w_out,
    post_attn_gain,
    pre_ffw_gain,
    w_gate,
    w_up,
    w_down,
    post_ffw_gain,
):
    dp_size, seq_size, mp_size = (lax.axis_size(axis) for axis in ("dp", "seq", "mp"))
    dp, seq, mp = lax.axis_index("dp"), lax.axis_index("seq"), lax.axis_index("mp")
    both = ("dp", "seq")
    heads = w_query.shape[1] // HEAD_DIM
    group = Q_HEADS // KV_HEADS
    kv_first = mp * heads // group
    q_width = heads * HEAD_DIM
    span = tokens.shape[1]
    width = tokens.shape[2]
    share = span // mp_size
    plan = attention_plan(span, seq_size)

    def gather_weight(x):
        return lax.all_gather(x, both, axis=0, tiled=True)

    w_qkv_own = jnp.concatenate(
        [
            w_query,
            lax.dynamic_slice_in_dim(w_key, kv_first * HEAD_DIM, HEAD_DIM, 1),
            lax.dynamic_slice_in_dim(w_value, kv_first * HEAD_DIM, HEAD_DIM, 1),
        ],
        axis=1,
    )
    w_qkv = gather_weight(w_qkv_own)
    gain_one, gain_two, gain_three, gain_four = gather_gains(
        [pre_attn_gain, post_attn_gain, pre_ffw_gain, post_ffw_gain], dp_size, seq_size
    )

    inputs = tokens[0].astype(F32)
    positions = seq * span + jnp.arange(span, dtype=jnp.int32)
    half_dim = HEAD_DIM // 2
    frequency = ROPE_BASE ** (-jnp.arange(half_dim, dtype=F32) * 2.0 / HEAD_DIM)
    angles = positions.astype(F32)[:, None, None] * frequency
    cosine = jnp.cos(angles)
    sine = jnp.sin(angles)
    scale_one = rms_scale(inputs)
    normed_one = (inputs * scale_one * gain_one).astype(BF16)
    w_out_t = gather_weight(after(w_out.T, w_qkv, normed_one))
    key_lin = dot_nn(normed_one, w_qkv[:, q_width : q_width + HEAD_DIM])
    keys_own = rotary(key_lin, cosine[:, 0], sine[:, 0], 1.0).astype(BF16)
    values_own = dot_nn(normed_one, w_qkv[:, q_width + HEAD_DIM :]).astype(BF16)
    own_pair = jnp.concatenate([keys_own, values_own], axis=1)
    pairs = lax.all_gather(after(own_pair, w_out_t), "seq", axis=0, tiled=True)
    query_lin = dot_nn(normed_one, w_qkv[:, :q_width]).reshape(span, heads, HEAD_DIM)
    queries = (rotary(query_lin, cosine, sine, 1.0) * HEAD_DIM ** (-0.5)).astype(BF16)
    queries = queries.reshape(span, q_width)

    ffw = w_gate.shape[1]
    gate_up_w = gather_weight(after(jnp.concatenate([w_gate, w_up], axis=1), pairs))
    gate_w, up_w = gate_up_w[:, :ffw], gate_up_w[:, ffw:]

    attn_o, attn_exact, lse = attend(queries, pairs, plan)
    own_first = mp * share
    tokens_own = lax.dynamic_slice_in_dim(tokens[0], own_first, share, 0)
    cotangent_own = lax.dynamic_slice_in_dim(cotangent[0], own_first, share, 0)

    def by_owner(x):
        return jnp.concatenate(
            [lax.dynamic_slice_in_dim(x, (mp ^ k) * share, share, 0) for k in range(mp_size)], axis=0
        )

    attn, resid, normed_two = sum_rows(
        (attn_o,),
        w_out_t,
        after_attention,
        (tokens_own, gain_two, gain_three),
        ((share, F32), (share, F32)),
        True,
        True,
        mp_size,
        3,
    )
    down_wt = gather_weight(after(w_down.T, gate_up_w, normed_two))

    gate_lin = dot_nn(normed_two, gate_w)
    up_lin = dot_nn(normed_two, up_w)
    gate_act, gelu_pull = jax.vjp(lambda gate_in: jax.nn.gelu(gate_in, approximate=True), gate_lin)
    hidden = (gate_act * up_lin).astype(BF16)
    slope = gelu_pull(up_lin)[0].astype(BF16)
    gate_act = gate_act.astype(BF16)
    output, grad_gain_four, dmixed_low = sum_rows(
        (hidden,),
        down_wt,
        after_ffw,
        (resid, cotangent_own, gain_four),
        ((share, BF16), (8, F32)),
        True,
        False,
        mp_size,
        4,
    )

    def spread(x):
        return lax.psum_scatter(x, "seq", scatter_dimension=0, tiled=True)

    grad_down_sum = weight_grad(dmixed_low, (hidden,), 7)
    grad_down_t = spread(grad_down_sum)
    dgate_low, dup_low = hidden_back(after(dmixed_low, grad_down_sum), down_wt, gate_act, slope)
    grad_gate_up_sum = weight_grad(normed_two, (dgate_low, dup_low), 8)
    dresid, grad_gain_two, grad_gain_three, dattn_low = sum_rows(
        (after(dgate_low, grad_down_t, grad_gate_up_sum), dup_low),
        gate_up_w,
        before_ffw,
        (resid, attn, cotangent_own, gain_two, gain_three),
        ((share, F32), (8, F32), (8, F32)),
        True,
        False,
        mp_size,
        5,
    )
    grad_gate_up = spread(after(grad_gate_up_sum, grad_down_t))

    dattn_o = by_owner(dot_nn(dattn_low, w_out_t)).astype(BF16)
    dquery, dpairs = attend_back(queries, dattn_o, attn_exact, lse, pairs, plan)
    own_grads = spread(after(dpairs, grad_gate_up)).astype(F32)
    dkey_rot = own_grads[:, :HEAD_DIM]
    dkey_low = rotary(dkey_rot, cosine[:, 0], sine[:, 0], -1.0).astype(BF16)
    dvalue_low = own_grads[:, HEAD_DIM:].astype(BF16)
    dquery = dquery.reshape(span, heads, HEAD_DIM)
    dquery_low = (
        rotary(dquery * HEAD_DIM ** (-0.5), cosine, sine, -1.0).reshape(span, q_width).astype(BF16)
    )
    dkv_low = jnp.concatenate([dkey_low, dvalue_low], axis=1)
    grad_out_t = spread(after(weight_grad(dattn_low, (by_owner(attn_o),), 9), own_grads))
    grad_qkv = spread(after(weight_grad(normed_one, (dquery_low, dkv_low), 10), grad_out_t))
    tokens_grad, grad_gain_one = sum_rows(
        (dquery_low, after(dkv_low, grad_out_t)),
        w_qkv,
        before_attention,
        (tokens_own, dresid, gain_one),
        ((share, BF16), (8, F32)),
        False,
        True,
        mp_size,
        6,
    )

    gain_grads, grad_key, grad_value = last_sums(
        [
            jnp.sum(grad, axis=0)
            for grad in (grad_gain_one, grad_gain_two, grad_gain_three, grad_gain_four)
        ],
        grad_qkv[:, q_width:],
        w_key.shape[1],
        heads,
        (dp_size, seq_size, mp_size),
    )
    return (
        output[None],
        tokens_grad[None],
        gain_grads[0],
        grad_qkv[:, :q_width].astype(F32),
        grad_key,
        grad_value,
        grad_out_t.astype(F32).T,
        gain_grads[1],
        gain_grads[2],
        grad_gate_up[:, :ffw].astype(F32),
        grad_gate_up[:, ffw:].astype(F32),
        grad_down_t.astype(F32).T,
        gain_grads[3],
    )


def solution(mesh):
    weight = P(("dp", "seq"), "mp")
    whole_rows = P(("dp", "seq"), None)
    columns = P("mp", ("dp", "seq"))
    gain = P(("dp", "seq"))
    tokens = P("dp", "seq", None)
    rows = P("dp", ("seq", "mp"), None)
    in_specs = (
        tokens,
        tokens,
        gain,
        weight,
        whole_rows,
        whole_rows,
        columns,
        gain,
        gain,
        weight,
        weight,
        columns,
        gain,
    )
    out_specs = (
        rows,
        rows,
        gain,
        weight,
        whole_rows,
        whole_rows,
        columns,
        gain,
        gain,
        weight,
        weight,
        columns,
        gain,
    )
    return jax.shard_map(shards, mesh=mesh, in_specs=in_specs, out_specs=out_specs, check_vma=False)
```

time: 1410 us -> 1080 us (0.77)
  waiting for transfers between devices: 906 us -> 431 us
  Pallas kernels: 71.1 us -> 492 us
  matrix products: 284 us -> 60.6 us
  starting transfers between devices: 29.7 us -> 1.02 us
  other arithmetic: 55.1 us -> 37.5 us
    pallas_call x1 -> x10, Pallas kernels: 40.4 us -> 461 us  [the longest x4 333 us: sum_rows(): pl.pallas_call(functools.partial(rows_kernel, plan, rows_fn), out_shape=o...]
    ppermute x29 -> x0, waiting for transfers between devices: 351 us -> none  [swapped(): lax.ppermute(x, axis, [(i, i ^ k) for i in range(lax.axis_size(axis))])]
    dot_general x30 -> x0, matrix products: 199 us -> none  [the longest x20 122 us: dot_nt(): lax.dot_general(left, right, (((1,), (1,)), ((), ())), preferred_element_...]
    all_gather x5 -> x4, waiting for transfers between devices: 244 us -> 182 us  [gather_weight(): return lax.all_gather(x, both, axis=0, tiled=True)]
    reduce_scatter x5, waiting for transfers between devices: 224 us -> 170 us  [spread(): return lax.psum_scatter(x, 'seq', scatter_dimension=0, tiled=True)]
    ppermute x29 -> x0, starting transfers between devices: 28.9 us -> none  [swapped(): lax.ppermute(x, axis, [(i, i ^ k) for i in range(lax.axis_size(axis))])]
    dot_general x7 -> x6, matrix products: 84.7 us -> 60.6 us  [dot_nn(): lax.dot_general(left, right, (((1,), (0,)), ((), ())), preferred_element_...]
  transfers between devices with their start and end apart: 41 -> 10, of which waited for: 27 -> 9; matrix products, arithmetic and copies ran while one was open for 18% -> 11% of each run, Pallas kernels for 4% -> 33%
where the time goes in v2:
time: 1080 us; the launch traced here: 1070 us
  Pallas kernels  492 us (46%)
  waiting for transfers between devices  431 us (40%)
  matrix products  60.6 us (6%)
  other arithmetic  37.5 us (3%)
  local copies, waits for them, and re-layouts  31 us (3%)
  between operations  15.1 us (1%)
    pallas_call x4, Pallas kernels, sum_rows(): pl.pallas_call(functools.partial(rows_kernel, plan, rows_fn), out_shape=o...  333 us
    all_gather x4, waiting for transfers between devices, gather_weight(): return lax.all_gather(x, both, axis=0, tiled=True)  182 us
    reduce_scatter x5, waiting for transfers between devices, spread(): return lax.psum_scatter(x, 'seq', scatter_dimension=0, tiled=True)  170 us
    pallas_call x4, Pallas kernels, weight_grad(): pl.pallas_call(functools.partial(weight_grad_kernel, (len(rights), tile,...  84.5 us
    all_gather x1, waiting for transfers between devices, shards(): pairs = lax.all_gather(after(own_pair, w_out_t), 'seq', axis=0, tiled=True)  79 us
    dot_general x6, matrix products, dot_nn(): lax.dot_general(left, right, (((1,), (0,)), ((), ())), preferred_element_...  60.6 us
    pallas_call x1, Pallas kernels, last_sums(): pl.pallas_call(functools.partial(last_kernel, sizes, heads), out_shape=(j...  23.5 us
  transfers between devices with their start and end apart: 10, of which 9 were waited for; matrix products, arithmetic and copies ran while one was open for 11% of the time, Pallas kernels for 33%

profile of v2, /device:TPU:0, one launch (start us, length us, event | category | flops | bytes accessed | tf_op | source)
XLA Modules:
  0.0 1068.2 jit_solution(11620573068071005498)
XLA Ops:
  7.2 1.0 constant_dynamic-slice_fusion.4
  8.3 1.9 pad_maximum_fusion.6
  10.2 0.7 stack.35
  13.5 9.9 shard_map.228
  23.5 0.9 slice_bitcast_fusion.1
  24.6 3.5 fusion.6
  28.4 3.3 fusion.8.refs_0_
  31.8 32.9 %all-gather.6.cloned.1.call-done.refs_2_ = bf16[2304,1024]{1,0:T(8,128)(2,1)} async-done(((bf16[288,1024]{1,0:T(8,128)(2,1)}), bf16[2304,1024]{1,0:T(8,128)(2,1)}) %all-gather.6.cloned.1.call-update) | async-done | bytes 4718608 | tf_op jit(solution)/shard_map/all_gather | solution.py:775
  64.8 4.2 fusion.26
  69.0 3.1 fusion.37
  72.1 2.8 convolution_convert_fusion
  74.9 1.1 pad_maximum_fusion.1
  76.0 20.8 %all-gather.8.cloned.1.call-done.refs_1_ = bf16[2304,512]{1,0:T(8,128)(2,1)} async-done(((bf16[288,512]{1,0:T(8,128)(2,1)}), bf16[2304,512]{1,0:T(8,128)(2,1)}) %all-gather.8.cloned.1.call-update) | async-done | bytes 2359312 | tf_op jit(solution)/shard_map/all_gather | solution.py:775
  96.8 3.0 pad_maximum_fusion
  99.8 79.0 %all-gather.10.cloned.1.call-done.kv_ref = bf16[4096,512]{1,0:T(8,128)(2,1)} async-done(((bf16[1024,512]{1,0:T(8,128)(2,1)}), bf16[4096,512]{1,0:T(8,128)(2,1)}) %all-gather.10.cloned.1.call-update) | async-done | bytes 4194320 | tf_op jit(solution)/shard_map/all_gather | solution.py:804
  180.3 2.4 dynamic-slice_bitcast_fusion.1.refs_2_.refs_3_
  182.6 1.8 slice_bitcast_fusion
  184.4 2.4 copy.38
  187.1 1.3 copy.27
  188.4 6.4 fusion.19
  195.5 1.3 copy.39.q_ref
  196.8 8.0 shard_map.229
  204.9 88.7 %shard_map.230 = (f32[256,2304]{1,0:T(8,128)}, f32[256,2304]{1,0:T(8,128)}, bf16[1024,2304]{1,0:T(8,128)(2,1)}) custom-call(bf16[1024,512]{1,0:T(8,128)(2,1)} %get-tuple-element.48.refs_0_, bf16[2304,512]{1,0:T(8,128)(2,1)} %all-gather.8.cloned.1.call-done.refs_1_, bf16[256,2304]{1,0:T(8,128)(2,1)} %dynamic-slice_bitcast_fusion.1.refs_2_.refs_3_, ...), custom_call_target="tpu_custom_call" | custom-call | tf_op jit(solution)/shard_map/pallas_call | solution.py:552
  293.5 73.5 %all-gather.12.cloned.1.call-done.refs_2_ = bf16[2304,4608]{1,0:T(8,128)(2,1)} async-done(((bf16[288,4608]{1,0:T(8,128)(2,1)}), bf16[2304,4608]{1,0:T(8,128)(2,1)}) %all-gather.12.cloned.1.call-update) | async-done | bytes 21233680 | tf_op jit(solution)/shard_map/all_gather | solution.py:775
  367.5 0.7 slice.113.refs_4_
  368.2 2.5 dynamic-slice_bitcast_fusion.refs_3_.refs_5_
  370.7 17.0 %fusion.2 = f32[1024,2304]{1,0:T(8,128)} fusion(bf16[1024,2304]{1,0:T(8,128)(2,1)} %get-tuple-element.49.refs_0_, bf16[2304,4608]{1,0:T(8,128)(2,1)} %all-gather.12.cloned.1.call-done.refs_2_), kind=kOutput, calls=%fused_computation.6 | convolution fusion | flops 10871635968 | bytes 24772608 | tf_op jit(solution)/shard_map/dot_general | solution.py:30
  387.7 25.2 %fusion.17 = (bf16[1024,2304]{1,0:T(8,128)(2,1)}, bf16[1024,2304]{1,0:T(8,128)(2,1)}, bf16[1024,2304]{1,0:T(8,128)(2,1)}) fusion(f32[1024,2304]{1,0:T(8,128)} %fusion.2, bf16[1024,2304]{1,0:T(8,128)(2,1)S(1)} %bitcast.49, bf16[2304,4608]{1,0:T(8,128)(2,1)} %all-gather.12.cloned.1.call-done.refs_2_), kind=kOutput, calls=%fused_computation.21 | convolution fusion | flops 10928259072 | bytes 38928384 | tf_op jit(solution)/shard_map/dot_general | solution.py:30
  412.9 54.3 %all-gather.14.cloned.1.call-done.refs_1_.down_ref = bf16[2304,2304]{1,0:T(8,128)(2,1)} async-done(((bf16[288,2304]{1,0:T(8,128)(2,1)}), bf16[2304,2304]{1,0:T(8,128)(2,1)}) %all-gather.14.cloned.1.call-update) | async-done | bytes 10616848 | tf_op jit(solution)/shard_map/all_gather | solution.py:775
  467.2 93.1 %shard_map.231 = (bf16[256,2304]{1,0:T(8,128)(2,1)}, f32[8,2304]{1,0:T(8,128)}, bf16[1024,2304]{1,0:T(8,128)(2,1)}) custom-call(bf16[1024,2304]{1,0:T(8,128)(2,1)} %get-tuple-element.88.refs_0_.refs_1_, bf16[2304,2304]{1,0:T(8,128)(2,1)} %all-gather.14.cloned.1.call-done.refs_1_.down_ref, f32[256,2304]{1,0:T(8,128)} %get-tuple-element.52.refs_2_.refs_3_, ...), custom_call_target="tpu_custom_call" | custom-call | tf_op jit(solution)/shard_map/pallas_call | solution.py:552
  560.4 21.2 %shard_map.232 = bf16[1152,2304]{1,0:T(8,128)(2,1)} custom-call(bf16[1024,2304]{1,0:T(8,128)(2,1)} %get-tuple-element.55.refs_0_.dmixed_ref, bf16[1024,2304]{1,0:T(8,128)(2,1)} %get-tuple-element.88.refs_0_.refs_1_), custom_call_target="tpu_custom_call" | custom-call | tf_op jit(solution)/shard_map/pallas_call | solution.py:641
  581.6 19.7 %shard_map.233 = (bf16[1024,2304]{1,0:T(8,128)(2,1)}, bf16[1024,2304]{1,0:T(8,128)(2,1)}) custom-call(bf16[1024,2304]{1,0:T(8,128)(2,1)} %get-tuple-element.55.refs_0_.dmixed_ref, bf16[2304,2304]{1,0:T(8,128)(2,1)} %all-gather.14.cloned.1.call-done.refs_1_.down_ref, bf16[1024,2304]{1,0:T(8,128)(2,1)} %get-tuple-element.89.act_ref, ...), custom_call_target="tpu_custom_call" | custom-call | tf_op jit(solution)/shard_map/pallas_call | solution.py:674
  601.3 38.7 %shard_map.234 = bf16[1152,4608]{1,0:T(8,128)(2,1)} custom-call(bf16[1024,2304]{1,0:T(8,128)(2,1)} %get-tuple-element.49.refs_0_, bf16[1024,2304]{1,0:T(8,128)(2,1)} %get-tuple-element.58.refs_1_.refs_0_, bf16[1024,2304]{1,0:T(8,128)(2,1)} %get-tuple-element.57.refs_2_.refs_1_), custom_call_target="tpu_custom_call" | custom-call | tf_op jit(solution)/shard_map/pallas_call | solution.py:641
  640.0 34.1 %reduce-scatter.6.cloned.1.call-done = bf16[288,2304]{1,0:T(8,128)(2,1)} async-done(((bf16[1152,2304]{1,0:T(8,128)(2,1)}), bf16[288,2304]{1,0:T(8,128)(2,1)}) %reduce-scatter.6.cloned.1.call-update) | async-done | bytes 1327120 | tf_op jit(solution)/shard_map/reduce_scatter | solution.py:855
  674.5 101.4 %shard_map.235 = (f32[256,2304]{1,0:T(8,128)}, f32[8,2304]{1,0:T(8,128)}, f32[8,2304]{1,0:T(8,128)}, bf16[1024,2304]{1,0:T(8,128)(2,1)}) custom-call(bf16[1024,2304]{1,0:T(8,128)(2,1)} %get-tuple-element.58.refs_1_.refs_0_, bf16[1024,2304]{1,0:T(8,128)(2,1)} %get-tuple-element.57.refs_2_.refs_1_, bf16[2304,4608]{1,0:T(8,128)(2,1)} %all-gather.12.cloned.1.call-done.refs_2_, ...), custom_call_target="tpu_custom_call" | custom-call | tf_op jit(solution)/shard_map/pallas_call | solution.py:552
  775.9 4.9 fusion.59
  780.9 1.0 pad_maximum_fusion.2.do_ref
  782.0 13.0 %shard_map.236 = (f32[1024,512]{1,0:T(8,128)}, bf16[4096,512]{1,0:T(8,128)(2,1)}) custom-call(bf16[1024,512]{1,0:T(8,128)(2,1)} %copy.39.q_ref, bf16[1024,512]{1,0:T(8,128)(2,1)} %pad_maximum_fusion.2.do_ref, f32[1024,512]{1,0:T(8,128)} %get-tuple-element.61.of_ref, f32[4,1,512]{2,1,0:T(1,128)} %get-tuple-element.62.lse_ref, ...), custom_call_target="tpu_custom_call" | custom-call | flops 16106127360 | bytes 4194304 | tf_op jit(solution)/shard_map/pallas_call | solution.py:333
  795.0 62.3 %reduce-scatter.8.cloned.1.call-done = bf16[288,4608]{1,0:T(8,128)(2,1)} async-done(((bf16[1152,4608]{1,0:T(8,128)(2,1)}), bf16[288,4608]{1,0:T(8,128)(2,1)}) %reduce-scatter.8.cloned.1.call-update) | async-done | bytes 2654224 | tf_op jit(solution)/shard_map/reduce_scatter | solution.py:855
  857.5 1.0 pad_maximum_fusion.5.refs_1_
  858.5 9.4 shard_map.237
  867.9 69.5 %reduce-scatter.10.cloned.1.call-done = bf16[1024,512]{1,0:T(8,128)(2,1)} async-done(((bf16[4096,512]{1,0:T(8,128)(2,1)}), bf16[1024,512]{1,0:T(8,128)(2,1)}) %reduce-scatter.10.cloned.1.call-update) | async-done | bytes 1048592 | tf_op jit(solution)/shard_map/reduce_scatter | solution.py:855
  937.4 2.8 convert_element_type.85
  940.4 1.6 broadcast_multiply_fusion
  941.9 1.9 copy.41
  944.3 1.3 copy.40.refs_0_.refs_1_
  945.7 1.1 slice.145
  946.8 2.6 fusion.42
  949.4 1.1 pad_maximum_fusion.4.refs_1_.refs_2_
  950.4 15.1 %shard_map.239 = bf16[1152,1024]{1,0:T(8,128)(2,1)} custom-call(bf16[1024,2304]{1,0:T(8,128)(2,1)} %fusion.8.refs_0_, bf16[1024,512]{1,0:T(8,128)(2,1)} %copy.40.refs_0_.refs_1_, bf16[1024,512]{1,0:T(8,128)(2,1)} %pad_maximum_fusion.4.refs_1_.refs_2_), custom_call_target="tpu_custom_call" | custom-call | tf_op jit(solution)/shard_map/pallas_call | solution.py:641
  965.6 4.5 reduce-scatter.12.cloned.1.call-done
  970.1 0.7 slice.119.refs_5_
  971.2 3.0 convert_bitcast_fusion.1
  974.2 2.8 slice_convert_fusion
  977.0 50.0 %shard_map.238 = (bf16[256,2304]{1,0:T(8,128)(2,1)}, f32[8,2304]{1,0:T(8,128)}) custom-call(bf16[1024,512]{1,0:T(8,128)(2,1)} %copy.40.refs_0_.refs_1_, bf16[1024,512]{1,0:T(8,128)(2,1)} %pad_maximum_fusion.4.refs_1_.refs_2_, bf16[2304,1024]{1,0:T(8,128)(2,1)} %all-gather.6.cloned.1.call-done.refs_2_, ...), custom_call_target="tpu_custom_call" | custom-call | tf_op jit(solution)/shard_map/pallas_call | solution.py:552
  1027.0 1.0 reduce_sum.46
  1028.8 0.9 convert_bitcast_fusion.2
  1029.7 2.0 slice_convert_fusion.2
  1031.7 23.5 %shard_map.240 = (f32[8,384]{1,0:T(8,128)}, f32[288,1024]{1,0:T(8,128)}, f32[288,1024]{1,0:T(8,128)}) custom-call(f32[8,8,384]{2,1,0:T(8,128)} %pad.12.x_ref, bf16[288,512]{1,0:T(8,128)(2,1)} %get-tuple-element.109.kv_ref), custom_call_target="tpu_custom_call" | custom-call | tf_op jit(solution)/shard_map/pallas_call | solution.py:189
  1055.3 1.5 slice_reduce_fusion.4
  1056.8 1.0 copy.46
  1057.8 1.0 copy.47
  1058.8 1.0 copy.48
  1059.9 1.0 copy.49
  (92 shorter events, 8.4 us)
Async XLA Ops:
  7.2 57.5 %all-gather.6.cloned.1.call-start = ((), (), s32[]{:S(2)}) async-start(), calls=%async_computation.5 | async-start | bytes 5308416 | tf_op jit(solution)/shard_map/all_gather | solution.py:775
  10.1 86.6 %all-gather.8.cloned.1.call-start = ((), (), s32[]{:S(2)}) async-start(), calls=%async_computation.6 | async-start | bytes 2654208 | tf_op jit(solution)/shard_map/all_gather | solution.py:775
  24.5 7.2 copy-start.12
  24.6 3.8 copy-start
  64.7 7.4 slice-start
  64.7 114.1 %all-gather.10.cloned.1.call-start = ((), (), s32[]{:S(2)}) async-start(), calls=%async_computation.7 | async-start | bytes 5242880 | tf_op jit(solution)/shard_map/all_gather | solution.py:804
  64.8 7.3 slice-start.1
  72.1 24.7 %copy-start.6 = (bf16[288,2304]{1,0:T(8,128)(2,1)S(1)}, bf16[288,2304]{1,0:T(8,128)(2,1)}, u32[]{:S(2)}) copy-start(bf16[288,2304]{1,0:T(8,128)(2,1)} %param.23) | copy-start | bytes 3981316
  96.8 270.3 %all-gather.12.cloned.1.call-start = ((), (), s32[]{:S(2)}) async-start(), calls=%async_computation.8 | async-start | bytes 23887872 | tf_op jit(solution)/shard_map/all_gather | solution.py:775
  178.8 288.4 %all-gather.14.cloned.1.call-start = ((), (), s32[]{:S(2)}) async-start(), calls=%async_computation.9 | async-start | bytes 11943936 | tf_op jit(solution)/shard_map/all_gather | solution.py:775
  367.1 307.1 %reduce-scatter.6.cloned.1.call-start = ((), (), s32[]{:S(2)}) async-start(), calls=%async_computation.10 | async-start | bytes 6635520 | tf_op jit(solution)/shard_map/reduce_scatter | solution.py:855
  368.2 19.5 %slice-start.2 = ((s8[4718592]{0:T(1024)(128)(4,1)}), s8[4194304]{0:T(1024)(128)(4,1)S(1)}, s32[]{:S(2)}) async-start(s8[4718592]{0:T(1024)(128)(4,1)} %bitcast.48), calls=%async_computation.17 | async-start | bytes 8388608
  370.7 17.0 %slice-start.3 = ((s8[4718592]{0:T(1024)(128)(4,1)}), s8[524288]{0:T(1024)(128)(4,1)S(1)}, s32[]{:S(2)}) async-start(s8[4718592]{0:T(1024)(128)(4,1)} %bitcast.48), calls=%async_computation.18 | async-start | bytes 1048576
  581.6 275.7 %reduce-scatter.8.cloned.1.call-start = ((), (), s32[]{:S(2)}) async-start(), calls=%async_computation.11 | async-start | bytes 13271040 | tf_op jit(solution)/shard_map/reduce_scatter | solution.py:855
  674.2 263.3 %reduce-scatter.10.cloned.1.call-start = ((), (), s32[]{:S(2)}) async-start(), calls=%async_computation.12 | async-start | bytes 5242880 | tf_op jit(solution)/shard_map/reduce_scatter | solution.py:855
  674.5 101.4 %copy-start.4 = (bf16[2304,512]{1,0:T(8,128)(2,1)S(1)}, bf16[2304,512]{1,0:T(8,128)(2,1)}, u32[]{:S(2)}) copy-start(bf16[2304,512]{1,0:T(8,128)(2,1)} %all-gather.8.cloned.1.call-done.refs_1_) | copy-start | bytes 7077892
  795.0 62.4 %copy-start.2 = (bf16[1024,512]{1,0:T(8,128)(2,1)S(1)}, bf16[1024,512]{1,0:T(8,128)(2,1)}, u32[]{:S(2)}) copy-start(bf16[1024,512]{1,0:T(8,128)(2,1)} %get-tuple-element.48.refs_0_) | copy-start | bytes 3145732
  857.3 112.8 %reduce-scatter.12.cloned.1.call-start = ((), (), s32[]{:S(2)}) async-start(), calls=%async_computation.13 | async-start | bytes 1474560 | tf_op jit(solution)/shard_map/reduce_scatter | solution.py:855
  858.5 81.9 %copy-start.5 = (f32[1024,512]{1,0:T(8,128)S(1)}, f32[1024,512]{1,0:T(8,128)}, u32[]{:S(2)}) copy-start(f32[1024,512]{1,0:T(8,128)} %get-tuple-element.63) | copy-start | bytes 6291460
  940.3 89.4 %reduce-scatter.14.cloned.1.call-start = ((), (), s32[]{:S(2)}) async-start(), calls=%async_computation.14 | async-start | bytes 2949120 | tf_op jit(solution)/shard_map/reduce_scatter | solution.py:855
  944.2 2.5 copy-start.1
  950.4 19.7 %copy-start.13 = (f32[8,288]{1,0:T(8,128)S(1)}, f32[8,288]{1,0:T(8,128)}, u32[]{:S(2)}) copy-start(f32[8,288]{1,0:T(8,128)} %copy-done.12) | copy-start | bytes 27652
  950.4 20.4 %copy-start.14 = (f32[8,2304]{1,0:T(8,128)S(1)}, f32[8,2304]{1,0:T(8,128)}, u32[]{:S(2)}) copy-start(f32[8,2304]{1,0:T(8,128)} %get-tuple-element.74) | copy-start | bytes 221188
  950.4 20.5 %copy-start.16 = (f32[8,2304]{1,0:T(8,128)S(1)}, f32[8,2304]{1,0:T(8,128)}, u32[]{:S(2)}) copy-start(f32[8,2304]{1,0:T(8,128)} %get-tuple-element.72) | copy-start | bytes 221188
  950.4 20.6 %copy-start.15 = (f32[8,2304]{1,0:T(8,128)S(1)}, f32[8,2304]{1,0:T(8,128)}, u32[]{:S(2)}) copy-start(f32[8,2304]{1,0:T(8,128)} %get-tuple-element.73) | copy-start | bytes 221188
  965.6 8.6 copy-start.3
  977.0 51.9 %copy-start.11 = (bf16[288,512]{1,0:T(8,128)(2,1)S(1)}, bf16[288,512]{1,0:T(8,128)(2,1)}, u32[]{:S(2)}) copy-start(bf16[288,512]{1,0:T(8,128)(2,1)} %reduce-scatter.12.cloned.1.call-done) | copy-start | bytes 884740
  977.0 79.8 %copy-start.7 = (bf16[256,2304]{1,0:T(8,128)(2,1)S(1)}, bf16[256,2304]{1,0:T(8,128)(2,1)}, u32[]{:S(2)}) copy-start(bf16[256,2304]{1,0:T(8,128)(2,1)} %get-tuple-element.53) | copy-start | bytes 3538948
  1027.0 30.8 %copy-start.8 = (bf16[256,2304]{1,0:T(8,128)(2,1)S(1)}, bf16[256,2304]{1,0:T(8,128)(2,1)}, u32[]{:S(2)}) copy-start(bf16[256,2304]{1,0:T(8,128)(2,1)} %get-tuple-element.70) | copy-start | bytes 3538948
  1055.3 3.6 copy-start.10
  1055.3 4.6 copy-start.9
Sparse Core Ops, SparseCore 0:
  10.3 54.3 all-gather.5
  66.3 30.4 all-gather.7
  98.9 79.8 all-gather.9
  180.8 186.1 all-gather.11
  368.5 98.6 all-gather.13
  581.7 92.4 reduce-scatter.5
  676.6 180.6 reduce-scatter.7
  859.6 77.8 reduce-scatter.9
  940.4 29.6 reduce-scatter.11
  972.4 46.7 reduce-scatter.13

commit v3 on v2

--- a/solution.py
+++ b/solution.py
@@ -15,6 +15,8 @@
 EPSILON = 1e-06
 SOFT_CAP = 50.0
 ROPE_BASE = 10000.0
+GELU_SCALE = (2.0 / 3.141592653589793) ** 0.5
+GELU_CUBE = 0.044715
 MESH = pl.DeviceIdType.MESH
 VMEM_LIMIT = 56 * 1024 * 1024
 LANES = 128
@@ -456,7 +458,7 @@
     outs, refs = refs[:n_out], refs[n_out:]
     if gather:
         gathered, refs = refs[0], refs[1:]
-    left, weight, kept, sent, arrived, total, own, in_sem, sum_sem, row_sem = refs
+    left, weight, total, own, kept, sent, arrived, in_sem, sum_sem, row_sem = refs
     steps = total.shape[1] // step
     dp, seq, mp = lax.axis_index("dp"), lax.axis_index("seq"), lax.axis_index("mp")
 
@@ -504,6 +506,22 @@
                 copy.wait()
         return dot_nt(left[k], weight[t % 2])
 
+    finish_rows(
+        parts_at,
+        (mp_size, share, step, row_step),
+        (rows_fn, aux, outs, gathered if gather else None),
+        peer,
+        (total, own, kept, sent, arrived),
+        (sum_sem, row_sem, in_sem.at[0]),
+    )
+
+
+def finish_rows(parts_at, sizes, rows, peer, buffers, sems):
+    mp_size, share, step, row_step = sizes
+    rows_fn, aux, outs, gathered = rows
+    total, own, kept, sent, arrived = buffers
+    sum_sem, row_sem, keep_sem = sems
+    steps = total.shape[1] // step
     if mp_size == 4:
         sums = sum_square(parts_at, steps, step, peer, total, kept, sent, arrived, sum_sem)
     else:
@@ -512,7 +530,7 @@
     def rows_at(r, carry):
         rows = pl.ds(pl.multiple_of(r * row_step, row_step), row_step)
         result = rows_fn(total[rows, :], rows, aux, outs)
-        if gather:
+        if gathered is not None:
             own[rows, :] = result.astype(BF16)
         return carry
 
@@ -520,8 +538,8 @@
         if ref.shape[0] == 8:
             ref[...] = jnp.zeros_like(ref)
     lax.fori_loop(0, share // row_step, rows_at, 0)
-    if gather:
-        keep = pltpu.make_async_copy(own, gathered.at[pl.ds(0, share)], in_sem.at[0])
+    if gathered is not None:
+        keep = pltpu.make_async_copy(own, gathered.at[pl.ds(0, share)], keep_sem)
         keep.start()
         if mp_size == 4:
             gather_square(own, gathered, share, peer, row_sem)
@@ -532,23 +550,38 @@
         copy.wait_send()
 
 
+def row_plan(width, share, mp_size):
+    step = 768 if width % 768 == 0 else width
+    steps = width // step
+    if mp_size == 4:
+        pieces, kept = (steps, 2, 3, share, step // 2), (steps, 2, share, step // 2)
+    else:
+        pieces, kept = (steps, mp_size - 1, share, step), (8, LANES)
+    buffers = [
+        pltpu.VMEM((share, width), F32),
+        pltpu.VMEM((share, width), BF16),
+        pltpu.VMEM(kept, F32),
+        pltpu.VMEM(pieces, BF16),
+        pltpu.VMEM(pieces, BF16),
+    ]
+    sems = [
+        pltpu.SemaphoreType.DMA((2, steps, max(4, mp_size - 1))),
+        pltpu.SemaphoreType.DMA((2, max(6, mp_size))),
+    ]
+    return step, min(32, share), buffers, sems
+
+
 def sum_rows(lefts, weight, rows_fn, aux, outs, gather, natural, mp_size, collective_id):
     span = lefts[0].shape[0]
     width, depth = weight.shape
     share = span // mp_size
-    step = 768 if width % 768 == 0 else width
-    row_step = min(32, share)
-    steps = width // step
+    step, row_step, buffers, sems = row_plan(width, share, mp_size)
     plan = (mp_size, share, step, row_step, natural, len(lefts), len(aux), len(outs), gather)
     out_shape = [jax.ShapeDtypeStruct((rows, width), dtype) for rows, dtype in outs]
     out_specs = [pl.BlockSpec(memory_space=pltpu.VMEM)] * len(outs)
     if gather:
         out_shape.append(jax.ShapeDtypeStruct((span, width), BF16))
         out_specs.append(pl.BlockSpec(memory_space=pl.ANY))
-    if mp_size == 4:
-        pieces, kept = (steps, 2, 3, share, step // 2), (steps, 2, share, step // 2)
-    else:
-        pieces, kept = (steps, mp_size - 1, share, step), (8, LANES)
     return pl.pallas_call(
         functools.partial(rows_kernel, plan, rows_fn),
         out_shape=out_shape,
@@ -558,14 +591,9 @@
         scratch_shapes=[
             pltpu.VMEM((mp_size, share, depth), BF16),
             pltpu.VMEM((2, step, depth), BF16),
-            pltpu.VMEM(kept, F32),
-            pltpu.VMEM(pieces, BF16),
-            pltpu.VMEM(pieces, BF16),
-            pltpu.VMEM((share, width), F32),
-            pltpu.VMEM((share, width), BF16),
+            *buffers,
             pltpu.SemaphoreType.DMA((2 + mp_size * len(lefts),)),
-            pltpu.SemaphoreType.DMA((2, steps, max(4, mp_size - 1))),
-            pltpu.SemaphoreType.DMA((2, max(6, mp_size))),
+            *sems,
         ],
         compiler_params=pltpu.CompilerParams(
             collective_id=collective_id, has_side_effects=True, vmem_limit_bytes=VMEM_LIMIT
@@ -574,16 +602,25 @@
 
 
 def weight_grad_kernel(plan, *refs):
-    n_right, tile, half = plan
+    n_right, tile, half, steps, seq_size = plan
     left_ref, rights, out_ref = refs[0], refs[1 : 1 + n_right], refs[1 + n_right]
     left, right, sent, arrived, own, result, in_sem, swap_sem, out_sem = refs[2 + n_right :]
     dp, seq, mp = lax.axis_index("dp"), lax.axis_index("seq"), lax.axis_index("mp")
     other = (1 - dp, seq, mp)
     lefts = []
+    part = half // steps
     for i, side in enumerate((1 - dp, dp)):
-        columns = pl.ds(pl.multiple_of(side * half, LANES), half)
-        lefts.append(pltpu.make_async_copy(left_ref.at[:, columns], left.at[i], in_sem.at[2 + i]))
-        lefts[i].start()
+        for n in range(steps):
+            columns = pl.ds(pl.multiple_of((2 * n + side) * part, LANES), part)
+            lefts.append(
+                pltpu.make_async_copy(
+                    left_ref.at[:, columns],
+                    left.at[i, :, pl.ds(n * part, part)],
+                    in_sem.at[2 + i * steps + n],
+                )
+            )
+    for load in lefts:
+        load.start()
     sources = []
     for ref in rights:
         for first in range(0, ref.shape[1], tile):
@@ -599,39 +636,54 @@
     pl.semaphore_wait(barrier, 1)
     swaps, stores = [], []
 
+    def store(t):
+        piece = part // seq_size
+        copies = []
+        for n in range(steps):
+            for z in range(seq_size):
+                copies.append(
+                    pltpu.make_async_copy(
+                        result.at[t % 2, pl.ds(n * part + z * piece, piece)],
+                        out_ref.at[pl.ds((z * steps + n) * piece, piece), pl.ds(t * tile, tile)],
+                        out_sem.at[t % 2, n * seq_size + z],
+                    )
+                )
+        return copies
+
     def finish(t):
         swaps[t].wait_recv()
         if t >= 2:
-            stores[t - 2].wait()
+            for copy in stores[t - 2]:
+                copy.wait()
         result[t % 2] = (own[t % 2] + arrived[t].astype(F32)).astype(BF16)
-        stores.append(
-            pltpu.make_async_copy(
-                result.at[t % 2], out_ref.at[:, pl.ds(t * tile, tile)], out_sem.at[t % 2]
-            )
-        )
-        stores[t].start()
+        stores.append(store(t))
+        for copy in stores[t]:
+            copy.start()
 
     for t in range(tiles):
         loads[t].wait()
         if t + 1 < tiles:
             loads[t + 1].start()
         if t == 0:
-            lefts[0].wait()
+            for load in lefts[:steps]:
+                load.wait()
         sent[t] = dot_tn(left[0], right[t % 2]).astype(BF16)
         swaps.append(remote_copy(sent.at[t], arrived.at[t], swap_sem, (t,), other))
         if t == 0:
-            lefts[1].wait()
+            for load in lefts[steps:]:
+                load.wait()
         own[t % 2] = dot_tn(left[1], right[t % 2])
         if t >= 1:
             finish(t - 1)
     finish(tiles - 1)
-    for store in stores[-2:]:
-        store.wait()
+    for copies in stores[-2:]:
+        for copy in copies:
+            copy.wait()
     for swap in swaps:
         swap.wait_send()
 
 
-def weight_grad(left, rights, collective_id):
+def weight_grad(left, rights, collective_id, steps=1, seq_size=1):
     rows, width = left.shape
     half = width // 2
     total = sum(right.shape[1] for right in rights)
@@ -639,7 +691,7 @@
     tile = next(t for t in (tile, 256, LANES) if all(right.shape[1] % t == 0 for right in rights))
     tiles = total // tile
     return pl.pallas_call(
-        functools.partial(weight_grad_kernel, (len(rights), tile, half)),
+        functools.partial(weight_grad_kernel, (len(rights), tile, half, steps, seq_size)),
         out_shape=jax.ShapeDtypeStruct((half, total), BF16),
         in_specs=[pl.BlockSpec(memory_space=pl.ANY)] * (1 + len(rights)),
         out_specs=pl.BlockSpec(memory_space=pl.ANY),
@@ -650,14 +702,270 @@
             pltpu.VMEM((tiles, half, tile), BF16),
             pltpu.VMEM((2, half, tile), F32),
             pltpu.VMEM((2, half, tile), BF16),
-            pltpu.SemaphoreType.DMA((4,)),
+            pltpu.SemaphoreType.DMA((2 + 2 * steps,)),
             pltpu.SemaphoreType.DMA((2, tiles)),
-            pltpu.SemaphoreType.DMA((2,)),
+            pltpu.SemaphoreType.DMA((2, steps * seq_size)),
         ],
         compiler_params=pltpu.CompilerParams(
             collective_id=collective_id, has_side_effects=True, vmem_limit_bytes=VMEM_LIMIT
         ),
     )(left, *rights)
+
+
+def ffw_kernel(plan, normed_ref, gate_up_ref, shard_ref, resid_ref, cotangent_ref, gain_ref, *refs):
+    mp_size, seq_size, share, step, row_step, tile = plan
+    output_ref, gain_grad_ref, dmixed_ref, hidden_ref, act_ref, slope_ref, down_ref = refs[:7]
+    normed, gate_up, hidden, down, staged, *refs = refs[7:]
+    buffers, refs = refs[:5], refs[5:]
+    load_sem, store_sem, local_sem, line_sem, pair_sem, sum_sem, row_sem = refs
+    steps, _, units = down.shape
+    piece = step // (2 * seq_size)
+    far = seq_size - 1
+    dp, seq, mp = lax.axis_index("dp"), lax.axis_index("seq"), lax.axis_index("mp")
+    sibling = (1 - dp, seq, mp)
+
+    def peer(k):
+        return (dp, seq, flipped(mp, k))
+
+    def along(way):
+        return (dp, seq + 1 - 2 * way, mp)
+
+    def goes_on(way):
+        return seq < far if way == 0 else seq > 0
+
+    def comes(way, distance):
+        return seq >= distance if way == 0 else seq + distance <= far
+
+    def block(t, at):
+        first = pl.multiple_of((dp * seq_size + at) * piece, piece)
+        return down.at[t, pl.ds(first, piece)]
+
+    def line(t, way, distance):
+        at = seq - distance if way == 0 else seq + distance
+        return pltpu.make_async_remote_copy(
+            src_ref=block(t, at),
+            dst_ref=block(t, at),
+            send_sem=line_sem.at[0, t, way, distance],
+            recv_sem=line_sem.at[1, t, way, distance],
+            device_id=along(way),
+            device_id_type=MESH,
+        )
+
+    def pair(t, way, distance):
+        at = seq - distance if way == 0 else seq + distance
+        return pltpu.make_async_remote_copy(
+            src_ref=block(t, at),
+            dst_ref=block(t, at),
+            send_sem=pair_sem.at[0, t, way, distance],
+            recv_sem=pair_sem.at[1, t, way, distance],
+            device_id=sibling,
+            device_id_type=MESH,
+        )
+
+    normed_load = pltpu.make_async_copy(normed_ref, normed, local_sem.at[0])
+    normed_load.start()
+    shard_loads = [
+        pltpu.make_async_copy(
+            shard_ref.at[pl.ds(t * piece, piece)], block(t, seq), local_sem.at[1 + t]
+        )
+        for t in range(steps)
+    ]
+    for load in shard_loads:
+        load.start()
+
+    def loads(i, slot):
+        return [
+            pltpu.make_async_copy(
+                gate_up_ref.at[:, pl.ds(pl.multiple_of(side * units + i * tile, LANES), tile)],
+                gate_up.at[slot, side],
+                load_sem.at[slot, side],
+            )
+            for side in range(2)
+        ]
+
+    def stores(i, slot):
+        columns = pl.ds(pl.multiple_of(i * tile, LANES), tile)
+        return [
+            pltpu.make_async_copy(staged.at[slot, 0], act_ref.at[:, columns], store_sem.at[slot, 0]),
+            pltpu.make_async_copy(staged.at[slot, 1], slope_ref.at[:, columns], store_sem.at[slot, 1]),
+        ]
+
+    for load in loads(0, 0):
+        load.start()
+    barrier = pltpu.get_barrier_semaphore()
+    for k in range(1, mp_size):
+        pl.semaphore_signal(barrier, inc=1, device_id=peer(k), device_id_type=MESH)
+    pl.semaphore_signal(barrier, inc=1, device_id=sibling, device_id_type=MESH)
+    for way in range(2):
+        @pl.when(goes_on(way))
+        def _(way=way):
+            pl.semaphore_signal(barrier, inc=1, device_id=along(way), device_id_type=MESH)
+
+    line_peers = (seq + far) // seq_size + (2 * far - seq) // seq_size
+    pl.semaphore_wait(barrier, mp_size + line_peers)
+
+    for t in range(steps):
+        shard_loads[t].wait()
+        for way in range(2):
+            @pl.when(goes_on(way))
+            def _(t=t, way=way):
+                line(t, way, 0).start()
+    for t in range(steps):
+        pair(t, 0, 0).start()
+    normed_load.wait()
+
+    def arrival(t, distance):
+        for way in range(2):
+            @pl.when(comes(way, distance))
+            def _(way=way):
+                line(t, way, distance - 1).wait_recv()
+                if distance < far:
+                    @pl.when(goes_on(way))
+                    def _():
+                        line(t, way, distance).start()
+
+                pair(t, way, distance).start()
+
+    arrivals = [(t, distance) for distance in range(1, seq_size) for t in range(steps)]
+    tiles = units // tile
+    early = [(2 * n + 2, event) for n, event in enumerate(arrivals) if 2 * n + 2 < tiles]
+    late = arrivals[len(early) :]
+
+    def units_at(i, carry):
+        slot = lax.rem(i, 2)
+        for load in loads(i, slot):
+            load.wait()
+
+        @pl.when(i + 1 < tiles)
+        def _():
+            for load in loads(i + 1, 1 - slot):
+                load.start()
+
+        @pl.when(i >= 2)
+        def _():
+            for store in stores(i - 2, slot):
+                store.wait()
+
+        gate = dot_nn(normed[...], gate_up[slot, 0])
+        up = dot_nn(normed[...], gate_up[slot, 1])
+        squared = gate * gate
+        bend = jnp.tanh(GELU_SCALE * gate * (1.0 + GELU_CUBE * squared))
+        side = 0.5 * (1.0 + bend)
+        act = gate * side
+        slope = side + (0.5 * GELU_SCALE) * gate * (1.0 - bend * bend) * (1.0 + 3.0 * GELU_CUBE * squared)
+        staged[slot, 0] = act.astype(BF16)
+        staged[slot, 1] = (slope * up).astype(BF16)
+        for store in stores(i, slot):
+            store.start()
+        product = (act * up).astype(BF16)
+        for k in range(mp_size):
+            hidden[k, :, pl.ds(pl.multiple_of(i * tile, LANES), tile)] = product[
+                k * share : (k + 1) * share
+            ]
+        for at, event in early:
+            @pl.when(i == at)
+            def _(event=event):
+                arrival(*event)
+
+        return carry
+
+    lax.fori_loop(0, tiles, units_at, 0)
+    for i in range(max(0, tiles - 2), tiles):
+        for store in stores(i, i % 2):
+            store.wait()
+    hidden_stores = [
+        pltpu.make_async_copy(hidden.at[k], hidden_ref.at[pl.ds(k * share, share)], local_sem.at[1 + k])
+        for k in range(mp_size)
+    ]
+    for store in hidden_stores:
+        store.start()
+    down_stores = [
+        pltpu.make_async_copy(
+            down.at[t], down_ref.at[pl.ds(t * step, step)], local_sem.at[1 + mp_size + t]
+        )
+        for t in range(steps)
+    ]
+    waiting = list(late)
+
+    def parts_at(t, k):
+        if k == mp_size - 1:
+            while (t, far) in waiting:
+                arrival(*waiting.pop(0))
+            pair(t, 0, 0).wait_recv()
+            for way in range(2):
+                for distance in range(1, seq_size):
+                    @pl.when(comes(way, distance))
+                    def _(way=way, distance=distance):
+                        pair(t, way, distance).wait_recv()
+
+            down_stores[t].start()
+        return dot_nt(hidden[k], down[t])
+
+    finish_rows(
+        parts_at,
+        (mp_size, share, step, row_step),
+        (after_ffw, (resid_ref, cotangent_ref, gain_ref), (output_ref, gain_grad_ref), dmixed_ref),
+        peer,
+        buffers,
+        (sum_sem, row_sem, local_sem.at[0]),
+    )
+    for store in hidden_stores + down_stores:
+        store.wait()
+    for t in range(steps):
+        pair(t, 0, 0).wait_send()
+        for way in range(2):
+            for distance in range(seq_size - 1):
+                @pl.when(goes_on(way) & comes(way, distance))
+                def _(t=t, way=way, distance=distance):
+                    line(t, way, distance).wait_send()
+
+            for distance in range(1, seq_size):
+                @pl.when(comes(way, distance))
+                def _(t=t, way=way, distance=distance):
+                    pair(t, way, distance).wait_send()
+
+
+def ffw(normed, gate_up_w, down_shard, resid, cotangent, gain, sizes, collective_id):
+    dp_size, seq_size, mp_size = sizes
+    span, width = normed.shape
+    units = gate_up_w.shape[1] // 2
+    share = span // mp_size
+    step, row_step, buffers, sems = row_plan(width, share, mp_size)
+    steps = width // step
+    tile = 256 if units % 256 == 0 else LANES
+    plan = (mp_size, seq_size, share, step, row_step, tile)
+    per_unit = jax.ShapeDtypeStruct((span, units), BF16)
+    return pl.pallas_call(
+        functools.partial(ffw_kernel, plan),
+        out_shape=(
+            jax.ShapeDtypeStruct((share, width), BF16),
+            jax.ShapeDtypeStruct((8, width), F32),
+            jax.ShapeDtypeStruct((span, width), BF16),
+            per_unit,
+            per_unit,
+            per_unit,
+            jax.ShapeDtypeStruct((width, units), BF16),
+        ),
+        in_specs=[pl.BlockSpec(memory_space=pl.ANY)] * 3 + [pl.BlockSpec(memory_space=pltpu.VMEM)] * 3,
+        out_specs=(pl.BlockSpec(memory_space=pltpu.VMEM),) * 2 + (pl.BlockSpec(memory_space=pl.ANY),) * 5,
+        scratch_shapes=[
+            pltpu.VMEM((span, width), BF16),
+            pltpu.VMEM((2, 2, width, tile), BF16),
+            pltpu.VMEM((mp_size, share, units), BF16),
+            pltpu.VMEM((steps, step, units), BF16),
+            pltpu.VMEM((2, 2, span, tile), BF16),
+            *buffers,
+            pltpu.SemaphoreType.DMA((2, 2)),
+            pltpu.SemaphoreType.DMA((2, 2)),
+            pltpu.SemaphoreType.DMA((1 + mp_size + steps,)),
+            pltpu.SemaphoreType.DMA((2, steps, 2, seq_size)),
+            pltpu.SemaphoreType.DMA((2, steps, 2, seq_size)),
+            *sems,
+        ],
+        compiler_params=pltpu.CompilerParams(
+            collective_id=collective_id, has_side_effects=True, vmem_limit_bytes=VMEM_LIMIT
+        ),
+    )(normed, gate_up_w, down_shard, resid, cotangent, gain)
 
 
 def hidden_back_kernel(dmixed_ref, down_ref, act_ref, slope_ref, dgate_ref, dup_ref):
@@ -806,9 +1114,8 @@
     queries = (rotary(query_lin, cosine, sine, 1.0) * HEAD_DIM ** (-0.5)).astype(BF16)
     queries = queries.reshape(span, q_width)
 
-    ffw = w_gate.shape[1]
+    units = w_gate.shape[1]
     gate_up_w = gather_weight(after(jnp.concatenate([w_gate, w_up], axis=1), pairs))
-    gate_w, up_w = gate_up_w[:, :ffw], gate_up_w[:, ffw:]
 
     attn_o, attn_exact, lse = attend(queries, pairs, plan)
     own_first = mp * share
@@ -831,30 +1138,33 @@
         mp_size,
         3,
     )
-    down_wt = gather_weight(after(w_down.T, gate_up_w, normed_two))
-
-    gate_lin = dot_nn(normed_two, gate_w)
-    up_lin = dot_nn(normed_two, up_w)
-    gate_act, gelu_pull = jax.vjp(lambda gate_in: jax.nn.gelu(gate_in, approximate=True), gate_lin)
-    hidden = (gate_act * up_lin).astype(BF16)
-    slope = gelu_pull(up_lin)[0].astype(BF16)
-    gate_act = gate_act.astype(BF16)
-    output, grad_gain_four, dmixed_low = sum_rows(
-        (hidden,),
-        down_wt,
-        after_ffw,
-        (resid, cotangent_own, gain_four),
-        ((share, BF16), (8, F32)),
-        True,
-        False,
-        mp_size,
+    sizes = (dp_size, seq_size, mp_size)
+    shard_count = dp_size * seq_size
+    steps = width // row_plan(width, share, mp_size)[0]
+
+    def to_steps(x):
+        return jnp.swapaxes(x.reshape(x.shape[0], shard_count, steps, -1), 1, 2).reshape(x.shape)
+
+    def to_shards(x):
+        return jnp.swapaxes(x.reshape(x.shape[0], steps, shard_count, -1), 1, 2).reshape(x.shape)
+
+    output, grad_gain_four, dmixed_low, hidden, gate_act, slope, down_wt = ffw(
+        normed_two,
+        gate_up_w,
+        w_down.T,
+        to_steps(resid),
+        to_steps(cotangent_own),
+        to_steps(gain_four),
+        sizes,
         4,
     )
+    output = to_shards(output)
+    grad_gain_four = to_shards(grad_gain_four)
 
     def spread(x):
         return lax.psum_scatter(x, "seq", scatter_dimension=0, tiled=True)
 
-    grad_down_sum = weight_grad(dmixed_low, (hidden,), 7)
+    grad_down_sum = weight_grad(dmixed_low, (hidden,), 7, steps, seq_size)
     grad_down_t = spread(grad_down_sum)
     dgate_low, dup_low = hidden_back(after(dmixed_low, grad_down_sum), down_wt, gate_act, slope)
     grad_gate_up_sum = weight_grad(normed_two, (dgate_low, dup_low), 8)
@@ -873,7 +1183,8 @@
 
     dattn_o = by_owner(dot_nn(dattn_low, w_out_t)).astype(BF16)
     dquery, dpairs = attend_back(queries, dattn_o, attn_exact, lse, pairs, plan)
-    own_grads = spread(after(dpairs, grad_gate_up)).astype(F32)
+    grad_out_sum = weight_grad(dattn_low, (by_owner(attn_o),), 9)
+    own_grads = spread(after(dpairs, grad_gate_up, grad_out_sum)).astype(F32)
     dkey_rot = own_grads[:, :HEAD_DIM]
     dkey_low = rotary(dkey_rot, cosine[:, 0], sine[:, 0], -1.0).astype(BF16)
     dvalue_low = own_grads[:, HEAD_DIM:].astype(BF16)
@@ -882,10 +1193,10 @@
         rotary(dquery * HEAD_DIM ** (-0.5), cosine, sine, -1.0).reshape(span, q_width).astype(BF16)
     )
     dkv_low = jnp.concatenate([dkey_low, dvalue_low], axis=1)
-    grad_out_t = spread(after(weight_grad(dattn_low, (by_owner(attn_o),), 9), own_grads))
-    grad_qkv = spread(after(weight_grad(normed_one, (dquery_low, dkv_low), 10), grad_out_t))
+    grad_qkv_sum = weight_grad(normed_one, (dquery_low, dkv_low), 10)
+    grad_qkv = spread(grad_qkv_sum)
     tokens_grad, grad_gain_one = sum_rows(
-        (dquery_low, after(dkv_low, grad_out_t)),
+        (dquery_low, after(dkv_low, grad_qkv_sum)),
         w_qkv,
         before_attention,
         (tokens_own, dresid, gain_one),
@@ -896,6 +1207,7 @@
         6,
     )
 
+    grad_out_t = spread(after(grad_out_sum, grad_qkv, tokens_grad))
     gain_grads, grad_key, grad_value = last_sums(
         [
             jnp.sum(grad, axis=0)
@@ -904,7 +1216,7 @@
         grad_qkv[:, q_width:],
         w_key.shape[1],
         heads,
-        (dp_size, seq_size, mp_size),
+        sizes,
     )
     return (
         output[None],
@@ -916,8 +1228,8 @@
         grad_out_t.astype(F32).T,
         gain_grads[1],
         gain_grads[2],
-        grad_gate_up[:, :ffw].astype(F32),
-        grad_gate_up[:, ffw:].astype(F32),
+        grad_gate_up[:, :units].astype(F32),
+        grad_gate_up[:, units:].astype(F32),
         grad_down_t.astype(F32).T,
         gain_grads[3],
     )

time: 1080 us -> 1040 us (0.963)
  Pallas kernels: 492 us -> 566 us
  waiting for transfers between devices: 431 us -> 359 us
  matrix products: 60.6 us -> 18 us
    pallas_call x0 -> x1, Pallas kernels: none -> 164 us  [ffw(): pl.pallas_call(functools.partial(ffw_kernel, plan), out_shape=(jax.ShapeD...]
    pallas_call x4 -> x3, Pallas kernels: 333 us -> 241 us  [sum_rows(): pl.pallas_call(functools.partial(rows_kernel, plan, rows_fn), out_shape=o...]
    all_gather x4 -> x3, waiting for transfers between devices: 182 us -> 119 us  [gather_weight(): return lax.all_gather(x, both, axis=0, tiled=True)]
    dot_general x6 -> x4, matrix products: 60.6 us -> 18 us  [dot_nn(): lax.dot_general(left, right, (((1,), (0,)), ((), ())), preferred_element_...]
    reduce_scatter x5, waiting for transfers between devices: 170 us -> 159 us  [spread(): return lax.psum_scatter(x, 'seq', scatter_dimension=0, tiled=True)]
  transfers between devices with their start and end apart: 10 -> 9, of which waited for: 9 -> 7; matrix products, arithmetic and copies ran while one was open for 11% -> 7% of each run, Pallas kernels for 33% -> 35%
where the time goes in v3:
time: 1040 us; the launch traced here: 1030 us
  Pallas kernels  566 us (54%)
  waiting for transfers between devices  359 us (35%)
  local copies, waits for them, and re-layouts  38.3 us (4%)
  other arithmetic  33.7 us (3%)
  matrix products  18 us (2%)
  between operations  14.9 us (1%)
    pallas_call x3, Pallas kernels, sum_rows(): pl.pallas_call(functools.partial(rows_kernel, plan, rows_fn), out_shape=o...  241 us
    pallas_call x1, Pallas kernels, ffw(): pl.pallas_call(functools.partial(ffw_kernel, plan), out_shape=(jax.ShapeD...  164 us
    reduce_scatter x5, waiting for transfers between devices, spread(): return lax.psum_scatter(x, 'seq', scatter_dimension=0, tiled=True)  159 us
    all_gather x3, waiting for transfers between devices, gather_weight(): return lax.all_gather(x, both, axis=0, tiled=True)  119 us
    pallas_call x4, Pallas kernels, weight_grad(): pl.pallas_call(functools.partial(weight_grad_kernel, (len(rights), tile,...  85.1 us
    all_gather x1, waiting for transfers between devices, shards(): pairs = lax.all_gather(after(own_pair, w_out_t), 'seq', axis=0, tiled=True)  80.3 us
    pallas_call x1, Pallas kernels, last_sums(): pl.pallas_call(functools.partial(last_kernel, sizes, heads), out_shape=(j...  25.2 us
  transfers between devices with their start and end apart: 9, of which 7 were waited for; matrix products, arithmetic and copies ran while one was open for 7% of the time, Pallas kernels for 35%

profile of v3, /device:TPU:0, one launch (start us, length us, event | category | flops | bytes accessed | tf_op | source)
XLA Modules:
  0.0 1030.9 jit_solution(398653752184888071)
XLA Ops:
  7.3 1.0 constant_dynamic-slice_fusion.5
  8.3 1.9 pad_maximum_fusion.6
  10.9 10.0 shard_map.228
  20.9 0.9 slice_bitcast_fusion.1
  22.0 3.5 fusion.2
  25.8 3.3 fusion.4.refs_0_
  29.1 35.7 %all-gather.5.cloned.1.call-done.refs_2_ = bf16[2304,1024]{1,0:T(8,128)(2,1)} async-done(((bf16[288,1024]{1,0:T(8,128)(2,1)}), bf16[2304,1024]{1,0:T(8,128)(2,1)}) %all-gather.5.cloned.1.call-update) | async-done | bytes 4718608 | tf_op jit(solution)/shard_map/all_gather | solution.py:1083
  64.9 4.2 fusion.14
  69.1 3.1 fusion.25
  72.2 2.7 convolution_convert_fusion
  74.9 1.1 pad_maximum_fusion.1
  75.9 20.9 %all-gather.7.cloned.1.call-done.refs_1_ = bf16[2304,512]{1,0:T(8,128)(2,1)} async-done(((bf16[288,512]{1,0:T(8,128)(2,1)}), bf16[2304,512]{1,0:T(8,128)(2,1)}) %all-gather.7.cloned.1.call-update) | async-done | bytes 2359312 | tf_op jit(solution)/shard_map/all_gather | solution.py:1083
  96.9 1.7 pad_maximum_fusion
  98.6 80.3 %all-gather.9.cloned.1.call-done.kv_ref = bf16[4096,512]{1,0:T(8,128)(2,1)} async-done(((bf16[1024,512]{1,0:T(8,128)(2,1)}), bf16[4096,512]{1,0:T(8,128)(2,1)}) %all-gather.9.cloned.1.call-update) | async-done | bytes 4194320 | tf_op jit(solution)/shard_map/all_gather | solution.py:1112
  178.9 0.7 slice.101.refs_4_.refs_7_
  179.6 0.7 slice.99.refs_3_.refs_6_
  180.3 1.3 constant_dynamic-slice_fusion.4
  182.4 1.5 copy.52.cotangent_ref
  184.0 0.7 reshape.189.gain_ref
  184.7 2.5 dynamic-slice_bitcast_fusion.refs_2_.refs_3_
  187.6 2.2 slice_bitcast_fusion
  189.8 2.4 copy.64
  192.2 6.1 fusion.8
  199.0 1.3 copy.65.q_ref
  200.3 8.1 shard_map.229
  208.4 88.9 %shard_map.230 = (f32[256,2304]{1,0:T(8,128)}, f32[256,2304]{1,0:T(8,128)}, bf16[1024,2304]{1,0:T(8,128)(2,1)}) custom-call(bf16[1024,512]{1,0:T(8,128)(2,1)} %get-tuple-element.50.refs_0_, bf16[2304,512]{1,0:T(8,128)(2,1)} %all-gather.7.cloned.1.call-done.refs_1_, bf16[256,2304]{1,0:T(8,128)(2,1)} %dynamic-slice_bitcast_fusion.refs_2_.refs_3_, ...), custom_call_target="tpu_custom_call" | custom-call | tf_op jit(solution)/shard_map/pallas_call | solution.py:585
  297.4 3.1 copy.46
  300.4 1.9 copy.47
  302.3 2.0 copy.51.resid_ref
  304.3 62.8 %all-gather.11.cloned.1.call-done.gate_up_ref.refs_2_ = bf16[2304,4608]{1,0:T(8,128)(2,1)} async-done(((bf16[288,4608]{1,0:T(8,128)(2,1)}), bf16[2304,4608]{1,0:T(8,128)(2,1)}) %all-gather.11.cloned.1.call-update) | async-done | bytes 21233680 | tf_op jit(solution)/shard_map/all_gather | solution.py:1083
  367.1 163.5 %shard_map.231 = (bf16[256,2304]{1,0:T(8,128)(2,1)}, f32[8,2304]{1,0:T(8,128)}, bf16[1024,2304]{1,0:T(8,128)(2,1)}, bf16[1024,2304]{1,0:T(8,128)(2,1)}, bf16[102...) custom-call(bf16[1024,2304]{1,0:T(8,128)(2,1)} %get-tuple-element.51.normed_ref.refs_0_, ...), custom_call_target="tpu_custom_call" | custom-call | tf_op jit(solution)/shard_map/pallas_call | solution.py:938
  530.6 21.6 %shard_map.232 = bf16[1152,2304]{1,0:T(8,128)(2,1)} custom-call(bf16[1024,2304]{1,0:T(8,128)(2,1)} %get-tuple-element.57.refs_0_.dmixed_ref, bf16[1024,2304]{1,0:T(8,128)(2,1)} %get-tuple-element.56.refs_1_), custom_call_target="tpu_custom_call" | custom-call | tf_op jit(solution)/shard_map/pallas_call | solution.py:693
  552.3 20.3 %shard_map.233 = (bf16[1024,2304]{1,0:T(8,128)(2,1)}, bf16[1024,2304]{1,0:T(8,128)(2,1)}) custom-call(bf16[1024,2304]{1,0:T(8,128)(2,1)} %get-tuple-element.57.refs_0_.dmixed_ref, bf16[2304,2304]{1,0:T(8,128)(2,1)} %get-tuple-element.58.down_ref, bf16[1024,2304]{1,0:T(8,128)(2,1)} %get-tuple-element.59.act_ref, bf16[1024,2304]{1,0:T(8,128)(2,1)} %get-tuple-element.60.slope_ref), custom_call_target="tpu_custom_call" | custom-call | tf_op jit(solution)/shard_map/pallas_call | solution.py:982
  572.5 39.0 %shard_map.234 = bf16[1152,4608]{1,0:T(8,128)(2,1)} custom-call(bf16[1024,2304]{1,0:T(8,128)(2,1)} %get-tuple-element.51.normed_ref.refs_0_, bf16[1024,2304]{1,0:T(8,128)(2,1)} %get-tuple-element.63.refs_1_.refs_0_, bf16[1024,2304]{1,0:T(8,128)(2,1)} %get-tuple-element.62.refs_2_.refs_1_), custom_call_target="tpu_custom_call" | custom-call | tf_op jit(solution)/shard_map/pallas_call | solution.py:693
  611.5 35.8 %reduce-scatter.6.cloned.1.call-done = bf16[288,2304]{1,0:T(8,128)(2,1)} async-done(((bf16[1152,2304]{1,0:T(8,128)(2,1)}), bf16[288,2304]{1,0:T(8,128)(2,1)}) %reduce-scatter.6.cloned.1.call-update) | async-done | bytes 1327120 | tf_op jit(solution)/shard_map/reduce_scatter | solution.py:1165
  647.6 2.4 fusion.53.refs_5_
  650.1 1.0 pad_maximum_fusion.4.refs_1_
  651.1 101.7 %shard_map.235 = (f32[256,2304]{1,0:T(8,128)}, f32[8,2304]{1,0:T(8,128)}, f32[8,2304]{1,0:T(8,128)}, bf16[1024,2304]{1,0:T(8,128)(2,1)}) custom-call(bf16[1024,2304]{1,0:T(8,128)(2,1)} %get-tuple-element.63.refs_1_.refs_0_, bf16[1024,2304]{1,0:T(8,128)(2,1)} %get-tuple-element.62.refs_2_.refs_1_, ...), custom_call_target="tpu_custom_call" | custom-call | tf_op jit(solution)/shard_map/pallas_call | solution.py:585
  752.8 9.4 shard_map.237
  762.3 4.9 fusion.47
  767.3 1.0 pad_maximum_fusion.2.do_ref
  768.4 13.0 %shard_map.236 = (f32[1024,512]{1,0:T(8,128)}, bf16[4096,512]{1,0:T(8,128)(2,1)}) custom-call(bf16[1024,512]{1,0:T(8,128)(2,1)} %copy.65.q_ref, bf16[1024,512]{1,0:T(8,128)(2,1)} %pad_maximum_fusion.2.do_ref, f32[1024,512]{1,0:T(8,128)} %get-tuple-element.66.of_ref, f32[4,1,512]{2,1,0:T(1,128)} %get-tuple-element.67.lse_ref, ...), custom_call_target="tpu_custom_call" | custom-call | flops 16106127360 | bytes 4194304 | tf_op jit(solution)/shard_map/pallas_call | solution.py:335
  781.4 48.9 %reduce-scatter.8.cloned.1.call-done = bf16[288,4608]{1,0:T(8,128)(2,1)} async-done(((bf16[1152,4608]{1,0:T(8,128)(2,1)}), bf16[288,4608]{1,0:T(8,128)(2,1)}) %reduce-scatter.8.cloned.1.call-update) | async-done | bytes 2654224 | tf_op jit(solution)/shard_map/reduce_scatter | solution.py:1165
  830.4 1.6 broadcast_multiply_fusion
  831.9 1.9 copy.67
  834.3 1.3 copy.66.refs_1_.refs_0_
  835.6 74.8 %reduce-scatter.10.cloned.1.call-done = bf16[1024,512]{1,0:T(8,128)(2,1)} async-done(((bf16[4096,512]{1,0:T(8,128)(2,1)}), bf16[1024,512]{1,0:T(8,128)(2,1)}) %reduce-scatter.10.cloned.1.call-update) | async-done | bytes 1048592 | tf_op jit(solution)/shard_map/reduce_scatter | solution.py:1165
  910.4 1.6 convert_element_type.73
  912.0 2.4 fusion.30
  914.4 1.1 pad_maximum_fusion.5.refs_2_.refs_1_
  915.5 15.1 %shard_map.238 = bf16[1152,1024]{1,0:T(8,128)(2,1)} custom-call(bf16[1024,2304]{1,0:T(8,128)(2,1)} %fusion.4.refs_0_, bf16[1024,512]{1,0:T(8,128)(2,1)} %copy.66.refs_1_.refs_0_, bf16[1024,512]{1,0:T(8,128)(2,1)} %pad_maximum_fusion.5.refs_2_.refs_1_), custom_call_target="tpu_custom_call" | custom-call | tf_op jit(solution)/shard_map/pallas_call | solution.py:693
  930.9 0.7 slice.108.refs_5_
  931.6 50.3 %shard_map.239 = (bf16[256,2304]{1,0:T(8,128)(2,1)}, f32[8,2304]{1,0:T(8,128)}) custom-call(bf16[1024,512]{1,0:T(8,128)(2,1)} %copy.66.refs_1_.refs_0_, bf16[1024,512]{1,0:T(8,128)(2,1)} %pad_maximum_fusion.5.refs_2_.refs_1_, bf16[2304,1024]{1,0:T(8,128)(2,1)} %all-gather.5.cloned.1.call-done.refs_2_, ...), custom_call_target="tpu_custom_call" | custom-call | tf_op jit(solution)/shard_map/pallas_call | solution.py:585
  982.9 1.5 copy.61
  984.7 3.1 convert_bitcast_fusion.1
  987.8 2.8 slice_convert_fusion
  990.7 0.7 pad.12.x_ref
  991.4 1.0 slice_convert_fusion.2
  992.4 25.2 %shard_map.240 = (f32[8,384]{1,0:T(8,128)}, f32[288,1024]{1,0:T(8,128)}, f32[288,1024]{1,0:T(8,128)}) custom-call(f32[8,8,384]{2,1,0:T(8,128)} %pad.12.x_ref, bf16[288,512]{1,0:T(8,128)(2,1)} %get-tuple-element.123.kv_ref), custom_call_target="tpu_custom_call" | custom-call | tf_op jit(solution)/shard_map/pallas_call | solution.py:191
  1017.6 1.5 slice_reduce_fusion.4
  1019.1 1.8 convert_bitcast_fusion.2
  1020.9 1.0 copy.72
  1022.0 1.0 copy.73
  1023.0 1.0 copy.74
  (104 shorter events, 5.9 us)
Async XLA Ops:
  7.2 3.1 copy-start.17
  7.2 3.1 copy-start.18
  7.2 3.1 copy-start.19
  7.2 3.1 copy-start.20
  7.2 57.5 %all-gather.5.cloned.1.call-start = ((), (), s32[]{:S(2)}) async-start(), calls=%async_computation.5 | async-start | bytes 5308416 | tf_op jit(solution)/shard_map/all_gather | solution.py:1083
  10.2 86.6 %all-gather.7.cloned.1.call-start = ((), (), s32[]{:S(2)}) async-start(), calls=%async_computation.6 | async-start | bytes 2654208 | tf_op jit(solution)/shard_map/all_gather | solution.py:1083
  22.0 3.8 copy-start
  64.7 7.4 slice-start
  64.8 114.1 %all-gather.9.cloned.1.call-start = ((), (), s32[]{:S(2)}) async-start(), calls=%async_computation.7 | async-start | bytes 5242880 | tf_op jit(solution)/shard_map/all_gather | solution.py:1112
  64.8 7.3 slice-start.1
  74.8 22.0 %copy-start.6 = (bf16[288,2304]{1,0:T(8,128)(2,1)S(1)}, bf16[288,2304]{1,0:T(8,128)(2,1)}, u32[]{:S(2)}) copy-start(bf16[288,2304]{1,0:T(8,128)(2,1)} %param.23) | copy-start | bytes 3981316
  74.8 22.0 %copy-start.7 = (bf16[288,2304]{1,0:T(8,128)(2,1)S(1)}, bf16[288,2304]{1,0:T(8,128)(2,1)}, u32[]{:S(2)}) copy-start(bf16[288,2304]{1,0:T(8,128)(2,1)} %param.22) | copy-start | bytes 3981316
  96.8 270.3 %all-gather.11.cloned.1.call-start = ((), (), s32[]{:S(2)}) async-start(), calls=%async_computation.8 | async-start | bytes 23887872 | tf_op jit(solution)/shard_map/all_gather | solution.py:1083
  178.9 468.4 %reduce-scatter.6.cloned.1.call-start = ((), (), s32[]{:S(2)}) async-start(), calls=%async_computation.9 | async-start | bytes 6635520 | tf_op jit(solution)/shard_map/reduce_scatter | solution.py:1165
  182.4 5.0 copy-start.5
  552.2 278.1 %reduce-scatter.8.cloned.1.call-start = ((), (), s32[]{:S(2)}) async-start(), calls=%async_computation.10 | async-start | bytes 13271040 | tf_op jit(solution)/shard_map/reduce_scatter | solution.py:1165
  647.3 2.7 copy-start.1
  647.3 263.1 %reduce-scatter.10.cloned.1.call-start = ((), (), s32[]{:S(2)}) async-start(), calls=%async_computation.11 | async-start | bytes 5242880 | tf_op jit(solution)/shard_map/reduce_scatter | solution.py:1165
  752.8 9.5 copy-start.3
  781.4 49.0 %copy-start.4 = (f32[1024,512]{1,0:T(8,128)S(1)}, f32[1024,512]{1,0:T(8,128)}, u32[]{:S(2)}) copy-start(f32[1024,512]{1,0:T(8,128)} %get-tuple-element.68) | copy-start | bytes 6291460
  830.3 151.6 %reduce-scatter.12.cloned.1.call-start = ((), (), s32[]{:S(2)}) async-start(), calls=%async_computation.12 | async-start | bytes 2949120 | tf_op jit(solution)/shard_map/reduce_scatter | solution.py:1165
  910.4 4.0 slice-start.2
  930.6 88.5 %reduce-scatter.14.cloned.1.call-start = ((), (), s32[]{:S(2)}) async-start(), calls=%async_computation.13 | async-start | bytes 1474560 | tf_op jit(solution)/shard_map/reduce_scatter | solution.py:1165
  931.5 50.4 %copy-start.13 = (f32[8,2304]{1,0:T(8,128)S(1)}, f32[8,2304]{1,0:T(8,128)}, u32[]{:S(2)}) copy-start(f32[8,2304]{1,0:T(8,128)} %get-tuple-element.78) | copy-start | bytes 221188
  931.5 50.6 %copy-start.8 = (bf16[256,2304]{1,0:T(8,128)(2,1)S(1)}, bf16[256,2304]{1,0:T(8,128)(2,1)}, u32[]{:S(2)}) copy-start(bf16[256,2304]{1,0:T(8,128)(2,1)} %get-tuple-element.54) | copy-start | bytes 3538948
  982.8 1.6 copy-start.15
  982.8 1.8 copy-start.14
  984.4 3.4 copy-start.2
  987.8 2.8 copy-start.16
  987.8 3.6 copy-start.12
  990.6 30.4 %copy-start.9 = (bf16[256,2304]{1,0:T(8,128)(2,1)S(1)}, bf16[256,2304]{1,0:T(8,128)(2,1)}, u32[]{:S(2)}) copy-start(bf16[256,2304]{1,0:T(8,128)(2,1)} %get-tuple-element.74) | copy-start | bytes 3538948
  1017.6 4.3 copy-start.11
  1020.9 2.0 copy-start.10
Sparse Core Ops, SparseCore 0:
  10.3 54.3 all-gather.4
  66.3 30.4 all-gather.6
  98.9 79.8 all-gather.8
  180.9 186.1 all-gather.10
  552.3 94.8 reduce-scatter.5
  649.6 180.6 reduce-scatter.7
  832.6 77.7 reduce-scatter.9
  930.7 48.6 reduce-scatter.11
  982.0 30.3 reduce-scatter.13

commit v4 on v3

--- a/solution.py
+++ b/solution.py
@@ -383,6 +383,15 @@
 def sum_square(parts_at, steps, step, peer, total, kept, sent, arrived, sems):
     half = step // 2
     copies, second = [], []
+
+    def second_hop(t):
+        copies[2 * t].wait_recv()
+        sent[t, 1, 2] = (kept[t, 1] + arrived[t, 0, 1].astype(F32)).astype(BF16)
+        second.append(remote_copy(sent.at[t, 1, 2], arrived.at[t, 1, 2], sems, (t, 2), peer(2)))
+        copies[2 * t + 1].wait_recv()
+        sent[t, 0, 2] = (kept[t, 0] + arrived[t, 1, 1].astype(F32)).astype(BF16)
+        second.append(remote_copy(sent.at[t, 0, 2], arrived.at[t, 0, 2], sems, (t, 3), peer(1)))
+
     for t in range(steps):
         first = t * step
         far = parts_at(t, 3)
@@ -402,12 +411,7 @@
         )
         total[:, first : first + step] = parts_at(t, 0)
     for t in range(steps):
-        copies[2 * t].wait_recv()
-        sent[t, 1, 2] = (kept[t, 1] + arrived[t, 0, 1].astype(F32)).astype(BF16)
-        second.append(remote_copy(sent.at[t, 1, 2], arrived.at[t, 1, 2], sems, (t, 2), peer(2)))
-        copies[2 * t + 1].wait_recv()
-        sent[t, 0, 2] = (kept[t, 0] + arrived[t, 1, 1].astype(F32)).astype(BF16)
-        second.append(remote_copy(sent.at[t, 0, 2], arrived.at[t, 0, 2], sems, (t, 3), peer(1)))
+        second_hop(t)
     for t in range(steps):
         first = t * step
         second[2 * t].wait_recv()
@@ -419,16 +423,20 @@
     return copies + second
 
 
-def gather_direct(own, gathered, share, mp_size, peer, sems):
-    copies = [
-        remote_copy(own, gathered.at[pl.ds(k * share, share)], sems, (k,), peer(k))
-        for k in range(mp_size - 1, 0, -1)
-    ]
-    for copy in copies:
-        copy.wait()
-
-
-def gather_square(own, gathered, share, peer, sems):
+def row_gather(own, gathered, mp_size, peer, sems):
+    share = own.shape[0]
+    if mp_size != 4:
+        copies = [
+            remote_copy(own, gathered.at[pl.ds(k * share, share)], sems, (k,), peer(k))
+            for k in range(mp_size - 1, 0, -1)
+        ]
+
+        def finish():
+            for copy in copies:
+                copy.wait()
+
+        return lambda: None, finish
+
     half = share // 2
 
     def place(k, lower):
@@ -441,14 +449,20 @@
         remote_copy(upper, place(2, 0), sems, (2,), peer(2)),
         remote_copy(lower, place(1, 1), sems, (3,), peer(1)),
     ]
-    to_one.wait_recv()
-    copies.append(remote_copy(place(1, 0), place(3, 0), sems, (4,), peer(2)))
-    to_two.wait_recv()
-    copies.append(remote_copy(place(2, 1), place(3, 1), sems, (5,), peer(1)))
-    to_one.wait_send()
-    to_two.wait_send()
-    for copy in copies:
-        copy.wait()
+
+    def pass_on():
+        to_one.wait_recv()
+        copies.append(remote_copy(place(1, 0), place(3, 0), sems, (4,), peer(2)))
+        to_two.wait_recv()
+        copies.append(remote_copy(place(2, 1), place(3, 1), sems, (5,), peer(1)))
+
+    def finish():
+        to_one.wait_send()
+        to_two.wait_send()
+        for copy in copies:
+            copy.wait()
+
+    return pass_on, finish
 
 
 def rows_kernel(plan, rows_fn, *refs):
@@ -531,7 +545,12 @@
         rows = pl.ds(pl.multiple_of(r * row_step, row_step), row_step)
         result = rows_fn(total[rows, :], rows, aux, outs)
         if gathered is not None:
-            own[rows, :] = result.astype(BF16)
+            result = result.astype(BF16)
+            if len(own.shape) == 2:
+                own[rows, :] = result
+            else:
+                for t in range(steps):
+                    own[t, rows, :] = result[:, t * step : (t + 1) * step]
         return carry
 
     for ref in outs:
@@ -539,12 +558,12 @@
             ref[...] = jnp.zeros_like(ref)
     lax.fori_loop(0, share // row_step, rows_at, 0)
     if gathered is not None:
-        keep = pltpu.make_async_copy(own, gathered.at[pl.ds(0, share)], keep_sem)
+        first = own if len(own.shape) == 2 else own.at[0]
+        keep = pltpu.make_async_copy(first, gathered.at[pl.ds(0, share)], keep_sem)
         keep.start()
-        if mp_size == 4:
-            gather_square(own, gathered, share, peer, row_sem)
-        else:
-            gather_direct(own, gathered, share, mp_size, peer, row_sem)
+        pass_on, finish = row_gather(first, gathered, mp_size, peer, row_sem)
+        pass_on()
+        finish()
         keep.wait()
     for copy in sums:
         copy.wait_send()
@@ -602,25 +621,28 @@
 
 
 def weight_grad_kernel(plan, *refs):
-    n_right, tile, half, steps, seq_size = plan
-    left_ref, rights, out_ref = refs[0], refs[1 : 1 + n_right], refs[1 + n_right]
-    left, right, sent, arrived, own, result, in_sem, swap_sem, out_sem = refs[2 + n_right :]
+    n_right, tile, half, first_column, n_into, next_step, mp_size = plan
+    left_ref, rights, refs = refs[0], refs[1 : 1 + n_right], refs[1 + n_right + n_into :]
+    if next_step:
+        steps_ref, out_ref, gathered, refs = refs[0], refs[1], refs[2], refs[3:]
+        own_rows, row_sem, refs = refs[0], refs[1], refs[2:]
+    else:
+        out_ref, refs = refs[0], refs[1:]
+    left, right, sent, arrived, own, result, in_sem, swap_sem, out_sem = refs
     dp, seq, mp = lax.axis_index("dp"), lax.axis_index("seq"), lax.axis_index("mp")
     other = (1 - dp, seq, mp)
+
+    def peer(k):
+        return (dp, seq, flipped(mp, k))
+
+    if next_step:
+        rows_load = pltpu.make_async_copy(steps_ref.at[next_step], own_rows, in_sem.at[4])
+        rows_load.start()
     lefts = []
-    part = half // steps
     for i, side in enumerate((1 - dp, dp)):
-        for n in range(steps):
-            columns = pl.ds(pl.multiple_of((2 * n + side) * part, LANES), part)
-            lefts.append(
-                pltpu.make_async_copy(
-                    left_ref.at[:, columns],
-                    left.at[i, :, pl.ds(n * part, part)],
-                    in_sem.at[2 + i * steps + n],
-                )
-            )
-    for load in lefts:
-        load.start()
+        columns = pl.ds(pl.multiple_of(side * half, LANES), half)
+        lefts.append(pltpu.make_async_copy(left_ref.at[:, columns], left.at[i], in_sem.at[2 + i]))
+        lefts[i].start()
     sources = []
     for ref in rights:
         for first in range(0, ref.shape[1], tile):
@@ -633,89 +655,108 @@
     loads[0].start()
     barrier = pltpu.get_barrier_semaphore()
     pl.semaphore_signal(barrier, inc=1, device_id=other, device_id_type=MESH)
-    pl.semaphore_wait(barrier, 1)
+    if next_step:
+        for k in range(1, mp_size):
+            pl.semaphore_signal(barrier, inc=1, device_id=peer(k), device_id_type=MESH)
+    pl.semaphore_wait(barrier, mp_size if next_step else 1)
+    if next_step:
+        rows_load.wait()
+        share = own_rows.shape[0]
+        keep = pltpu.make_async_copy(own_rows, gathered.at[pl.ds(0, share)], in_sem.at[4])
+        keep.start()
+        pass_on, end_rows = row_gather(own_rows, gathered, mp_size, peer, row_sem)
     swaps, stores = [], []
-
-    def store(t):
-        piece = part // seq_size
-        copies = []
-        for n in range(steps):
-            for z in range(seq_size):
-                copies.append(
-                    pltpu.make_async_copy(
-                        result.at[t % 2, pl.ds(n * part + z * piece, piece)],
-                        out_ref.at[pl.ds((z * steps + n) * piece, piece), pl.ds(t * tile, tile)],
-                        out_sem.at[t % 2, n * seq_size + z],
-                    )
-                )
-        return copies
 
     def finish(t):
         swaps[t].wait_recv()
         if t >= 2:
-            for copy in stores[t - 2]:
-                copy.wait()
+            stores[t - 2].wait()
         result[t % 2] = (own[t % 2] + arrived[t].astype(F32)).astype(BF16)
-        stores.append(store(t))
-        for copy in stores[t]:
-            copy.start()
+        stores.append(
+            pltpu.make_async_copy(
+                result.at[t % 2],
+                out_ref.at[:, pl.ds(first_column + t * tile, tile)],
+                out_sem.at[t % 2],
+            )
+        )
+        stores[t].start()
 
     for t in range(tiles):
         loads[t].wait()
         if t + 1 < tiles:
             loads[t + 1].start()
         if t == 0:
-            for load in lefts[:steps]:
-                load.wait()
+            lefts[0].wait()
         sent[t] = dot_tn(left[0], right[t % 2]).astype(BF16)
         swaps.append(remote_copy(sent.at[t], arrived.at[t], swap_sem, (t,), other))
         if t == 0:
-            for load in lefts[steps:]:
-                load.wait()
+            lefts[1].wait()
         own[t % 2] = dot_tn(left[1], right[t % 2])
         if t >= 1:
             finish(t - 1)
+        if t == tiles // 2 and next_step:
+            pass_on()
     finish(tiles - 1)
-    for copies in stores[-2:]:
-        for copy in copies:
-            copy.wait()
+    for store in stores[-2:]:
+        store.wait()
     for swap in swaps:
         swap.wait_send()
-
-
-def weight_grad(left, rights, collective_id, steps=1, seq_size=1):
+    if next_step:
+        keep.wait()
+        end_rows()
+
+
+def weight_grad(left, rights, collective_id, into=None, columns=0, steps=None, next_step=0, mp_size=1):
     rows, width = left.shape
     half = width // 2
     total = sum(right.shape[1] for right in rights)
-    tile = min(768 if rights[0].shape[1] % 768 == 0 else 384, rights[0].shape[1])
-    tile = next(t for t in (tile, 256, LANES) if all(right.shape[1] % t == 0 for right in rights))
+    tile = next(
+        t
+        for t in (768, 512, 384, 256, LANES)
+        if total >= 2 * t and all(right.shape[1] % t == 0 for right in rights)
+    )
     tiles = total // tile
-    return pl.pallas_call(
-        functools.partial(weight_grad_kernel, (len(rights), tile, half, steps, seq_size)),
-        out_shape=jax.ShapeDtypeStruct((half, total), BF16),
-        in_specs=[pl.BlockSpec(memory_space=pl.ANY)] * (1 + len(rights)),
-        out_specs=pl.BlockSpec(memory_space=pl.ANY),
+    first = 0 if into is None else into.shape[1] - total
+    earlier = () if into is None else (into,)
+    out_shape = [jax.ShapeDtypeStruct((half, first + total + columns), BF16)]
+    scratch = []
+    if next_step:
+        earlier = (steps,)
+        out_shape.append(jax.ShapeDtypeStruct((steps.shape[1] * mp_size, steps.shape[2]), BF16))
+        scratch = [
+            pltpu.VMEM(steps.shape[1:], BF16),
+            pltpu.SemaphoreType.DMA((2, max(6, mp_size))),
+        ]
+    plan = (len(rights), tile, half, first, 0 if into is None else 1, next_step, mp_size)
+    results = pl.pallas_call(
+        functools.partial(weight_grad_kernel, plan),
+        out_shape=out_shape,
+        in_specs=[pl.BlockSpec(memory_space=pl.ANY)] * (1 + len(rights) + len(earlier)),
+        out_specs=[pl.BlockSpec(memory_space=pl.ANY)] * len(out_shape),
+        input_output_aliases={} if into is None else {1 + len(rights): 0},
         scratch_shapes=[
+            *scratch,
             pltpu.VMEM((2, rows, half), BF16),
             pltpu.VMEM((2, rows, tile), BF16),
             pltpu.VMEM((tiles, half, tile), BF16),
             pltpu.VMEM((tiles, half, tile), BF16),
             pltpu.VMEM((2, half, tile), F32),
             pltpu.VMEM((2, half, tile), BF16),
-            pltpu.SemaphoreType.DMA((2 + 2 * steps,)),
+            pltpu.SemaphoreType.DMA((5,)),
             pltpu.SemaphoreType.DMA((2, tiles)),
-            pltpu.SemaphoreType.DMA((2, steps * seq_size)),
+            pltpu.SemaphoreType.DMA((2,)),
         ],
         compiler_params=pltpu.CompilerParams(
             collective_id=collective_id, has_side_effects=True, vmem_limit_bytes=VMEM_LIMIT
         ),
-    )(left, *rights)
+    )(left, *rights, *earlier)
+    return results if next_step else results[0]
 
 
 def ffw_kernel(plan, normed_ref, gate_up_ref, shard_ref, resid_ref, cotangent_ref, gain_ref, *refs):
     mp_size, seq_size, share, step, row_step, tile = plan
-    output_ref, gain_grad_ref, dmixed_ref, hidden_ref, act_ref, slope_ref, down_ref = refs[:7]
-    normed, gate_up, hidden, down, staged, *refs = refs[7:]
+    output_ref, gain_grad_ref, own_ref, dmixed_ref, hidden_ref, act_ref, slope_ref, down_ref = refs[:8]
+    normed, gate_up, hidden, down, staged, *refs = refs[8:]
     buffers, refs = refs[:5], refs[5:]
     load_sem, store_sem, local_sem, line_sem, pair_sem, sum_sem, row_sem = refs
     steps, _, units = down.shape
@@ -909,8 +950,11 @@
         buffers,
         (sum_sem, row_sem, local_sem.at[0]),
     )
+    own_store = pltpu.make_async_copy(buffers[1], own_ref, local_sem.at[0])
+    own_store.start()
     for store in hidden_stores + down_stores:
         store.wait()
+    own_store.wait()
     for t in range(steps):
         pair(t, 0, 0).wait_send()
         for way in range(2):
@@ -932,6 +976,7 @@
     share = span // mp_size
     step, row_step, buffers, sems = row_plan(width, share, mp_size)
     steps = width // step
+    buffers[1] = pltpu.VMEM((steps, share, step), BF16)
     tile = 256 if units % 256 == 0 else LANES
     plan = (mp_size, seq_size, share, step, row_step, tile)
     per_unit = jax.ShapeDtypeStruct((span, units), BF16)
@@ -940,14 +985,15 @@
         out_shape=(
             jax.ShapeDtypeStruct((share, width), BF16),
             jax.ShapeDtypeStruct((8, width), F32),
-            jax.ShapeDtypeStruct((span, width), BF16),
+            jax.ShapeDtypeStruct((steps, share, step), BF16),
+            jax.ShapeDtypeStruct((span, step), BF16),
             per_unit,
             per_unit,
             per_unit,
             jax.ShapeDtypeStruct((width, units), BF16),
         ),
         in_specs=[pl.BlockSpec(memory_space=pl.ANY)] * 3 + [pl.BlockSpec(memory_space=pltpu.VMEM)] * 3,
-        out_specs=(pl.BlockSpec(memory_space=pltpu.VMEM),) * 2 + (pl.BlockSpec(memory_space=pl.ANY),) * 5,
+        out_specs=(pl.BlockSpec(memory_space=pltpu.VMEM),) * 2 + (pl.BlockSpec(memory_space=pl.ANY),) * 6,
         scratch_shapes=[
             pltpu.VMEM((span, width), BF16),
             pltpu.VMEM((2, 2, width, tile), BF16),
@@ -968,30 +1014,31 @@
     )(normed, gate_up_w, down_shard, resid, cotangent, gain)
 
 
-def hidden_back_kernel(dmixed_ref, down_ref, act_ref, slope_ref, dgate_ref, dup_ref):
-    dhidden = dot_nn(dmixed_ref[...], down_ref[...])
+def hidden_back_kernel(n_parts, *refs):
+    parts, (down_ref, act_ref, slope_ref, dgate_ref, dup_ref) = refs[:n_parts], refs[n_parts:]
+    first, dhidden = 0, 0.0
+    for part in parts:
+        depth = part.shape[1]
+        dhidden = dhidden + dot_nn(part[...], down_ref[first : first + depth, :])
+        first += depth
     dgate_ref[...] = (dhidden * slope_ref[...].astype(F32)).astype(BF16)
     dup_ref[...] = (dhidden * act_ref[...].astype(F32)).astype(BF16)
 
 
 def hidden_back(dmixed, down_wt, act, slope):
-    rows, width = dmixed.shape
-    units = down_wt.shape[1]
+    rows, depth = dmixed[0].shape
+    width, units = down_wt.shape
     tile = 256 if units % 256 == 0 else units
     columns = pl.BlockSpec((rows, tile), lambda i: (0, i))
     return pl.pallas_call(
-        hidden_back_kernel,
+        functools.partial(hidden_back_kernel, len(dmixed)),
         grid=(units // tile,),
         out_shape=(jax.ShapeDtypeStruct((rows, units), BF16),) * 2,
-        in_specs=[
-            pl.BlockSpec((rows, width), lambda i: (0, 0)),
-            pl.BlockSpec((width, tile), lambda i: (0, i)),
-            columns,
-            columns,
-        ],
+        in_specs=[pl.BlockSpec((rows, depth), lambda i: (0, 0))] * len(dmixed)
+        + [pl.BlockSpec((width, tile), lambda i: (0, i)), columns, columns],
         out_specs=(columns, columns),
         compiler_params=pltpu.CompilerParams(vmem_limit_bytes=VMEM_LIMIT),
-    )(dmixed, down_wt, act, slope)
+    )(*dmixed, down_wt, act, slope)
 
 
 def fold_rows(x):
@@ -1148,7 +1195,7 @@
     def to_shards(x):
         return jnp.swapaxes(x.reshape(x.shape[0], steps, shard_count, -1), 1, 2).reshape(x.shape)
 
-    output, grad_gain_four, dmixed_low, hidden, gate_act, slope, down_wt = ffw(
+    output, grad_gain_four, dmixed_own, dmixed_first, hidden, gate_act, slope, down_wt = ffw(
         normed_two,
         gate_up_w,
         w_down.T,
@@ -1164,12 +1211,37 @@
     def spread(x):
         return lax.psum_scatter(x, "seq", scatter_dimension=0, tiled=True)
 
-    grad_down_sum = weight_grad(dmixed_low, (hidden,), 7, steps, seq_size)
-    grad_down_t = spread(grad_down_sum)
-    dgate_low, dup_low = hidden_back(after(dmixed_low, grad_down_sum), down_wt, gate_act, slope)
+    dmixed_low, grad_sums = [dmixed_first], []
+    for t in range(steps):
+        into = grad_sums[-1] if t > 1 else None
+        columns = units * (steps - 2) if t == 1 else 0
+        if t + 1 < steps:
+            grad_sum, arrived = weight_grad(
+                dmixed_low[t],
+                (hidden,),
+                20 + t,
+                into=into,
+                columns=columns,
+                steps=dmixed_own,
+                next_step=t + 1,
+                mp_size=mp_size,
+            )
+            dmixed_low.append(arrived)
+        else:
+            grad_sum = weight_grad(dmixed_low[t], (hidden,), 20 + t, into=into, columns=columns)
+        grad_sums.append(grad_sum)
+    grad_down_first = spread(grad_sums[0])
+    grad_down_rest = spread(after(grad_sums[-1], grad_down_first))
+    grad_down = [grad_down_first] + [
+        grad_down_rest[:, t * units : (t + 1) * units] for t in range(steps - 1)
+    ]
+    grad_down = jnp.concatenate(grad_down, axis=0).astype(F32).T
+    dgate_low, dup_low = hidden_back(
+        (after(dmixed_low[0], grad_sum), *dmixed_low[1:]), down_wt, gate_act, slope
+    )
     grad_gate_up_sum = weight_grad(normed_two, (dgate_low, dup_low), 8)
     dresid, grad_gain_two, grad_gain_three, dattn_low = sum_rows(
-        (after(dgate_low, grad_down_t, grad_gate_up_sum), dup_low),
+        (after(dgate_low, grad_down_rest, grad_gate_up_sum), dup_low),
         gate_up_w,
         before_ffw,
         (resid, attn, cotangent_own, gain_two, gain_three),
@@ -1179,21 +1251,25 @@
         mp_size,
         5,
     )
-    grad_gate_up = spread(after(grad_gate_up_sum, grad_down_t))
+    grad_gate_up = spread(after(grad_gate_up_sum, grad_down_rest))
 
     dattn_o = by_owner(dot_nn(dattn_low, w_out_t)).astype(BF16)
     dquery, dpairs = attend_back(queries, dattn_o, attn_exact, lse, pairs, plan)
     grad_out_sum = weight_grad(dattn_low, (by_owner(attn_o),), 9)
-    own_grads = spread(after(dpairs, grad_gate_up, grad_out_sum)).astype(F32)
+    dquery = dquery.reshape(span, heads, HEAD_DIM)
+    dquery_low = (
+        rotary(dquery * HEAD_DIM ** (-0.5), cosine, sine, -1.0).reshape(span, q_width).astype(BF16)
+    )
+    grad_q_sum = weight_grad(normed_one, (dquery_low,), 10, columns=2 * HEAD_DIM)
+    own_grads = spread(after(dpairs, grad_gate_up, grad_out_sum, grad_q_sum)).astype(F32)
+    grad_gate = grad_gate_up[:, :units].astype(F32)
+    grad_up = grad_gate_up[:, units:].astype(F32)
+    own_grads = after(own_grads, grad_gate, grad_up, grad_down)
     dkey_rot = own_grads[:, :HEAD_DIM]
     dkey_low = rotary(dkey_rot, cosine[:, 0], sine[:, 0], -1.0).astype(BF16)
     dvalue_low = own_grads[:, HEAD_DIM:].astype(BF16)
-    dquery = dquery.reshape(span, heads, HEAD_DIM)
-    dquery_low = (
-        rotary(dquery * HEAD_DIM ** (-0.5), cosine, sine, -1.0).reshape(span, q_width).astype(BF16)
-    )
     dkv_low = jnp.concatenate([dkey_low, dvalue_low], axis=1)
-    grad_qkv_sum = weight_grad(normed_one, (dquery_low, dkv_low), 10)
+    grad_qkv_sum = weight_grad(normed_one, (dkv_low,), 11, into=grad_q_sum)
     grad_qkv = spread(grad_qkv_sum)
     tokens_grad, grad_gain_one = sum_rows(
         (dquery_low, after(dkv_low, grad_qkv_sum)),
@@ -1222,15 +1298,15 @@
         output[None],
         tokens_grad[None],
         gain_grads[0],
-        grad_qkv[:, :q_width].astype(F32),
+        after(grad_qkv, grad_key)[:, :q_width].astype(F32),
         grad_key,
         grad_value,
         grad_out_t.astype(F32).T,
         gain_grads[1],
         gain_grads[2],
-        grad_gate_up[:, :units].astype(F32),
-        grad_gate_up[:, units:].astype(F32),
-        grad_down_t.astype(F32).T,
+        grad_gate,
+        grad_up,
+        grad_down,
         gain_grads[3],
     )
 

time: 1040 us -> 1010 us (0.971)
  waiting for transfers between devices: 359 us -> 329 us
    reduce_scatter x5 -> x6, waiting for transfers between devices: 159 us -> 130 us  [spread(): return lax.psum_scatter(x, 'seq', scatter_dimension=0, tiled=True)]
    pallas_call x1, Pallas kernels: 164 us -> 139 us  [ffw(): pl.pallas_call(functools.partial(ffw_kernel, plan), out_shape=(jax.ShapeD...]
    pallas_call x5 -> x8, Pallas kernels: 105 us -> 127 us  [the longest x7 107 us: weight_grad(): pl.pallas_call(functools.partial(weight_grad_kernel, plan), out_shape=out...]
  transfers between devices with their start and end apart: 9 -> 10, of which waited for: 7 -> 8; matrix products, arithmetic and copies ran while one was open for 7% -> 8% of each run, Pallas kernels for 35% -> 40%
where the time goes in v4:
time: 1010 us; the launch traced here: 1000 us
  Pallas kernels  564 us (56%)
  waiting for transfers between devices  329 us (33%)
  local copies, waits for them, and re-layouts  39.7 us (4%)
  other arithmetic  33.6 us (3%)
  matrix products  18 us (2%)
  between operations  15.1 us (1%)
    pallas_call x3, Pallas kernels, sum_rows(): pl.pallas_call(functools.partial(rows_kernel, plan, rows_fn), out_shape=o...  241 us
    pallas_call x1, Pallas kernels, ffw(): pl.pallas_call(functools.partial(ffw_kernel, plan), out_shape=(jax.ShapeD...  139 us
    reduce_scatter x6, waiting for transfers between devices, spread(): return lax.psum_scatter(x, 'seq', scatter_dimension=0, tiled=True)  130 us
    all_gather x3, waiting for transfers between devices, gather_weight(): return lax.all_gather(x, both, axis=0, tiled=True)  119 us
    pallas_call x7, Pallas kernels, weight_grad(): pl.pallas_call(functools.partial(weight_grad_kernel, plan), out_shape=out...  107 us
    all_gather x1, waiting for transfers between devices, shards(): pairs = lax.all_gather(after(own_pair, w_out_t), 'seq', axis=0, tiled=True)  80.3 us
    pallas_call x1, Pallas kernels, last_sums(): pl.pallas_call(functools.partial(last_kernel, sizes, heads), out_shape=(j...  25.2 us
  transfers between devices with their start and end apart: 10, of which 8 were waited for; matrix products, arithmetic and copies ran while one was open for 8% of the time, Pallas kernels for 40%

profile of v4, /device:TPU:0, one launch (start us, length us, event | category | flops | bytes accessed | tf_op | source)
XLA Modules:
  0.0 1000.7 jit_solution(12863625092943370904)
XLA Ops:
  7.3 1.0 constant_dynamic-slice_fusion.5
  8.3 1.9 pad_maximum_fusion.6
  10.9 10.0 shard_map.228
  20.9 0.9 slice_bitcast_fusion.1
  22.0 3.5 fusion.2
  25.8 3.2 fusion.4.refs_0_
  29.0 35.7 %all-gather.5.cloned.1.call-done.refs_2_ = bf16[2304,1024]{1,0:T(8,128)(2,1)} async-done(((bf16[288,1024]{1,0:T(8,128)(2,1)}), bf16[2304,1024]{1,0:T(8,128)(2,1)}) %all-gather.5.cloned.1.call-update) | async-done | bytes 4718608 | tf_op jit(solution)/shard_map/all_gather | solution.py:1130
  64.9 4.2 fusion.14
  69.1 3.1 fusion.25
  72.2 2.7 convolution_convert_fusion
  74.9 1.1 pad_maximum_fusion.1
  75.9 20.9 %all-gather.7.cloned.1.call-done.refs_1_ = bf16[2304,512]{1,0:T(8,128)(2,1)} async-done(((bf16[288,512]{1,0:T(8,128)(2,1)}), bf16[2304,512]{1,0:T(8,128)(2,1)}) %all-gather.7.cloned.1.call-update) | async-done | bytes 2359312 | tf_op jit(solution)/shard_map/all_gather | solution.py:1130
  96.9 1.7 pad_maximum_fusion
  98.6 80.3 %all-gather.9.cloned.1.call-done.kv_ref = bf16[4096,512]{1,0:T(8,128)(2,1)} async-done(((bf16[1024,512]{1,0:T(8,128)(2,1)}), bf16[4096,512]{1,0:T(8,128)(2,1)}) %all-gather.9.cloned.1.call-update) | async-done | bytes 4194320 | tf_op jit(solution)/shard_map/all_gather | solution.py:1159
  180.3 1.3 constant_dynamic-slice_fusion.4
  182.4 1.5 copy.54.cotangent_ref
  184.7 2.5 dynamic-slice_bitcast_fusion.refs_2_.refs_3_
  187.5 2.2 slice_bitcast_fusion
  189.8 2.4 copy.66
  192.2 6.1 fusion.8
  199.0 1.3 copy.67.q_ref
  200.3 8.4 shard_map.229
  208.7 89.0 %shard_map.230 = (f32[256,2304]{1,0:T(8,128)}, f32[256,2304]{1,0:T(8,128)}, bf16[1024,2304]{1,0:T(8,128)(2,1)}) custom-call(bf16[1024,512]{1,0:T(8,128)(2,1)} %get-tuple-element.58.refs_0_, bf16[2304,512]{1,0:T(8,128)(2,1)} %all-gather.7.cloned.1.call-done.refs_1_, bf16[256,2304]{1,0:T(8,128)(2,1)} %dynamic-slice_bitcast_fusion.refs_2_.refs_3_, ...), custom_call_target="tpu_custom_call" | custom-call | tf_op jit(solution)/shard_map/pallas_call | solution.py:604
  297.7 3.1 copy.48
  300.7 1.9 copy.49
  302.6 2.0 copy.53.resid_ref
  304.6 62.5 %all-gather.11.cloned.1.call-done.gate_up_ref.refs_2_ = bf16[2304,4608]{1,0:T(8,128)(2,1)} async-done(((bf16[288,4608]{1,0:T(8,128)(2,1)}), bf16[2304,4608]{1,0:T(8,128)(2,1)}) %all-gather.11.cloned.1.call-update) | async-done | bytes 21233680 | tf_op jit(solution)/shard_map/all_gather | solution.py:1130
  367.1 139.5 %shard_map.231 = (bf16[256,2304]{1,0:T(8,128)(2,1)}, f32[8,2304]{1,0:T(8,128)}, bf16[3,256,768]{2,1,0:T(8,128)(2,1)}, bf16[1024,768]{1,0:T(8,128)(2,1)}, bf16[10...) custom-call(bf16[1024,2304]{1,0:T(8,128)(2,1)} %get-tuple-element.59., ...), custom_call_target="tpu_custom_call" | custom-call | tf_op jit(solution)/shard_map/pallas_call | solution.py:983
  506.6 15.3 %shard_map.232 = (bf16[384,2304]{1,0:T(8,128)(2,1)}, bf16[1024,768]{1,0:T(8,128)(2,1)}) custom-call(bf16[1024,768]{1,0:T(8,128)(2,1)} %get-tuple-element.69.refs_0_, bf16[1024,2304]{1,0:T(8,128)(2,1)} %get-tuple-element.64.refs_1_, bf16[3,256,768]{2,1,0:T(8,128)(2,1)} %get-tuple-element.65.refs_2_), custom_call_target="tpu_custom_call" | custom-call | tf_op jit(solution)/shard_map/pallas_call | solution.py:731
  521.9 15.8 %shard_map.233 = (bf16[384,4608]{1,0:T(8,128)(2,1)}, bf16[1024,768]{1,0:T(8,128)(2,1)}) custom-call(bf16[1024,768]{1,0:T(8,128)(2,1)} %get-tuple-element.66.refs_0_.refs_1_, bf16[1024,2304]{1,0:T(8,128)(2,1)} %get-tuple-element.64.refs_1_, bf16[3,256,768]{2,1,0:T(8,128)(2,1)} %get-tuple-element.65.refs_2_), custom_call_target="tpu_custom_call" | custom-call | tf_op jit(solution)/shard_map/pallas_call | solution.py:731
  537.8 9.4 shard_map.234
  547.1 13.3 %reduce-scatter.7.cloned.1.call-done = bf16[96,2304]{1,0:T(8,128)(2,1)} async-done(((bf16[384,2304]{1,0:T(8,128)(2,1)}), bf16[96,2304]{1,0:T(8,128)(2,1)}) %reduce-scatter.7.cloned.1.call-update) | async-done | bytes 442384 | tf_op jit(solution)/shard_map/reduce_scatter | solution.py:1212
  560.5 19.7 %shard_map.235 = (bf16[1024,2304]{1,0:T(8,128)(2,1)}, bf16[1024,2304]{1,0:T(8,128)(2,1)}) custom-call(bf16[1024,768]{1,0:T(8,128)(2,1)} %get-tuple-element.69.refs_0_, bf16[1024,768]{1,0:T(8,128)(2,1)} %get-tuple-element.66.refs_0_.refs_1_, bf16[1024,768]{1,0:T(8,128)(2,1)} %get-tuple-element.67.refs_0_.refs_2_, ...), custom_call_target="tpu_custom_call" | custom-call | tf_op jit(solution)/shard_map/pallas_call | solution.py:1033
  580.1 38.3 %shard_map.236 = bf16[1152,4608]{1,0:T(8,128)(2,1)} custom-call(bf16[1024,2304]{1,0:T(8,128)(2,1)} %get-tuple-element.59.normed_ref.refs_0_, bf16[1024,2304]{1,0:T(8,128)(2,1)} %get-tuple-element.77.refs_1_.refs_0_, bf16[1024,2304]{1,0:T(8,128)(2,1)} %get-tuple-element.76.refs_2_.refs_1_), custom_call_target="tpu_custom_call" | custom-call | tf_op jit(solution)/shard_map/pallas_call | solution.py:731
  618.5 9.7 reduce-scatter.9.cloned.1.call-done
  628.7 2.4 fusion.54.refs_5_
  631.2 1.0 pad_maximum_fusion.4.refs_1_
  632.2 101.5 %shard_map.237 = (f32[256,2304]{1,0:T(8,128)}, f32[8,2304]{1,0:T(8,128)}, f32[8,2304]{1,0:T(8,128)}, bf16[1024,2304]{1,0:T(8,128)(2,1)}) custom-call(bf16[1024,2304]{1,0:T(8,128)(2,1)} %get-tuple-element.77.refs_1_.refs_0_, bf16[1024,2304]{1,0:T(8,128)(2,1)} %get-tuple-element.76.refs_2_.refs_1_, ...), custom_call_target="tpu_custom_call" | custom-call | tf_op jit(solution)/shard_map/pallas_call | solution.py:604
  733.7 4.9 fusion.48
  738.7 1.0 pad_maximum_fusion.2.do_ref
  739.8 13.3 %shard_map.238 = (f32[1024,512]{1,0:T(8,128)}, bf16[4096,512]{1,0:T(8,128)(2,1)}) custom-call(bf16[1024,512]{1,0:T(8,128)(2,1)} %copy.67.q_ref, bf16[1024,512]{1,0:T(8,128)(2,1)} %pad_maximum_fusion.2.do_ref, f32[1024,512]{1,0:T(8,128)} %get-tuple-element.80.of_ref, f32[4,1,512]{2,1,0:T(1,128)} %get-tuple-element.81.lse_ref, ...), custom_call_target="tpu_custom_call" | custom-call | flops 16106127360 | bytes 4194304 | tf_op jit(solution)/shard_map/pallas_call | solution.py:335
  753.1 3.1 broadcast_multiply_fusion
  756.2 1.9 copy.69
  758.6 1.3 copy.68.refs_1_.refs_0_
  760.0 9.4 shard_map.240.refs_2_
  769.3 9.5 shard_map.239
  778.9 32.2 %reduce-scatter.11.cloned.1.call-done = bf16[288,4608]{1,0:T(8,128)(2,1)} async-done(((bf16[1152,4608]{1,0:T(8,128)(2,1)}), bf16[288,4608]{1,0:T(8,128)(2,1)}) %reduce-scatter.11.cloned.1.call-update) | async-done | bytes 2654224 | tf_op jit(solution)/shard_map/reduce_scatter | solution.py:1212
  812.1 1.7 convert_bitcast_fusion.1
  813.8 2.8 slice_convert_fusion
  816.6 74.6 %reduce-scatter.13.cloned.1.call-done = bf16[1024,512]{1,0:T(8,128)(2,1)} async-done(((bf16[4096,512]{1,0:T(8,128)(2,1)}), bf16[1024,512]{1,0:T(8,128)(2,1)}) %reduce-scatter.13.cloned.1.call-update) | async-done | bytes 1048592 | tf_op jit(solution)/shard_map/reduce_scatter | solution.py:1212
  891.2 1.5 convert_element_type.73
  892.7 2.4 fusion.30
  895.2 1.1 pad_maximum_fusion.5.refs_1_
  896.3 9.3 shard_map.241
  906.4 50.4 %shard_map.242 = (bf16[256,2304]{1,0:T(8,128)(2,1)}, f32[8,2304]{1,0:T(8,128)}) custom-call(bf16[1024,512]{1,0:T(8,128)(2,1)} %copy.68.refs_1_.refs_0_, bf16[1024,512]{1,0:T(8,128)(2,1)} %pad_maximum_fusion.5.refs_1_, bf16[2304,1024]{1,0:T(8,128)(2,1)} %all-gather.5.cloned.1.call-done.refs_2_, bf16[256,2304]{1,0:T(8,128)(2,1)} %dynamic-slice_bitcast_fusion.refs_2_.refs_3_, ...), custom_call_target="tpu_custom_call" | custom-call | tf_op jit(solution)/shard_map/pallas_call | solution.py:604
  957.8 1.5 copy.63
  960.4 0.7 slice.143.kv_ref
  961.1 25.2 %shard_map.243 = (f32[8,384]{1,0:T(8,128)}, f32[288,1024]{1,0:T(8,128)}, f32[288,1024]{1,0:T(8,128)}) custom-call(f32[8,8,384]{2,1,0:T(8,128)} %pad.12.x_ref, bf16[288,512]{1,0:T(8,128)(2,1)} %slice.143.kv_ref), custom_call_target="tpu_custom_call" | custom-call | tf_op jit(solution)/shard_map/pallas_call | solution.py:191
  986.4 1.5 slice_reduce_fusion.4
  987.9 0.9 slice_convert_fusion.3
  988.7 1.8 convert_bitcast_fusion.2
  990.6 1.0 copy.76
  991.6 1.0 copy.77
  992.6 1.0 copy.78
  (113 shorter events, 10.3 us)
Async XLA Ops:
  7.2 3.1 copy-start.18
  7.2 3.1 copy-start.19
  7.2 3.1 copy-start.20
  7.2 3.1 copy-start.21
  7.2 57.5 %all-gather.5.cloned.1.call-start = ((), (), s32[]{:S(2)}) async-start(), calls=%async_computation.6 | async-start | bytes 5308416 | tf_op jit(solution)/shard_map/all_gather | solution.py:1130
  10.2 86.6 %all-gather.7.cloned.1.call-start = ((), (), s32[]{:S(2)}) async-start(), calls=%async_computation.7 | async-start | bytes 2654208 | tf_op jit(solution)/shard_map/all_gather | solution.py:1130
  22.0 3.8 copy-start
  64.7 7.4 slice-start
  64.8 114.1 %all-gather.9.cloned.1.call-start = ((), (), s32[]{:S(2)}) async-start(), calls=%async_computation.8 | async-start | bytes 5242880 | tf_op jit(solution)/shard_map/all_gather | solution.py:1159
  64.8 7.3 slice-start.1
  74.8 22.0 %copy-start.5 = (bf16[288,2304]{1,0:T(8,128)(2,1)S(1)}, bf16[288,2304]{1,0:T(8,128)(2,1)}, u32[]{:S(2)}) copy-start(bf16[288,2304]{1,0:T(8,128)(2,1)} %param.23) | copy-start | bytes 3981316
  74.8 22.0 %copy-start.6 = (bf16[288,2304]{1,0:T(8,128)(2,1)S(1)}, bf16[288,2304]{1,0:T(8,128)(2,1)}, u32[]{:S(2)}) copy-start(bf16[288,2304]{1,0:T(8,128)(2,1)} %param.22) | copy-start | bytes 3981316
  96.8 270.3 %all-gather.11.cloned.1.call-start = ((), (), s32[]{:S(2)}) async-start(), calls=%async_computation.9 | async-start | bytes 23887872 | tf_op jit(solution)/shard_map/all_gather | solution.py:1130
  178.9 381.5 %reduce-scatter.7.cloned.1.call-start = ((), (), s32[]{:S(2)}) async-start(), calls=%async_computation.10 | async-start | bytes 2211840 | tf_op jit(solution)/shard_map/reduce_scatter | solution.py:1212
  182.4 5.0 copy-start.4
  521.9 106.3 %reduce-scatter.9.cloned.1.call-start = ((), (), s32[]{:S(2)}) async-start(), calls=%async_computation.11 | async-start | bytes 4423680 | tf_op jit(solution)/shard_map/reduce_scatter | solution.py:1212
  560.4 250.7 %reduce-scatter.11.cloned.1.call-start = ((), (), s32[]{:S(2)}) async-start(), calls=%async_computation.12 | async-start | bytes 13271040 | tf_op jit(solution)/shard_map/reduce_scatter | solution.py:1212
  628.2 2.9 copy-start.1
  628.2 263.0 %reduce-scatter.13.cloned.1.call-start = ((), (), s32[]{:S(2)}) async-start(), calls=%async_computation.13 | async-start | bytes 5242880 | tf_op jit(solution)/shard_map/reduce_scatter | solution.py:1212
  632.2 101.5 %copy-start.3 = (bf16[2304,512]{1,0:T(8,128)(2,1)S(1)}, bf16[2304,512]{1,0:T(8,128)(2,1)}, u32[]{:S(2)}) copy-start(bf16[2304,512]{1,0:T(8,128)(2,1)} %all-gather.7.cloned.1.call-done.refs_1_) | copy-start | bytes 7077892
  778.9 32.5 %copy-start.11 = (bf16[96,4608]{1,0:T(8,128)(2,1)S(1)}, bf16[96,4608]{1,0:T(8,128)(2,1)}, u32[]{:S(2)}) copy-start(bf16[96,4608]{1,0:T(8,128)(2,1)} %reduce-scatter.9.cloned.1.call-done) | copy-start | bytes 2654212
  811.1 1.0 copy-start.13
  811.1 145.6 %reduce-scatter.15.cloned.1.call-start = ((), (), s32[]{:S(2)}) async-start(), calls=%async_computation.14 | async-start | bytes 2949120 | tf_op jit(solution)/shard_map/reduce_scatter | solution.py:1212
  811.4 2.4 copy-start.2
  905.6 83.1 %reduce-scatter.17.cloned.1.call-start = ((), (), s32[]{:S(2)}) async-start(), calls=%async_computation.15 | async-start | bytes 1474560 | tf_op jit(solution)/shard_map/reduce_scatter | solution.py:1212
  906.4 50.4 %copy-start.14 = (f32[8,2304]{1,0:T(8,128)S(1)}, f32[8,2304]{1,0:T(8,128)}, u32[]{:S(2)}) copy-start(f32[8,2304]{1,0:T(8,128)} %get-tuple-element.93) | copy-start | bytes 221188
  906.4 50.7 %copy-start.7 = (bf16[256,2304]{1,0:T(8,128)(2,1)S(1)}, bf16[256,2304]{1,0:T(8,128)(2,1)}, u32[]{:S(2)}) copy-start(bf16[256,2304]{1,0:T(8,128)(2,1)} %get-tuple-element.62) | copy-start | bytes 3538948
  957.7 1.7 copy-start.16
  957.7 1.8 copy-start.15
  957.7 1.9 copy-start.17
  957.7 2.7 copy-start.12
  957.8 32.8 %copy-start.8 = (bf16[256,2304]{1,0:T(8,128)(2,1)S(1)}, bf16[256,2304]{1,0:T(8,128)(2,1)}, u32[]{:S(2)}) copy-start(bf16[256,2304]{1,0:T(8,128)(2,1)} %get-tuple-element.89) | copy-start | bytes 3538948
  986.4 5.2 copy-start.10
  990.6 2.0 copy-start.9
Sparse Core Ops, SparseCore 0:
  10.3 54.3 all-gather.4
  66.3 30.4 all-gather.6
  98.9 79.8 all-gather.8
  180.9 186.1 all-gather.10
  522.0 38.3 reduce-scatter.6
  562.7 65.4 reduce-scatter.8
  630.6 180.4 reduce-scatter.10
  813.4 77.7 reduce-scatter.12
  905.8 48.5 reduce-scatter.14
  956.9 30.3 reduce-scatter.16

commit v5 on v4

--- a/solution.py
+++ b/solution.py
@@ -57,59 +57,6 @@
     )
 
 
-def gather_kernel(sizes, x_ref, o_ref, send_sem, recv_sem):
-    dp_size, seq_size = sizes
-    count = dp_size * seq_size
-    dp, seq, mp = lax.axis_index("dp"), lax.axis_index("seq"), lax.axis_index("mp")
-    rank = dp * seq_size + seq
-
-    def peer(k):
-        other = lax.rem(rank + k, count)
-        return (other // seq_size, lax.rem(other, seq_size), mp)
-
-    barrier = pltpu.get_barrier_semaphore()
-    for k in range(1, count):
-        pl.semaphore_signal(barrier, inc=1, device_id=peer(k), device_id_type=MESH)
-    pl.semaphore_wait(barrier, count - 1)
-    copies = []
-    for k in range(1, count):
-        copies.append(
-            pltpu.make_async_remote_copy(
-                src_ref=x_ref,
-                dst_ref=o_ref.at[rank],
-                send_sem=send_sem.at[k],
-                recv_sem=recv_sem.at[k],
-                device_id=peer(k),
-                device_id_type=MESH,
-            )
-        )
-        copies[-1].start()
-    o_ref[pl.ds(rank, 1)] = x_ref[...][None]
-    for copy in copies:
-        copy.wait()
-
-
-def gather_gains(gains, dp_size, seq_size):
-    count = dp_size * seq_size
-    local = gains[0].shape[0]
-    width = -(-local // LANES) * LANES
-    block = jnp.stack([gain.astype(F32) for gain in gains])
-    block = jnp.pad(block, ((0, 8 - len(gains)), (0, width - local)))
-    full = pl.pallas_call(
-        functools.partial(gather_kernel, (dp_size, seq_size)),
-        out_shape=jax.ShapeDtypeStruct((count, 8, width), F32),
-        in_specs=[pl.BlockSpec(memory_space=pltpu.VMEM)],
-        out_specs=pl.BlockSpec(memory_space=pltpu.VMEM),
-        scratch_shapes=[
-            pltpu.SemaphoreType.DMA((count,)),
-            pltpu.SemaphoreType.DMA((count,)),
-        ],
-        compiler_params=pltpu.CompilerParams(collective_id=1, has_side_effects=True),
-    )(block)
-    full = jnp.transpose(full[:, : len(gains), :local], (1, 0, 2)).reshape(len(gains), -1)
-    return [full[i : i + 1] for i in range(len(gains))]
-
-
 def flipped(index, k):
     result, bit = index, 1
     while bit <= k:
@@ -119,7 +66,9 @@
     return result
 
 
-def last_kernel(sizes, heads, x_ref, kv_ref, o_ref, key_ref, value_ref, mine, from_mp, from_ws, kv_from, sems):
+def last_kernel(
+    sizes, heads, x_ref, kv_ref, o_ref, key_ref, value_ref, mine, from_mp, from_ws, kv_from, sems, kv_sem
+):
     dp_size, seq_size, mp_size = sizes
     count = dp_size * seq_size
     dp, seq, mp = lax.axis_index("dp"), lax.axis_index("seq"), lax.axis_index("mp")
@@ -153,31 +102,31 @@
     for k in range(1, count):
         pl.semaphore_signal(barrier, inc=1, device_id=ws_peer(k), device_id_type=MESH)
     pl.semaphore_wait(barrier, mp_size - 1 + count - 1)
-    copies = [remote(x_ref, from_mp.at[k], 0, k, mp_peer(k)) for k in range(1, mp_size)]
-    kv_copies = [remote(kv_ref, kv_from.at[k], 1, k, mp_peer(k)) for k in range(1, mp_size)]
+    copies = [remote(x_ref.at[ws_rank(k)], from_ws.at[k], 0, k, ws_peer(k)) for k in range(1, count)]
+    pass_on, end_rows = row_gather(kv_ref, kv_from, mp_size, mp_peer, kv_sem)
+    key_ref[...] = jnp.zeros_like(key_ref)
+    value_ref[...] = jnp.zeros_like(value_ref)
     for copy in copies:
         copy.wait()
-    total = x_ref[...]
+    total = x_ref[pl.ds(rank, 1)][0]
+    for k in range(1, count):
+        total = total + from_ws[k]
+    mine[...] = total
+    copies = [remote(mine, from_mp.at[k], 1, k, mp_peer(k)) for k in range(1, mp_size)]
+    pass_on()
+    for copy in copies:
+        copy.wait()
     for k in range(1, mp_size):
         total = total + from_mp[k]
-    mine[...] = total
-    copies = [remote(mine.at[ws_rank(k)], from_ws.at[k], 2, k, ws_peer(k)) for k in range(1, count)]
-    key_ref[...] = jnp.zeros_like(key_ref)
-    value_ref[...] = jnp.zeros_like(value_ref)
+    o_ref[...] = total
+    end_rows()
+    rows = kv_ref.shape[0]
     for k in range(mp_size):
-        if k:
-            kv_copies[k - 1].wait()
-        piece = (kv_from[k] if k else kv_ref[...]).astype(F32)
+        piece = (kv_from[k * rows : (k + 1) * rows, :] if k else kv_ref[...]).astype(F32)
         head = flipped(mp, k) * heads // (Q_HEADS // KV_HEADS)
         columns = pl.ds(pl.multiple_of(head * HEAD_DIM, HEAD_DIM), HEAD_DIM)
         key_ref[:, columns] += piece[:, :HEAD_DIM]
         value_ref[:, columns] += piece[:, HEAD_DIM:]
-    for copy in copies:
-        copy.wait()
-    own = mine[pl.ds(rank, 1)][0]
-    for k in range(1, count):
-        own = own + from_ws[k]
-    o_ref[...] = own
 
 
 def last_sums(grads, kv, kv_width, heads, sizes):
@@ -194,17 +143,238 @@
         in_specs=[pl.BlockSpec(memory_space=pltpu.VMEM)] * 2,
         out_specs=(pl.BlockSpec(memory_space=pltpu.VMEM),) * 3,
         scratch_shapes=[
+            pltpu.VMEM((8, width), F32),
+            pltpu.VMEM((mp_size, 8, width), F32),
             pltpu.VMEM((count, 8, width), F32),
-            pltpu.VMEM((mp_size, count, 8, width), F32),
-            pltpu.VMEM((count, 8, width), F32),
-            pltpu.VMEM((mp_size, *kv.shape), BF16),
-            pltpu.SemaphoreType.DMA((3, 2, max(count, mp_size))),
+            pltpu.VMEM((mp_size * kv.shape[0], kv.shape[1]), BF16),
+            pltpu.SemaphoreType.DMA((2, 2, max(count, mp_size))),
+            pltpu.SemaphoreType.DMA((2, max(6, mp_size))),
         ],
         compiler_params=pltpu.CompilerParams(
             collective_id=2, has_side_effects=True, vmem_limit_bytes=VMEM_LIMIT
         ),
     )(block, kv)
     return [total[i, :local] for i in range(len(grads))], key, value
+
+
+def travel(block, line_sem, pair_sem, seq_size):
+    far = seq_size - 1
+    dp, seq, mp = lax.axis_index("dp"), lax.axis_index("seq"), lax.axis_index("mp")
+
+    def goes_on(way):
+        return seq < far if way == 0 else seq > 0
+
+    def comes(way, distance):
+        return seq >= distance if way == 0 else seq + distance <= far
+
+    def piece(t, way, distance, sems, device):
+        place = block(t, seq - distance if way == 0 else seq + distance)
+        return pltpu.make_async_remote_copy(
+            src_ref=place,
+            dst_ref=place,
+            send_sem=sems.at[0, t, way, distance],
+            recv_sem=sems.at[1, t, way, distance],
+            device_id=device,
+            device_id_type=MESH,
+        )
+
+    def line(t, way, distance):
+        return piece(t, way, distance, line_sem, (dp, seq + 1 - 2 * way, mp))
+
+    def pair(t, way, distance):
+        return piece(t, way, distance, pair_sem, (1 - dp, seq, mp))
+
+    def start(t):
+        for way in range(2):
+            @pl.when(goes_on(way))
+            def _(way=way):
+                line(t, way, 0).start()
+
+    def share(t):
+        pair(t, 0, 0).start()
+
+    def arrival(t, distance):
+        for way in range(2):
+            @pl.when(comes(way, distance))
+            def _(way=way):
+                line(t, way, distance - 1).wait_recv()
+                if distance < far:
+                    @pl.when(goes_on(way))
+                    def _():
+                        line(t, way, distance).start()
+
+                pair(t, way, distance).start()
+
+    def complete(t):
+        pair(t, 0, 0).wait_recv()
+        for way in range(2):
+            for distance in range(1, seq_size):
+                @pl.when(comes(way, distance))
+                def _(way=way, distance=distance):
+                    pair(t, way, distance).wait_recv()
+
+    def drain(t):
+        pair(t, 0, 0).wait_send()
+        for way in range(2):
+            for distance in range(far):
+                @pl.when(goes_on(way) & comes(way, distance))
+                def _(way=way, distance=distance):
+                    line(t, way, distance).wait_send()
+
+            for distance in range(1, seq_size):
+                @pl.when(comes(way, distance))
+                def _(way=way, distance=distance):
+                    pair(t, way, distance).wait_send()
+
+    return start, share, arrival, complete, drain
+
+
+def window(rank, local):
+    return rank * local // LANES * LANES
+
+
+def window_width(count, local):
+    widest = max(rank * local - window(rank, local) for rank in range(count)) + local
+    return -(-widest // LANES) * LANES
+
+
+def front_kernel(plan, tokens_ref, wq_ref, wk_ref, wv_ref, wo_ref, gains_ref, *refs):
+    dp_size, seq_size, heads, pieces, row_step = plan
+    gain_rows, qkv_ref, normed_ref, w_qkv_ref, w_out_ref = refs[:5]
+    tokens, normed, w_qkv, w_out, gains, refs = *refs[5:10], refs[10:]
+    load_sem, gain_sem, line_sem, pair_sem, store_sem = refs
+    count = dp_size * seq_size
+    span, width = tokens.shape
+    shard, q_width = wq_ref.shape
+    columns = w_qkv.shape[1]
+    dp, seq, mp = lax.axis_index("dp"), lax.axis_index("seq"), lax.axis_index("mp")
+    rank = dp * seq_size + seq
+
+    def peer(k):
+        other = lax.rem(rank + k, count)
+        return (other // seq_size, lax.rem(other, seq_size), mp)
+
+    own = pl.ds(pl.multiple_of(rank * shard, 16), shard)
+    head = pl.ds(pl.multiple_of(mp * heads // (Q_HEADS // KV_HEADS) * HEAD_DIM, HEAD_DIM), HEAD_DIM)
+    loads = [
+        pltpu.make_async_copy(wq_ref, w_qkv.at[own, pl.ds(0, q_width)], load_sem.at[0]),
+        pltpu.make_async_copy(wk_ref.at[:, head], w_qkv.at[own, pl.ds(q_width, HEAD_DIM)], load_sem.at[1]),
+        pltpu.make_async_copy(
+            wv_ref.at[:, head], w_qkv.at[own, pl.ds(q_width + HEAD_DIM, HEAD_DIM)], load_sem.at[2]
+        ),
+        pltpu.make_async_copy(wo_ref, w_out.at[own], load_sem.at[3]),
+        pltpu.make_async_copy(tokens_ref, tokens, load_sem.at[4]),
+    ]
+    for load in loads:
+        load.start()
+    barrier = pltpu.get_barrier_semaphore()
+    for k in range(1, count):
+        pl.semaphore_signal(barrier, inc=1, device_id=peer(k), device_id_type=MESH)
+    pl.semaphore_wait(barrier, count - 1)
+
+    def block(t, at):
+        first = (dp * seq_size + at) * shard
+        if t == pieces:
+            return w_out.at[pl.ds(pl.multiple_of(first, 16), shard)]
+        piece = shard // pieces
+        return w_qkv.at[pl.ds(pl.multiple_of(first + t * piece, 16), piece)]
+
+    start, share, arrival, complete, drain = travel(block, line_sem, pair_sem, seq_size)
+    for load in loads[:4]:
+        load.wait()
+    gain_copies = [remote_copy(gains_ref, gains.at[rank], gain_sem, (k,), peer(k)) for k in range(1, count)]
+    for t in range(pieces):
+        start(t)
+    for t in range(pieces):
+        share(t)
+    gains[pl.ds(rank, 1)] = gains_ref[...][None]
+    gain_rows[...] = jnp.zeros_like(gain_rows)
+    for copy in gain_copies:
+        copy.wait()
+    for r in range(count):
+        first = window(r, shard)
+        gain_rows[:, first : first + gains.shape[2]] += gains[r]
+    loads[4].wait()
+
+    def norm_rows(r, carry):
+        rows = pl.ds(pl.multiple_of(r * row_step, row_step), row_step)
+        vector = tokens[rows, :].astype(F32)
+        normed[rows, :] = (vector * rms_scale(vector) * gain_rows[0:1, :]).astype(BF16)
+        return carry
+
+    blocks = span // row_step
+    for t in range(pieces):
+        lax.fori_loop(blocks * t // pieces, blocks * (t + 1) // pieces, norm_rows, 0)
+        arrival(t, 1)
+    for distance in range(2, seq_size):
+        if distance == seq_size - 1:
+            start(pieces)
+            share(pieces)
+        for t in range(pieces):
+            arrival(t, distance)
+    for t in range(pieces):
+        complete(t)
+    stores = [
+        pltpu.make_async_copy(w_qkv, w_qkv_ref, store_sem.at[0]),
+        pltpu.make_async_copy(normed, normed_ref, store_sem.at[1]),
+        pltpu.make_async_copy(w_out, w_out_ref, store_sem.at[2]),
+    ]
+    stores[0].start()
+    stores[1].start()
+    tiles = columns // HEAD_DIM
+    for i in range(max(tiles, seq_size - 1)):
+        if i < tiles:
+            part = slice(i * HEAD_DIM, (i + 1) * HEAD_DIM)
+            qkv_ref[:, part] = dot_nn(normed[...], w_qkv[:, part])
+        if i < seq_size - 1:
+            arrival(pieces, i + 1)
+    complete(pieces)
+    stores[2].start()
+    for store in stores:
+        store.wait()
+    for t in range(pieces + 1):
+        drain(t)
+
+
+def front(tokens, w_query, w_key, w_value, w_out_t, gains, heads, sizes):
+    dp_size, seq_size, _ = sizes
+    count = dp_size * seq_size
+    span, width = tokens.shape
+    shard, q_width = w_query.shape
+    columns = q_width + 2 * HEAD_DIM
+    pieces = 3
+    lanes = window_width(count, shard)
+    offset = (lax.axis_index("dp") * seq_size + lax.axis_index("seq")) * shard % LANES
+    block = jnp.pad(jnp.stack([gain.astype(F32) for gain in gains]), ((0, 8 - len(gains)), (0, 0)))
+    block = lax.dynamic_update_slice_in_dim(jnp.zeros((8, lanes), F32), block, offset, 1)
+    plan = (dp_size, seq_size, heads, pieces, min(32, span))
+    return pl.pallas_call(
+        functools.partial(front_kernel, plan),
+        out_shape=(
+            jax.ShapeDtypeStruct((8, max(width, window(count - 1, shard) + lanes)), F32),
+            jax.ShapeDtypeStruct((span, columns), F32),
+            jax.ShapeDtypeStruct((span, width), BF16),
+            jax.ShapeDtypeStruct((width, columns), BF16),
+            jax.ShapeDtypeStruct((width, q_width), BF16),
+        ),
+        in_specs=[pl.BlockSpec(memory_space=pl.ANY)] * 5 + [pl.BlockSpec(memory_space=pltpu.VMEM)],
+        out_specs=(pl.BlockSpec(memory_space=pltpu.VMEM),) * 2 + (pl.BlockSpec(memory_space=pl.ANY),) * 3,
+        scratch_shapes=[
+            pltpu.VMEM((span, width), BF16),
+            pltpu.VMEM((span, width), BF16),
+            pltpu.VMEM((width, columns), BF16),
+            pltpu.VMEM((width, q_width), BF16),
+            pltpu.VMEM((count, 8, lanes), F32),
+            pltpu.SemaphoreType.DMA((5,)),
+            pltpu.SemaphoreType.DMA((2, count)),
+            pltpu.SemaphoreType.DMA((2, pieces + 1, 2, seq_size)),
+            pltpu.SemaphoreType.DMA((2, pieces + 1, 2, seq_size)),
+            pltpu.SemaphoreType.DMA((3,)),
+        ],
+        compiler_params=pltpu.CompilerParams(
+            collective_id=1, has_side_effects=True, vmem_limit_bytes=VMEM_LIMIT
+        ),
+    )(tokens, w_query, w_key, w_value, w_out_t, block)
 
 
 def key_mask(shape, first_key, first_query, tile, far):
@@ -233,7 +403,7 @@
 
 
 def head_rows(ref, index, tile):
-    block = ref[pl.ds(index * tile, tile), :]
+    block = ref[pl.ds(pl.multiple_of(index * tile, tile), tile), :]
     return jnp.concatenate(
         [block[:, h * HEAD_DIM : (h + 1) * HEAD_DIM] for h in range(ref.shape[1] // HEAD_DIM)], axis=0
     )
@@ -342,9 +512,6 @@
         out_specs=(pl.BlockSpec(memory_space=pltpu.VMEM),) * 2,
         scratch_shapes=[pltpu.VMEM(pairs.shape, F32), pltpu.VMEM((HEAD_DIM, rows), F32)],
         compiler_params=pltpu.CompilerParams(vmem_limit_bytes=VMEM_LIMIT),
-        cost_estimate=pl.CostEstimate(
-            flops=30 * queries.size * span, bytes_accessed=8 * queries.size, transcendentals=0
-        ),
     )(queries, dout, exact, lse, pairs)
 
 
@@ -361,9 +528,10 @@
     return copy
 
 
-def sum_direct(parts_at, steps, step, mp_size, peer, total, sent, arrived, sems):
+def sum_direct(ready, parts_at, steps, step, mp_size, peer, total, sent, arrived, sems):
     copies = []
     for t in range(steps):
+        ready(t)
         for k in range(mp_size - 1, -1, -1):
             part = parts_at(t, k)
             if k == 0:
@@ -380,7 +548,7 @@
     return copies
 
 
-def sum_square(parts_at, steps, step, peer, total, kept, sent, arrived, sems):
+def sum_square(ready, parts_at, steps, step, peer, total, kept, sent, arrived, sems, eager):
     half = step // 2
     copies, second = [], []
 
@@ -394,6 +562,9 @@
 
     for t in range(steps):
         first = t * step
+        ready(t)
+        if eager and t:
+            second_hop(t - 1)
         far = parts_at(t, 3)
         sent[t, 0, 1] = far[:, :half].astype(BF16)
         sent[t, 1, 1] = far[:, half:].astype(BF16)
@@ -410,7 +581,7 @@
             remote_copy(sent.at[t, 1, pl.ds(0, 2)], arrived.at[t, 1, pl.ds(0, 2)], sems, (t, 1), peer(2))
         )
         total[:, first : first + step] = parts_at(t, 0)
-    for t in range(steps):
+    for t in range(steps - 1 if eager else 0, steps):
         second_hop(t)
     for t in range(steps):
         first = t * step
@@ -510,17 +681,19 @@
         pl.semaphore_signal(barrier, inc=1, device_id=peer(k), device_id_type=MESH)
     pl.semaphore_wait(barrier, mp_size - 1)
 
+    def ready(t):
+        weight_copies[t].wait()
+        if t + 1 < steps:
+            weight_copies[t + 1].start()
+
     def parts_at(t, k):
-        if k == mp_size - 1:
-            weight_copies[t].wait()
-            if t + 1 < steps:
-                weight_copies[t + 1].start()
         if t == 0:
             for copy in left_copies[k]:
                 copy.wait()
         return dot_nt(left[k], weight[t % 2])
 
     finish_rows(
+        ready,
         parts_at,
         (mp_size, share, step, row_step),
         (rows_fn, aux, outs, gathered if gather else None),
@@ -530,16 +703,20 @@
     )
 
 
-def finish_rows(parts_at, sizes, rows, peer, buffers, sems):
+def finish_rows(ready, parts_at, sizes, rows, peer, buffers, sems, eager=False):
     mp_size, share, step, row_step = sizes
     rows_fn, aux, outs, gathered = rows
     total, own, kept, sent, arrived = buffers
     sum_sem, row_sem, keep_sem = sems
     steps = total.shape[1] // step
     if mp_size == 4:
-        sums = sum_square(parts_at, steps, step, peer, total, kept, sent, arrived, sum_sem)
+        sums = sum_square(
+            ready, parts_at, steps, step, peer, total, kept, sent, arrived, sum_sem, eager
+        )
     else:
-        sums = sum_direct(parts_at, steps, step, mp_size, peer, total, sent, arrived, sum_sem)
+        sums = sum_direct(
+            ready, parts_at, steps, step, mp_size, peer, total, sent, arrived, sum_sem
+        )
 
     def rows_at(r, carry):
         rows = pl.ds(pl.multiple_of(r * row_step, row_step), row_step)
@@ -621,13 +798,13 @@
 
 
 def weight_grad_kernel(plan, *refs):
-    n_right, tile, half, first_column, n_into, next_step, mp_size = plan
+    n_right, tile, half, first_column, n_into, steps, mp_size = plan
     left_ref, rights, refs = refs[0], refs[1 : 1 + n_right], refs[1 + n_right + n_into :]
-    if next_step:
-        steps_ref, out_ref, gathered, refs = refs[0], refs[1], refs[2], refs[3:]
-        own_rows, row_sem, refs = refs[0], refs[1], refs[2:]
-    else:
-        out_ref, refs = refs[0], refs[1:]
+    out_ref, refs = refs[0], refs[1:]
+    if steps:
+        steps_ref, gathered, refs = left_ref, refs[: len(steps)], refs[len(steps) :]
+        own_rows, row_sems, refs = refs[0], refs[1 : 1 + len(steps)], refs[1 + len(steps) :]
+        left_ref = gathered[0]
     left, right, sent, arrived, own, result, in_sem, swap_sem, out_sem = refs
     dp, seq, mp = lax.axis_index("dp"), lax.axis_index("seq"), lax.axis_index("mp")
     other = (1 - dp, seq, mp)
@@ -635,14 +812,15 @@
     def peer(k):
         return (dp, seq, flipped(mp, k))
 
-    if next_step:
-        rows_load = pltpu.make_async_copy(steps_ref.at[next_step], own_rows, in_sem.at[4])
+    if steps:
+        rows_load = pltpu.make_async_copy(
+            steps_ref.at[pl.ds(steps[0], len(steps))], own_rows, in_sem.at[4]
+        )
         rows_load.start()
     lefts = []
     for i, side in enumerate((1 - dp, dp)):
         columns = pl.ds(pl.multiple_of(side * half, LANES), half)
         lefts.append(pltpu.make_async_copy(left_ref.at[:, columns], left.at[i], in_sem.at[2 + i]))
-        lefts[i].start()
     sources = []
     for ref in rights:
         for first in range(0, ref.shape[1], tile):
@@ -655,16 +833,29 @@
     loads[0].start()
     barrier = pltpu.get_barrier_semaphore()
     pl.semaphore_signal(barrier, inc=1, device_id=other, device_id_type=MESH)
-    if next_step:
+    if steps:
         for k in range(1, mp_size):
             pl.semaphore_signal(barrier, inc=1, device_id=peer(k), device_id_type=MESH)
-    pl.semaphore_wait(barrier, mp_size if next_step else 1)
-    if next_step:
+    pl.semaphore_wait(barrier, mp_size if steps else 1)
+    if steps:
         rows_load.wait()
-        share = own_rows.shape[0]
-        keep = pltpu.make_async_copy(own_rows, gathered.at[pl.ds(0, share)], in_sem.at[4])
-        keep.start()
-        pass_on, end_rows = row_gather(own_rows, gathered, mp_size, peer, row_sem)
+        share = own_rows.shape[1]
+        keeps = [
+            pltpu.make_async_copy(own_rows.at[n], gathered[n].at[pl.ds(0, share)], in_sem.at[4 + n])
+            for n in range(len(steps))
+        ]
+        for copy in keeps:
+            copy.start()
+        pass_on, end_rows = row_gather(own_rows.at[0], gathered[0], mp_size, peer, row_sems[0])
+        pass_on()
+        end_rows()
+        keeps[0].wait()
+        rest = [
+            row_gather(own_rows.at[n], gathered[n], mp_size, peer, row_sems[n])
+            for n in range(1, len(steps))
+        ]
+    for copy in lefts:
+        copy.start()
     swaps, stores = [], []
 
     def finish(t):
@@ -694,20 +885,23 @@
         own[t % 2] = dot_tn(left[1], right[t % 2])
         if t >= 1:
             finish(t - 1)
-        if t == tiles // 2 and next_step:
-            pass_on()
+        if t == tiles // 2 and steps:
+            for pass_on, _ in rest:
+                pass_on()
     finish(tiles - 1)
     for store in stores[-2:]:
         store.wait()
     for swap in swaps:
         swap.wait_send()
-    if next_step:
-        keep.wait()
-        end_rows()
-
-
-def weight_grad(left, rights, collective_id, into=None, columns=0, steps=None, next_step=0, mp_size=1):
-    rows, width = left.shape
+    if steps:
+        for copy in keeps[1:]:
+            copy.wait()
+        for _, end_rows in rest:
+            end_rows()
+
+
+def weight_grad(left, rights, collective_id, into=None, columns=0, steps=(), mp_size=1):
+    rows, width = rights[0].shape[0], left.shape[-1]
     half = width // 2
     total = sum(right.shape[1] for right in rights)
     tile = next(
@@ -720,14 +914,11 @@
     earlier = () if into is None else (into,)
     out_shape = [jax.ShapeDtypeStruct((half, first + total + columns), BF16)]
     scratch = []
-    if next_step:
-        earlier = (steps,)
-        out_shape.append(jax.ShapeDtypeStruct((steps.shape[1] * mp_size, steps.shape[2]), BF16))
-        scratch = [
-            pltpu.VMEM(steps.shape[1:], BF16),
-            pltpu.SemaphoreType.DMA((2, max(6, mp_size))),
-        ]
-    plan = (len(rights), tile, half, first, 0 if into is None else 1, next_step, mp_size)
+    if steps:
+        out_shape += [jax.ShapeDtypeStruct((rows, width), BF16)] * len(steps)
+        scratch = [pltpu.VMEM((len(steps), *left.shape[1:]), BF16)]
+        scratch += [pltpu.SemaphoreType.DMA((2, max(6, mp_size)))] * len(steps)
+    plan = (len(rights), tile, half, first, len(earlier), tuple(steps), mp_size)
     results = pl.pallas_call(
         functools.partial(weight_grad_kernel, plan),
         out_shape=out_shape,
@@ -742,7 +933,7 @@
             pltpu.VMEM((tiles, half, tile), BF16),
             pltpu.VMEM((2, half, tile), F32),
             pltpu.VMEM((2, half, tile), BF16),
-            pltpu.SemaphoreType.DMA((5,)),
+            pltpu.SemaphoreType.DMA((4 + max(1, len(steps)),)),
             pltpu.SemaphoreType.DMA((2, tiles)),
             pltpu.SemaphoreType.DMA((2,)),
         ],
@@ -750,7 +941,7 @@
             collective_id=collective_id, has_side_effects=True, vmem_limit_bytes=VMEM_LIMIT
         ),
     )(left, *rights, *earlier)
-    return results if next_step else results[0]
+    return results if steps else results[0]
 
 
 def ffw_kernel(plan, normed_ref, gate_up_ref, shard_ref, resid_ref, cotangent_ref, gain_ref, *refs):
@@ -768,41 +959,11 @@
     def peer(k):
         return (dp, seq, flipped(mp, k))
 
-    def along(way):
-        return (dp, seq + 1 - 2 * way, mp)
-
-    def goes_on(way):
-        return seq < far if way == 0 else seq > 0
-
-    def comes(way, distance):
-        return seq >= distance if way == 0 else seq + distance <= far
-
     def block(t, at):
         first = pl.multiple_of((dp * seq_size + at) * piece, piece)
         return down.at[t, pl.ds(first, piece)]
 
-    def line(t, way, distance):
-        at = seq - distance if way == 0 else seq + distance
-        return pltpu.make_async_remote_copy(
-            src_ref=block(t, at),
-            dst_ref=block(t, at),
-            send_sem=line_sem.at[0, t, way, distance],
-            recv_sem=line_sem.at[1, t, way, distance],
-            device_id=along(way),
-            device_id_type=MESH,
-        )
-
-    def pair(t, way, distance):
-        at = seq - distance if way == 0 else seq + distance
-        return pltpu.make_async_remote_copy(
-            src_ref=block(t, at),
-            dst_ref=block(t, at),
-            send_sem=pair_sem.at[0, t, way, distance],
-            recv_sem=pair_sem.at[1, t, way, distance],
-            device_id=sibling,
-            device_id_type=MESH,
-        )
-
+    start, share_piece, arrival, complete, drain = travel(block, line_sem, pair_sem, seq_size)
     normed_load = pltpu.make_async_copy(normed_ref, normed, local_sem.at[0])
     normed_load.start()
     shard_loads = [
@@ -838,35 +999,21 @@
         pl.semaphore_signal(barrier, inc=1, device_id=peer(k), device_id_type=MESH)
     pl.semaphore_signal(barrier, inc=1, device_id=sibling, device_id_type=MESH)
     for way in range(2):
-        @pl.when(goes_on(way))
+        @pl.when(seq < far if way == 0 else seq > 0)
         def _(way=way):
-            pl.semaphore_signal(barrier, inc=1, device_id=along(way), device_id_type=MESH)
+            pl.semaphore_signal(
+                barrier, inc=1, device_id=(dp, seq + 1 - 2 * way, mp), device_id_type=MESH
+            )
 
     line_peers = (seq + far) // seq_size + (2 * far - seq) // seq_size
     pl.semaphore_wait(barrier, mp_size + line_peers)
 
     for t in range(steps):
         shard_loads[t].wait()
-        for way in range(2):
-            @pl.when(goes_on(way))
-            def _(t=t, way=way):
-                line(t, way, 0).start()
+        start(t)
     for t in range(steps):
-        pair(t, 0, 0).start()
+        share_piece(t)
     normed_load.wait()
-
-    def arrival(t, distance):
-        for way in range(2):
-            @pl.when(comes(way, distance))
-            def _(way=way):
-                line(t, way, distance - 1).wait_recv()
-                if distance < far:
-                    @pl.when(goes_on(way))
-                    def _():
-                        line(t, way, distance).start()
-
-                pair(t, way, distance).start()
-
     arrivals = [(t, distance) for distance in range(1, seq_size) for t in range(steps)]
     tiles = units // tile
     early = [(2 * n + 2, event) for n, event in enumerate(arrivals) if 2 * n + 2 < tiles]
@@ -928,27 +1075,24 @@
     ]
     waiting = list(late)
 
+    def ready(t):
+        while (t, far) in waiting:
+            arrival(*waiting.pop(0))
+        complete(t)
+        down_stores[t].start()
+
     def parts_at(t, k):
-        if k == mp_size - 1:
-            while (t, far) in waiting:
-                arrival(*waiting.pop(0))
-            pair(t, 0, 0).wait_recv()
-            for way in range(2):
-                for distance in range(1, seq_size):
-                    @pl.when(comes(way, distance))
-                    def _(way=way, distance=distance):
-                        pair(t, way, distance).wait_recv()
-
-            down_stores[t].start()
         return dot_nt(hidden[k], down[t])
 
     finish_rows(
+        ready,
         parts_at,
         (mp_size, share, step, row_step),
         (after_ffw, (resid_ref, cotangent_ref, gain_ref), (output_ref, gain_grad_ref), dmixed_ref),
         peer,
         buffers,
         (sum_sem, row_sem, local_sem.at[0]),
+        eager=True,
     )
     own_store = pltpu.make_async_copy(buffers[1], own_ref, local_sem.at[0])
     own_store.start()
@@ -956,17 +1100,7 @@
         store.wait()
     own_store.wait()
     for t in range(steps):
-        pair(t, 0, 0).wait_send()
-        for way in range(2):
-            for distance in range(seq_size - 1):
-                @pl.when(goes_on(way) & comes(way, distance))
-                def _(t=t, way=way, distance=distance):
-                    line(t, way, distance).wait_send()
-
-            for distance in range(1, seq_size):
-                @pl.when(comes(way, distance))
-                def _(t=t, way=way, distance=distance):
-                    pair(t, way, distance).wait_send()
+        drain(t)
 
 
 def ffw(normed, gate_up_w, down_shard, resid, cotangent, gain, sizes, collective_id):
@@ -1118,8 +1252,6 @@
     dp, seq, mp = lax.axis_index("dp"), lax.axis_index("seq"), lax.axis_index("mp")
     both = ("dp", "seq")
     heads = w_query.shape[1] // HEAD_DIM
-    group = Q_HEADS // KV_HEADS
-    kv_first = mp * heads // group
     q_width = heads * HEAD_DIM
     span = tokens.shape[1]
     width = tokens.shape[2]
@@ -1129,35 +1261,28 @@
     def gather_weight(x):
         return lax.all_gather(x, both, axis=0, tiled=True)
 
-    w_qkv_own = jnp.concatenate(
-        [
-            w_query,
-            lax.dynamic_slice_in_dim(w_key, kv_first * HEAD_DIM, HEAD_DIM, 1),
-            lax.dynamic_slice_in_dim(w_value, kv_first * HEAD_DIM, HEAD_DIM, 1),
-        ],
-        axis=1,
-    )
-    w_qkv = gather_weight(w_qkv_own)
-    gain_one, gain_two, gain_three, gain_four = gather_gains(
-        [pre_attn_gain, post_attn_gain, pre_ffw_gain, post_ffw_gain], dp_size, seq_size
-    )
-
-    inputs = tokens[0].astype(F32)
+    sizes = (dp_size, seq_size, mp_size)
+    gain_rows, qkv, normed_one, w_qkv, w_out_t = front(
+        tokens[0],
+        w_query,
+        w_key,
+        w_value,
+        w_out.T,
+        [pre_attn_gain, post_attn_gain, pre_ffw_gain, post_ffw_gain],
+        heads,
+        sizes,
+    )
+    gain_one, gain_two, gain_three, gain_four = (gain_rows[i : i + 1, :width] for i in range(4))
     positions = seq * span + jnp.arange(span, dtype=jnp.int32)
     half_dim = HEAD_DIM // 2
     frequency = ROPE_BASE ** (-jnp.arange(half_dim, dtype=F32) * 2.0 / HEAD_DIM)
     angles = positions.astype(F32)[:, None, None] * frequency
     cosine = jnp.cos(angles)
     sine = jnp.sin(angles)
-    scale_one = rms_scale(inputs)
-    normed_one = (inputs * scale_one * gain_one).astype(BF16)
-    w_out_t = gather_weight(after(w_out.T, w_qkv, normed_one))
-    key_lin = dot_nn(normed_one, w_qkv[:, q_width : q_width + HEAD_DIM])
-    keys_own = rotary(key_lin, cosine[:, 0], sine[:, 0], 1.0).astype(BF16)
-    values_own = dot_nn(normed_one, w_qkv[:, q_width + HEAD_DIM :]).astype(BF16)
-    own_pair = jnp.concatenate([keys_own, values_own], axis=1)
-    pairs = lax.all_gather(after(own_pair, w_out_t), "seq", axis=0, tiled=True)
-    query_lin = dot_nn(normed_one, w_qkv[:, :q_width]).reshape(span, heads, HEAD_DIM)
+    keys_own = rotary(qkv[:, q_width : q_width + HEAD_DIM], cosine[:, 0], sine[:, 0], 1.0)
+    own_pair = jnp.concatenate([keys_own, qkv[:, q_width + HEAD_DIM :]], axis=1).astype(BF16)
+    pairs = lax.all_gather(own_pair, "seq", axis=0, tiled=True)
+    query_lin = qkv[:, :q_width].reshape(span, heads, HEAD_DIM)
     queries = (rotary(query_lin, cosine, sine, 1.0) * HEAD_DIM ** (-0.5)).astype(BF16)
     queries = queries.reshape(span, q_width)
 
@@ -1185,7 +1310,6 @@
         mp_size,
         3,
     )
-    sizes = (dp_size, seq_size, mp_size)
     shard_count = dp_size * seq_size
     steps = width // row_plan(width, share, mp_size)[0]
 
@@ -1211,25 +1335,21 @@
     def spread(x):
         return lax.psum_scatter(x, "seq", scatter_dimension=0, tiled=True)
 
-    dmixed_low, grad_sums = [dmixed_first], []
-    for t in range(steps):
-        into = grad_sums[-1] if t > 1 else None
-        columns = units * (steps - 2) if t == 1 else 0
-        if t + 1 < steps:
-            grad_sum, arrived = weight_grad(
-                dmixed_low[t],
-                (hidden,),
-                20 + t,
-                into=into,
-                columns=columns,
-                steps=dmixed_own,
-                next_step=t + 1,
-                mp_size=mp_size,
-            )
-            dmixed_low.append(arrived)
-        else:
-            grad_sum = weight_grad(dmixed_low[t], (hidden,), 20 + t, into=into, columns=columns)
-        grad_sums.append(grad_sum)
+    grad_sums = [weight_grad(dmixed_first, (hidden,), 20)]
+    grad_sum, *arrived = weight_grad(
+        after(dmixed_own, grad_sums[0]),
+        (hidden,),
+        21,
+        columns=units * (steps - 2),
+        steps=tuple(range(1, steps)),
+        mp_size=mp_size,
+    )
+    for t in range(2, steps):
+        grad_sum = weight_grad(
+            arrived[t - 1], (hidden,), 20 + t, into=grad_sum, columns=units * (steps - 1 - t)
+        )
+    grad_sums.append(grad_sum)
+    dmixed_low = [dmixed_first, *arrived]
     grad_down_first = spread(grad_sums[0])
     grad_down_rest = spread(after(grad_sums[-1], grad_down_first))
     grad_down = [grad_down_first] + [

time: 1010 us -> 996 us (0.986)
  waiting for transfers between devices: 329 us -> 261 us
  Pallas kernels: 564 us -> 629 us
  matrix products: 18 us -> 5.1 us
    pallas_call x1, Pallas kernels: 9.96 us -> 73.2 us  [front(): pl.pallas_call(functools.partial(front_kernel, plan), out_shape=(jax.Shap...]
    all_gather x3 -> x1, waiting for transfers between devices: 119 us -> 67.9 us  [gather_weight(): return lax.all_gather(x, both, axis=0, tiled=True)]
    reduce_scatter x6, waiting for transfers between devices: 130 us -> 116 us  [spread(): return lax.psum_scatter(x, 'seq', scatter_dimension=0, tiled=True)]
    dot_general x4 -> x1, matrix products: 18 us -> 5.1 us  [dot_nn(): lax.dot_general(left, right, (((1,), (0,)), ((), ())), preferred_element_...]
  transfers between devices with their start and end apart: 10 -> 8, of which waited for: 8 -> 6; matrix products, arithmetic and copies ran while one was open for 8% -> 6% of each run, Pallas kernels for 40% -> 40%
where the time goes in v5:
time: 996 us; the launch traced here: 986 us
  Pallas kernels  629 us (63%)
  waiting for transfers between devices  261 us (26%)
  local copies, waits for them, and re-layouts  44.3 us (4%)
  other arithmetic  31.6 us (3%)
  between operations  15.1 us (2%)
    pallas_call x3, Pallas kernels, sum_rows(): pl.pallas_call(functools.partial(rows_kernel, plan, rows_fn), out_shape=o...  240 us
    pallas_call x1, Pallas kernels, ffw(): pl.pallas_call(functools.partial(ffw_kernel, plan), out_shape=(jax.ShapeD...  141 us
    reduce_scatter x6, waiting for transfers between devices, spread(): return lax.psum_scatter(x, 'seq', scatter_dimension=0, tiled=True)  116 us
    pallas_call x7, Pallas kernels, weight_grad(): pl.pallas_call(functools.partial(weight_grad_kernel, plan), out_shape=out...  115 us
    all_gather x1, waiting for transfers between devices, shards(): pairs = lax.all_gather(own_pair, 'seq', axis=0, tiled=True)  76.4 us
    pallas_call x1, Pallas kernels, front(): pl.pallas_call(functools.partial(front_kernel, plan), out_shape=(jax.Shap...  73.2 us
    all_gather x1, waiting for transfers between devices, gather_weight(): return lax.all_gather(x, both, axis=0, tiled=True)  67.9 us
  transfers between devices with their start and end apart: 8, of which 6 were waited for; matrix products, arithmetic and copies ran while one was open for 6% of the time, Pallas kernels for 40%

profile of v5, /device:TPU:0, one launch (start us, length us, event | category | flops | bytes accessed | tf_op | source)
XLA Modules:
  0.0 986.3 jit_solution(820823949747332811)
XLA Ops:
  7.3 0.7 stack.35
  10.9 73.2 %shard_map.228 = (f32[8,2304]{1,0:T(8,128)}, f32[1024,1024]{1,0:T(8,128)}, bf16[1024,2304]{1,0:T(8,128)(2,1)}, bf16[2304,1024]{1,0:T(8,128)(2,1)}, bf16[2304,512]{1,0:T(8,128)(2,1)}) custom-call(bf16[1024,2304]{1,0:T(8,128)(2,1)} %bitcast.40, bf16[288,512]{1,0:T(8,128)(2,1)} %wq_ref.1, bf16[288,1024]{1,0:T(8,128)(2,1)} %wk_ref.1, bf16[288,1024]{1,0:T(8,128)(2,1)} %wv_ref.1, ...), custom_call_target="tpu_custom_call" | custom-call | tf_op jit(solution)/shard_map/pallas_call | solution.py:351
  84.1 1.3 slice.146
  85.4 3.7 fusion.10
  89.2 1.1 pad_maximum_fusion.1
  90.9 3.0 pad_maximum_fusion
  93.9 76.4 %all-gather.3.cloned.1.call-done.kv_ref = bf16[4096,512]{1,0:T(8,128)(2,1)} async-done(((bf16[1024,512]{1,0:T(8,128)(2,1)}), bf16[4096,512]{1,0:T(8,128)(2,1)}) %all-gather.3.cloned.1.call-update) | async-done | bytes 4194320 | tf_op jit(solution)/shard_map/all_gather | solution.py:1284
  170.4 1.8 slice.83
  172.1 2.4 reshape.154
  174.5 2.3 multiply_subtract_fusion
  176.8 1.1 fusion
  178.0 1.2 copy.45
  180.6 1.5 constant_dynamic-slice_fusion.4
  182.8 1.5 copy.37.cotangent_ref
  184.3 2.5 dynamic-slice_bitcast_fusion.refs_2_.refs_3_
  186.8 8.0 shard_map.229
  194.8 89.1 %shard_map.230 = (f32[256,2304]{1,0:T(8,128)}, f32[256,2304]{1,0:T(8,128)}, bf16[1024,2304]{1,0:T(8,128)(2,1)}) custom-call(bf16[1024,512]{1,0:T(8,128)(2,1)} %get-tuple-element.60.refs_0_, bf16[2304,512]{1,0:T(8,128)(2,1)} %get-tuple-element.61.refs_1_, bf16[256,2304]{1,0:T(8,128)(2,1)} %dynamic-slice_bitcast_fusion.refs_2_.refs_3_, ...), custom_call_target="tpu_custom_call" | custom-call | tf_op jit(solution)/shard_map/pallas_call | solution.py:781
  283.9 3.0 copy.31
  286.9 1.9 copy.32
  288.8 2.0 copy.36.resid_ref
  290.8 67.9 %all-gather.5.cloned.1.call-done.gate_up_ref.refs_2_ = bf16[2304,4608]{1,0:T(8,128)(2,1)} async-done(((bf16[288,4608]{1,0:T(8,128)(2,1)}), bf16[2304,4608]{1,0:T(8,128)(2,1)}) %all-gather.5.cloned.1.call-update) | async-done | bytes 21233680 | tf_op jit(solution)/shard_map/all_gather | solution.py:1262
  358.7 141.4 %shard_map.231 = (bf16[256,2304]{1,0:T(8,128)(2,1)}, f32[8,2304]{1,0:T(8,128)}, bf16[3,256,768]{2,1,0:T(8,128)(2,1)}, bf16[1024,768]{1,0:T(8,128)(2,1)}, bf16[10...) custom-call(bf16[1024,2304]{1,0:T(8,128)(2,1)} %get-tuple-element.63., ...), custom_call_target="tpu_custom_call" | custom-call | tf_op jit(solution)/shard_map/pallas_call | solution.py:1117
  500.0 9.4 shard_map.232
  509.5 31.0 %shard_map.233 = (bf16[384,4608]{1,0:T(8,128)(2,1)}, bf16[1024,768]{1,0:T(8,128)(2,1)}, bf16[1024,768]{1,0:T(8,128)(2,1)}) custom-call(bf16[3,256,768]{2,1,0:T(8,128)(2,1)} %get-tuple-element.70.refs_0_, bf16[1024,2304]{1,0:T(8,128)(2,1)} %get-tuple-element.69.refs_1_), custom_call_target="tpu_custom_call" | custom-call | tf_op jit(solution)/shard_map/pallas_call | solution.py:922
  540.5 9.3 shard_map.234
  550.0 19.7 %shard_map.235 = (bf16[1024,2304]{1,0:T(8,128)(2,1)}, bf16[1024,2304]{1,0:T(8,128)(2,1)}) custom-call(bf16[1024,768]{1,0:T(8,128)(2,1)} %get-tuple-element.73.refs_0_, bf16[1024,768]{1,0:T(8,128)(2,1)} %get-tuple-element.74.refs_1_, bf16[1024,768]{1,0:T(8,128)(2,1)} %get-tuple-element.71.refs_0_.refs_2_, bf16[2304,2304]{1,0:T(8,128)(2,1)} %get-tuple-element.75.refs_3_, ...), custom_call_target="tpu_custom_call" | custom-call | tf_op jit(solution)/shard_map/pallas_call | solution.py:1167
  569.6 38.2 %shard_map.236 = bf16[1152,4608]{1,0:T(8,128)(2,1)} custom-call(bf16[1024,2304]{1,0:T(8,128)(2,1)} %get-tuple-element.63.normed_ref.refs_0_, bf16[1024,2304]{1,0:T(8,128)(2,1)} %get-tuple-element.81.refs_1_.refs_0_, bf16[1024,2304]{1,0:T(8,128)(2,1)} %get-tuple-element.80.refs_2_.refs_1_), custom_call_target="tpu_custom_call" | custom-call | tf_op jit(solution)/shard_map/pallas_call | solution.py:922
  607.8 7.9 reduce-scatter.9.cloned.1.call-done
  615.9 2.4 fusion.32.refs_5_
  618.3 100.5 %shard_map.237 = (f32[256,2304]{1,0:T(8,128)}, f32[8,2304]{1,0:T(8,128)}, f32[8,2304]{1,0:T(8,128)}, bf16[1024,2304]{1,0:T(8,128)(2,1)}) custom-call(bf16[1024,2304]{1,0:T(8,128)(2,1)} %get-tuple-element.81.refs_1_.refs_0_, bf16[1024,2304]{1,0:T(8,128)(2,1)} %get-tuple-element.80.refs_2_.refs_1_, ...), custom_call_target="tpu_custom_call" | custom-call | tf_op jit(solution)/shard_map/pallas_call | solution.py:781
  718.8 5.1 fusion.29
  723.9 1.0 dynamic-slice_convert_fusion.3
  724.9 1.0 pad_maximum_fusion.2.do_ref
  726.0 13.4 %shard_map.238 = (f32[1024,512]{1,0:T(8,128)}, bf16[4096,512]{1,0:T(8,128)(2,1)}) custom-call(bf16[1024,512]{1,0:T(8,128)(2,1)} %bitcast.46, bf16[1024,512]{1,0:T(8,128)(2,1)} %pad_maximum_fusion.2.do_ref, f32[1024,512]{1,0:T(8,128)} %get-tuple-element.84.of_ref, f32[4,1,512]{2,1,0:T(1,128)} %get-tuple-element.85.lse_ref, ...), custom_call_target="tpu_custom_call" | custom-call | tf_op jit(solution)/shard_map/pallas_call | solution.py:505
  739.3 3.1 broadcast_multiply_fusion
  742.5 2.7 mul.173
  745.2 1.4 subtract_convert_fusion
  746.7 1.1 pad_maximum_fusion.3
  747.8 1.2 copy.46
  749.0 1.0 pad_maximum_fusion.4.refs_1_
  750.1 8.9 shard_map.239
  759.0 9.0 shard_map.240.refs_2_
  768.0 30.4 %reduce-scatter.11.cloned.1.call-done = bf16[288,4608]{1,0:T(8,128)(2,1)} async-done(((bf16[1152,4608]{1,0:T(8,128)(2,1)}), bf16[288,4608]{1,0:T(8,128)(2,1)}) %reduce-scatter.11.cloned.1.call-update) | async-done | bytes 2654224 | tf_op jit(solution)/shard_map/reduce_scatter | solution.py:1336
  798.5 1.1 copy-done.11
  799.7 1.7 convert_bitcast_fusion
  801.4 1.0 copy-done.1
  802.4 2.8 slice_convert_fusion
  805.2 73.3 %reduce-scatter.13.cloned.1.call-done = bf16[1024,512]{1,0:T(8,128)(2,1)} async-done(((bf16[4096,512]{1,0:T(8,128)(2,1)}), bf16[1024,512]{1,0:T(8,128)(2,1)}) %reduce-scatter.13.cloned.1.call-update) | async-done | bytes 1048592 | tf_op jit(solution)/shard_map/reduce_scatter | solution.py:1336
  878.4 1.5 convert_element_type.47
  879.9 2.6 fusion.15
  882.6 1.1 pad_maximum_fusion.5.refs_1_
  883.7 9.0 shard_map.241
  892.7 50.4 %shard_map.242 = (bf16[256,2304]{1,0:T(8,128)(2,1)}, f32[8,2304]{1,0:T(8,128)}) custom-call(bf16[1024,512]{1,0:T(8,128)(2,1)} %bitcast.39, bf16[1024,512]{1,0:T(8,128)(2,1)} %pad_maximum_fusion.5.refs_1_, bf16[2304,1024]{1,0:T(8,128)(2,1)} %get-tuple-element.93.refs_2_, bf16[256,2304]{1,0:T(8,128)(2,1)} %dynamic-slice_bitcast_fusion.refs_2_.refs_3_, ...), custom_call_target="tpu_custom_call" | custom-call | tf_op jit(solution)/shard_map/pallas_call | solution.py:781
  943.4 1.0 copy-done.4
  945.1 1.5 copy.43
  947.8 0.7 slice.118.kv_ref
  948.5 18.4 %shard_map.243 = (f32[8,384]{1,0:T(8,128)}, f32[288,1024]{1,0:T(8,128)}, f32[288,1024]{1,0:T(8,128)}) custom-call(f32[8,8,384]{2,1,0:T(8,128)} %pad.13.x_ref, bf16[288,512]{1,0:T(8,128)(2,1)} %slice.118.kv_ref), custom_call_target="tpu_custom_call" | custom-call | tf_op jit(solution)/shard_map/pallas_call | solution.py:140
  966.9 1.5 slice_reduce_fusion.1
  968.4 0.9 slice_convert_fusion.4
  969.3 4.8 reduce-scatter.17.cloned.1.call-done
  974.1 1.8 convert_bitcast_fusion.1
  975.9 1.0 copy.53
  977.0 1.0 copy.54
  978.0 1.0 copy.55
  (85 shorter events, 8.4 us)
Async XLA Ops:
  7.2 163.1 %all-gather.3.cloned.1.call-start = ((), (), s32[]{:S(2)}) async-start(), calls=%async_computation.6 | async-start | bytes 5242880 | tf_op jit(solution)/shard_map/all_gather | solution.py:1284
  10.3 0.6 copy-start.18
  89.2 1.7 copy-start.3
  90.3 268.4 %all-gather.5.cloned.1.call-start = ((), (), s32[]{:S(2)}) async-start(), calls=%async_computation.7 | async-start | bytes 23887872 | tf_op jit(solution)/shard_map/all_gather | solution.py:1262
  170.3 379.6 %reduce-scatter.7.cloned.1.call-start = ((), (), s32[]{:S(2)}) async-start(), calls=%async_computation.8 | async-start | bytes 2211840 | tf_op jit(solution)/shard_map/reduce_scatter | solution.py:1336
  176.8 2.4 copy-start.19
  509.4 106.3 %reduce-scatter.9.cloned.1.call-start = ((), (), s32[]{:S(2)}) async-start(), calls=%async_computation.9 | async-start | bytes 4423680 | tf_op jit(solution)/shard_map/reduce_scatter | solution.py:1336
  549.9 248.5 %reduce-scatter.11.cloned.1.call-start = ((), (), s32[]{:S(2)}) async-start(), calls=%async_computation.10 | async-start | bytes 13271040 | tf_op jit(solution)/shard_map/reduce_scatter | solution.py:1336
  615.7 262.7 %reduce-scatter.13.cloned.1.call-start = ((), (), s32[]{:S(2)}) async-start(), calls=%async_computation.11 | async-start | bytes 5242880 | tf_op jit(solution)/shard_map/reduce_scatter | solution.py:1336
  618.3 100.5 %copy-start.2 = (bf16[2304,512]{1,0:T(8,128)(2,1)S(1)}, bf16[2304,512]{1,0:T(8,128)(2,1)}, u32[]{:S(2)}) copy-start(bf16[2304,512]{1,0:T(8,128)(2,1)} %get-tuple-element.61.refs_1_) | copy-start | bytes 7077892
  718.8 5.1 copy-start
  746.6 2.4 copy-start.8
  746.7 2.4 copy-start.9
  746.7 2.4 copy-start.10
  798.4 1.2 copy-start.11
  798.4 1.3 copy-start.13
  798.5 144.7 %reduce-scatter.15.cloned.1.call-start = ((), (), s32[]{:S(2)}) async-start(), calls=%async_computation.12 | async-start | bytes 2949120 | tf_op jit(solution)/shard_map/reduce_scatter | solution.py:1336
  799.7 2.7 copy-start.1
  892.7 81.4 %reduce-scatter.17.cloned.1.call-start = ((), (), s32[]{:S(2)}) async-start(), calls=%async_computation.13 | async-start | bytes 1474560 | tf_op jit(solution)/shard_map/reduce_scatter | solution.py:1336
  892.7 50.5 %copy-start.14 = (f32[8,2304]{1,0:T(8,128)S(1)}, f32[8,2304]{1,0:T(8,128)}, u32[]{:S(2)}) copy-start(f32[8,2304]{1,0:T(8,128)} %get-tuple-element.99) | copy-start | bytes 221188
  943.1 1.3 copy-start.4
  945.0 1.7 copy-start.16
  945.0 1.8 copy-start.15
  945.0 1.9 copy-start.17
  945.0 2.7 copy-start.12
  946.7 29.3 %copy-start.5 = (bf16[256,2304]{1,0:T(8,128)(2,1)S(1)}, bf16[256,2304]{1,0:T(8,128)(2,1)}, u32[]{:S(2)}) copy-start(bf16[256,2304]{1,0:T(8,128)(2,1)} %get-tuple-element.95) | copy-start | bytes 3538948
  966.9 10.0 %copy-start.7 = (f32[288,1024]{1,0:T(8,128)S(1)}, f32[288,1024]{1,0:T(8,128)}, u32[]{:S(2)}) copy-start(f32[288,1024]{1,0:T(8,128)} %get-tuple-element.169) | copy-start | bytes 3538948
  975.9 2.0 copy-start.6
Sparse Core Ops, SparseCore 0:
  90.4 79.8 all-gather.2
  172.5 186.1 all-gather.4
  509.5 37.6 reduce-scatter.6
  550.0 65.5 reduce-scatter.8
  618.0 180.3 reduce-scatter.10
  800.6 77.7 reduce-scatter.12
  892.8 48.5 reduce-scatter.14
  943.8 30.2 reduce-scatter.16

commit v6 on v5

--- a/solution.py
+++ b/solution.py
@@ -238,15 +238,14 @@
     return -(-widest // LANES) * LANES
 
 
-def front_kernel(plan, tokens_ref, wq_ref, wk_ref, wv_ref, wo_ref, gains_ref, *refs):
+def front_kernel(plan, tokens_ref, wq_ref, wk_ref, wv_ref, gains_ref, frequency_ref, *refs):
     dp_size, seq_size, heads, pieces, row_step = plan
-    gain_rows, qkv_ref, normed_ref, w_qkv_ref, w_out_ref = refs[:5]
-    tokens, normed, w_qkv, w_out, gains, refs = *refs[5:10], refs[10:]
+    gain_rows, pair_ref, cosine_ref, sine_ref, normed_ref, w_qkv_ref = refs[:6]
+    tokens, normed, w_qkv, gains, refs = *refs[6:10], refs[10:]
     load_sem, gain_sem, line_sem, pair_sem, store_sem = refs
     count = dp_size * seq_size
     span, width = tokens.shape
     shard, q_width = wq_ref.shape
-    columns = w_qkv.shape[1]
     dp, seq, mp = lax.axis_index("dp"), lax.axis_index("seq"), lax.axis_index("mp")
     rank = dp * seq_size + seq
 
@@ -262,8 +261,7 @@
         pltpu.make_async_copy(
             wv_ref.at[:, head], w_qkv.at[own, pl.ds(q_width + HEAD_DIM, HEAD_DIM)], load_sem.at[2]
         ),
-        pltpu.make_async_copy(wo_ref, w_out.at[own], load_sem.at[3]),
-        pltpu.make_async_copy(tokens_ref, tokens, load_sem.at[4]),
+        pltpu.make_async_copy(tokens_ref, tokens, load_sem.at[3]),
     ]
     for load in loads:
         load.start()
@@ -273,20 +271,22 @@
     pl.semaphore_wait(barrier, count - 1)
 
     def block(t, at):
+        piece = shard // pieces
         first = (dp * seq_size + at) * shard
-        if t == pieces:
-            return w_out.at[pl.ds(pl.multiple_of(first, 16), shard)]
-        piece = shard // pieces
         return w_qkv.at[pl.ds(pl.multiple_of(first + t * piece, 16), piece)]
 
     start, share, arrival, complete, drain = travel(block, line_sem, pair_sem, seq_size)
-    for load in loads[:4]:
+    for load in loads[:3]:
         load.wait()
     gain_copies = [remote_copy(gains_ref, gains.at[rank], gain_sem, (k,), peer(k)) for k in range(1, count)]
     for t in range(pieces):
         start(t)
     for t in range(pieces):
         share(t)
+    position = seq * span + lax.broadcasted_iota(jnp.int32, cosine_ref.shape, 0)
+    angle = position.astype(F32) * frequency_ref[0:1, :]
+    cosine_ref[...] = jnp.cos(angle)
+    sine_ref[...] = jnp.sin(angle)
     gains[pl.ds(rank, 1)] = gains_ref[...][None]
     gain_rows[...] = jnp.zeros_like(gain_rows)
     for copy in gain_copies:
@@ -294,7 +294,7 @@
     for r in range(count):
         first = window(r, shard)
         gain_rows[:, first : first + gains.shape[2]] += gains[r]
-    loads[4].wait()
+    loads[3].wait()
 
     def norm_rows(r, carry):
         rows = pl.ds(pl.multiple_of(r * row_step, row_step), row_step)
@@ -307,9 +307,6 @@
         lax.fori_loop(blocks * t // pieces, blocks * (t + 1) // pieces, norm_rows, 0)
         arrival(t, 1)
     for distance in range(2, seq_size):
-        if distance == seq_size - 1:
-            start(pieces)
-            share(pieces)
         for t in range(pieces):
             arrival(t, distance)
     for t in range(pieces):
@@ -317,64 +314,111 @@
     stores = [
         pltpu.make_async_copy(w_qkv, w_qkv_ref, store_sem.at[0]),
         pltpu.make_async_copy(normed, normed_ref, store_sem.at[1]),
-        pltpu.make_async_copy(w_out, w_out_ref, store_sem.at[2]),
     ]
-    stores[0].start()
-    stores[1].start()
-    tiles = columns // HEAD_DIM
-    for i in range(max(tiles, seq_size - 1)):
-        if i < tiles:
-            part = slice(i * HEAD_DIM, (i + 1) * HEAD_DIM)
-            qkv_ref[:, part] = dot_nn(normed[...], w_qkv[:, part])
-        if i < seq_size - 1:
-            arrival(pieces, i + 1)
-    complete(pieces)
-    stores[2].start()
+    for store in stores:
+        store.start()
+
+    def project(first):
+        return dot_nn(normed[...], w_qkv[:, first : first + HEAD_DIM])
+
+    key = rotary(project(q_width), cosine_ref[...], sine_ref[...], 1.0)
+    pair_ref[:, :HEAD_DIM] = key.astype(BF16)
+    pair_ref[:, HEAD_DIM:] = project(q_width + HEAD_DIM).astype(BF16)
     for store in stores:
         store.wait()
-    for t in range(pieces + 1):
+    for t in range(pieces):
         drain(t)
 
 
-def front(tokens, w_query, w_key, w_value, w_out_t, gains, heads, sizes):
+def front(tokens, w_query, w_key, w_value, gains, heads, sizes):
     dp_size, seq_size, _ = sizes
     count = dp_size * seq_size
     span, width = tokens.shape
     shard, q_width = w_query.shape
     columns = q_width + 2 * HEAD_DIM
+    half_dim = HEAD_DIM // 2
     pieces = 3
     lanes = window_width(count, shard)
     offset = (lax.axis_index("dp") * seq_size + lax.axis_index("seq")) * shard % LANES
     block = jnp.pad(jnp.stack([gain.astype(F32) for gain in gains]), ((0, 8 - len(gains)), (0, 0)))
     block = lax.dynamic_update_slice_in_dim(jnp.zeros((8, lanes), F32), block, offset, 1)
+    frequency = ROPE_BASE ** (-jnp.arange(half_dim, dtype=F32) * 2.0 / HEAD_DIM)
+    frequency = jnp.broadcast_to(frequency, (8, half_dim))
     plan = (dp_size, seq_size, heads, pieces, min(32, span))
     return pl.pallas_call(
         functools.partial(front_kernel, plan),
         out_shape=(
             jax.ShapeDtypeStruct((8, max(width, window(count - 1, shard) + lanes)), F32),
-            jax.ShapeDtypeStruct((span, columns), F32),
+            jax.ShapeDtypeStruct((span, 2 * HEAD_DIM), BF16),
+            jax.ShapeDtypeStruct((span, half_dim), F32),
+            jax.ShapeDtypeStruct((span, half_dim), F32),
             jax.ShapeDtypeStruct((span, width), BF16),
             jax.ShapeDtypeStruct((width, columns), BF16),
-            jax.ShapeDtypeStruct((width, q_width), BF16),
         ),
-        in_specs=[pl.BlockSpec(memory_space=pl.ANY)] * 5 + [pl.BlockSpec(memory_space=pltpu.VMEM)],
-        out_specs=(pl.BlockSpec(memory_space=pltpu.VMEM),) * 2 + (pl.BlockSpec(memory_space=pl.ANY),) * 3,
+        in_specs=[pl.BlockSpec(memory_space=pl.ANY)] * 4 + [pl.BlockSpec(memory_space=pltpu.VMEM)] * 2,
+        out_specs=(pl.BlockSpec(memory_space=pltpu.VMEM),) * 4 + (pl.BlockSpec(memory_space=pl.ANY),) * 2,
         scratch_shapes=[
             pltpu.VMEM((span, width), BF16),
             pltpu.VMEM((span, width), BF16),
             pltpu.VMEM((width, columns), BF16),
-            pltpu.VMEM((width, q_width), BF16),
             pltpu.VMEM((count, 8, lanes), F32),
-            pltpu.SemaphoreType.DMA((5,)),
+            pltpu.SemaphoreType.DMA((4,)),
             pltpu.SemaphoreType.DMA((2, count)),
-            pltpu.SemaphoreType.DMA((2, pieces + 1, 2, seq_size)),
-            pltpu.SemaphoreType.DMA((2, pieces + 1, 2, seq_size)),
-            pltpu.SemaphoreType.DMA((3,)),
+            pltpu.SemaphoreType.DMA((2, pieces, 2, seq_size)),
+            pltpu.SemaphoreType.DMA((2, pieces, 2, seq_size)),
+            pltpu.SemaphoreType.DMA((2,)),
         ],
         compiler_params=pltpu.CompilerParams(
             collective_id=1, has_side_effects=True, vmem_limit_bytes=VMEM_LIMIT
         ),
-    )(tokens, w_query, w_key, w_value, w_out_t, block)
+    )(tokens, w_query, w_key, w_value, block, frequency)
+
+
+def carry_kernel(seq_size, shard_ref, full_ref, load_sem, line_sem, pair_sem):
+    dp, seq, mp = lax.axis_index("dp"), lax.axis_index("seq"), lax.axis_index("mp")
+    far = seq_size - 1
+    shard = shard_ref.shape[0]
+
+    def block(t, at):
+        first = pl.multiple_of((dp * seq_size + at) * shard, 16)
+        return full_ref.at[pl.ds(first, shard)]
+
+    load = pltpu.make_async_copy(shard_ref, block(0, seq), load_sem)
+    load.start()
+    barrier = pltpu.get_barrier_semaphore()
+    pl.semaphore_signal(barrier, inc=1, device_id=(1 - dp, seq, mp), device_id_type=MESH)
+    for way in range(2):
+        @pl.when(seq < far if way == 0 else seq > 0)
+        def _(way=way):
+            pl.semaphore_signal(
+                barrier, inc=1, device_id=(dp, seq + 1 - 2 * way, mp), device_id_type=MESH
+            )
+
+    pl.semaphore_wait(barrier, 1 + (seq + far) // seq_size + (2 * far - seq) // seq_size)
+    load.wait()
+    start, share, arrival, complete, drain = travel(block, line_sem, pair_sem, seq_size)
+    start(0)
+    share(0)
+    for distance in range(1, seq_size):
+        arrival(0, distance)
+    complete(0)
+    drain(0)
+
+
+def carry(shard, sizes, collective_id):
+    dp_size, seq_size, _ = sizes
+    return pl.pallas_call(
+        functools.partial(carry_kernel, seq_size),
+        out_shape=jax.ShapeDtypeStruct((shard.shape[0] * dp_size * seq_size, shard.shape[1]), BF16),
+        in_specs=[pl.BlockSpec(memory_space=pl.ANY)],
+        out_specs=pl.BlockSpec(memory_space=pl.ANY),
+        scratch_shapes=[
+            pltpu.SemaphoreType.DMA,
+            pltpu.SemaphoreType.DMA((2, 1, 2, seq_size)),
+            pltpu.SemaphoreType.DMA((2, 1, 2, seq_size)),
+        ],
+        compiler_params=pltpu.CompilerParams(collective_id=collective_id, has_side_effects=True),
+    )(shard)
 
 
 def key_mask(shape, first_key, first_query, tile, far):
@@ -548,7 +592,7 @@
     return copies
 
 
-def sum_square(ready, parts_at, steps, step, peer, total, kept, sent, arrived, sems, eager):
+def sum_square(ready, parts_at, steps, step, peer, total, kept, sent, arrived, sems):
     half = step // 2
     copies, second = [], []
 
@@ -563,8 +607,6 @@
     for t in range(steps):
         first = t * step
         ready(t)
-        if eager and t:
-            second_hop(t - 1)
         far = parts_at(t, 3)
         sent[t, 0, 1] = far[:, :half].astype(BF16)
         sent[t, 1, 1] = far[:, half:].astype(BF16)
@@ -581,7 +623,7 @@
             remote_copy(sent.at[t, 1, pl.ds(0, 2)], arrived.at[t, 1, pl.ds(0, 2)], sems, (t, 1), peer(2))
         )
         total[:, first : first + step] = parts_at(t, 0)
-    for t in range(steps - 1 if eager else 0, steps):
+    for t in range(steps):
         second_hop(t)
     for t in range(steps):
         first = t * step
@@ -703,7 +745,7 @@
     )
 
 
-def finish_rows(ready, parts_at, sizes, rows, peer, buffers, sems, eager=False):
+def finish_rows(ready, parts_at, sizes, rows, peer, buffers, sems):
     mp_size, share, step, row_step = sizes
     rows_fn, aux, outs, gathered = rows
     total, own, kept, sent, arrived = buffers
@@ -711,7 +753,7 @@
     steps = total.shape[1] // step
     if mp_size == 4:
         sums = sum_square(
-            ready, parts_at, steps, step, peer, total, kept, sent, arrived, sum_sem, eager
+            ready, parts_at, steps, step, peer, total, kept, sent, arrived, sum_sem
         )
     else:
         sums = sum_direct(
@@ -764,7 +806,7 @@
         pltpu.SemaphoreType.DMA((2, steps, max(4, mp_size - 1))),
         pltpu.SemaphoreType.DMA((2, max(6, mp_size))),
     ]
-    return step, min(32, share), buffers, sems
+    return step, min(64, share), buffers, sems
 
 
 def sum_rows(lefts, weight, rows_fn, aux, outs, gather, natural, mp_size, collective_id):
@@ -1092,7 +1134,6 @@
         peer,
         buffers,
         (sum_sem, row_sem, local_sem.at[0]),
-        eager=True,
     )
     own_store = pltpu.make_async_copy(buffers[1], own_ref, local_sem.at[0])
     own_store.start()
@@ -1262,32 +1303,24 @@
         return lax.all_gather(x, both, axis=0, tiled=True)
 
     sizes = (dp_size, seq_size, mp_size)
-    gain_rows, qkv, normed_one, w_qkv, w_out_t = front(
+    gain_rows, own_pair, cosine, sine, normed_one, w_qkv = front(
         tokens[0],
         w_query,
         w_key,
         w_value,
-        w_out.T,
         [pre_attn_gain, post_attn_gain, pre_ffw_gain, post_ffw_gain],
         heads,
         sizes,
     )
     gain_one, gain_two, gain_three, gain_four = (gain_rows[i : i + 1, :width] for i in range(4))
-    positions = seq * span + jnp.arange(span, dtype=jnp.int32)
-    half_dim = HEAD_DIM // 2
-    frequency = ROPE_BASE ** (-jnp.arange(half_dim, dtype=F32) * 2.0 / HEAD_DIM)
-    angles = positions.astype(F32)[:, None, None] * frequency
-    cosine = jnp.cos(angles)
-    sine = jnp.sin(angles)
-    keys_own = rotary(qkv[:, q_width : q_width + HEAD_DIM], cosine[:, 0], sine[:, 0], 1.0)
-    own_pair = jnp.concatenate([keys_own, qkv[:, q_width + HEAD_DIM :]], axis=1).astype(BF16)
     pairs = lax.all_gather(own_pair, "seq", axis=0, tiled=True)
-    query_lin = qkv[:, :q_width].reshape(span, heads, HEAD_DIM)
-    queries = (rotary(query_lin, cosine, sine, 1.0) * HEAD_DIM ** (-0.5)).astype(BF16)
-    queries = queries.reshape(span, q_width)
+    w_out_t = carry(after(w_out.T, own_pair), sizes, 30)
+    query_lin = dot_nn(after(normed_one, pairs), w_qkv[:, :q_width]).reshape(span, heads, HEAD_DIM)
+    queries = rotary(query_lin, cosine[:, None], sine[:, None], 1.0) * HEAD_DIM ** (-0.5)
+    queries = queries.astype(BF16).reshape(span, q_width)
 
     units = w_gate.shape[1]
-    gate_up_w = gather_weight(after(jnp.concatenate([w_gate, w_up], axis=1), pairs))
+    gate_up_w = gather_weight(after(jnp.concatenate([w_gate, w_up], axis=1), pairs, w_out_t))
 
     attn_o, attn_exact, lse = attend(queries, pairs, plan)
     own_first = mp * share
@@ -1378,7 +1411,7 @@
     grad_out_sum = weight_grad(dattn_low, (by_owner(attn_o),), 9)
     dquery = dquery.reshape(span, heads, HEAD_DIM)
     dquery_low = (
-        rotary(dquery * HEAD_DIM ** (-0.5), cosine, sine, -1.0).reshape(span, q_width).astype(BF16)
+        rotary(dquery * HEAD_DIM ** (-0.5), cosine[:, None], sine[:, None], -1.0).reshape(span, q_width).astype(BF16)
     )
     grad_q_sum = weight_grad(normed_one, (dquery_low,), 10, columns=2 * HEAD_DIM)
     own_grads = spread(after(dpairs, grad_gate_up, grad_out_sum, grad_q_sum)).astype(F32)
@@ -1386,7 +1419,7 @@
     grad_up = grad_gate_up[:, units:].astype(F32)
     own_grads = after(own_grads, grad_gate, grad_up, grad_down)
     dkey_rot = own_grads[:, :HEAD_DIM]
-    dkey_low = rotary(dkey_rot, cosine[:, 0], sine[:, 0], -1.0).astype(BF16)
+    dkey_low = rotary(dkey_rot, cosine, sine, -1.0).astype(BF16)
     dvalue_low = own_grads[:, HEAD_DIM:].astype(BF16)
     dkv_low = jnp.concatenate([dkey_low, dvalue_low], axis=1)
     grad_qkv_sum = weight_grad(normed_one, (dkv_low,), 11, into=grad_q_sum)

time: 996 us -> 979 us (0.983)
  waiting for transfers between devices: 261 us -> 196 us
  Pallas kernels: 629 us -> 684 us
    pallas_call x0 -> x1, Pallas kernels: none -> 79.2 us  [carry(): pl.pallas_call(functools.partial(carry_kernel, seq_size), out_shape=jax.S...]
    all_gather x1, waiting for transfers between devices: 76.4 us -> 12 us  [shards(): pairs = lax.all_gather(own_pair, 'seq', axis=0, tiled=True)]
    pallas_call x1, Pallas kernels: 73.2 us -> 53.6 us  [front(): pl.pallas_call(functools.partial(front_kernel, plan), out_shape=(jax.Shap...]
  transfers between devices with their start and end apart: 8 -> 8, of which waited for: 6 -> 6; matrix products, arithmetic and copies ran while one was open for 6% -> 6% of each run, Pallas kernels for 40% -> 49%
where the time goes in v6:
time: 979 us; the launch traced here: 970 us
  Pallas kernels  684 us (70%)
  waiting for transfers between devices  196 us (20%)
  local copies, waits for them, and re-layouts  41.2 us (4%)
  other arithmetic  21.8 us (2%)
  between operations  15.1 us (2%)
  matrix products  11 us (1%)
    pallas_call x3, Pallas kernels, sum_rows(): pl.pallas_call(functools.partial(rows_kernel, plan, rows_fn), out_shape=o...  238 us
    pallas_call x1, Pallas kernels, ffw(): pl.pallas_call(functools.partial(ffw_kernel, plan), out_shape=(jax.ShapeD...  139 us
    reduce_scatter x6, waiting for transfers between devices, spread(): return lax.psum_scatter(x, 'seq', scatter_dimension=0, tiled=True)  118 us
    pallas_call x7, Pallas kernels, weight_grad(): pl.pallas_call(functools.partial(weight_grad_kernel, plan), out_shape=out...  115 us
    pallas_call x1, Pallas kernels, carry(): pl.pallas_call(functools.partial(carry_kernel, seq_size), out_shape=jax.S...  79.2 us
    all_gather x1, waiting for transfers between devices, gather_weight(): return lax.all_gather(x, both, axis=0, tiled=True)  65.1 us
    pallas_call x1, Pallas kernels, front(): pl.pallas_call(functools.partial(front_kernel, plan), out_shape=(jax.Shap...  53.6 us
    pallas_call x1, Pallas kernels, hidden_back(): pl.pallas_call(functools.partial(hidden_back_kernel, len(dmixed)), grid=(...  20.2 us
  transfers between devices with their start and end apart: 8, of which 6 were waited for; matrix products, arithmetic and copies ran while one was open for 6% of the time, Pallas kernels for 49%

profile of v6, /device:TPU:0, one launch (start us, length us, event | category | flops | bytes accessed | tf_op | source)
XLA Modules:
  0.0 969.7 jit_solution(5796387944262680466)
XLA Ops:
  7.3 0.7 stack.35
  8.6 0.7 stack.37
  9.3 0.7 stack.38
  10.9 53.6 %shard_map.228 = (f32[8,2304]{1,0:T(8,128)}, bf16[1024,512]{1,0:T(8,128)(2,1)}, f32[1024,128]{1,0:T(8,128)}, f32[1024,128]{1,0:T(8,128)}, bf16[1024,2304]{1,0:T(8,128)(2,1)}, /*index=5*/bf16[2304,1024]{1,0:T(8,128)(2,1)}) custom-call(bf16[1024,2304]{1,0:T(8,128)(2,1)} %bitcast.42, bf16[288,512]{1,0:T(8,128)(2,1)} %wq_ref.1, bf16[288,1024]{1,0:T(8,128)(2,1)} %wk_ref.1, ...), custom_call_target="tpu_custom_call" | custom-call | tf_op jit(solution)/shard_map/pallas_call | solution.py:348
  64.6 79.2 %shard_map.230.refs_1_ = bf16[2304,512]{1,0:T(8,128)(2,1)} custom-call(bf16[288,512]{1,0:T(8,128)(2,1)} %bitcast.54), custom_call_target="tpu_custom_call" | custom-call | tf_op jit(solution)/shard_map/pallas_call | solution.py:410
  143.9 1.7 pad_maximum_fusion
  145.6 12.0 %all-gather.3.cloned.1.call-done.kv_ref = bf16[4096,512]{1,0:T(8,128)(2,1)} async-done(((bf16[1024,512]{1,0:T(8,128)(2,1)}), bf16[4096,512]{1,0:T(8,128)(2,1)}) %all-gather.3.cloned.1.call-update) | async-done | bytes 4194320 | tf_op jit(solution)/shard_map/all_gather | solution.py:1316
  159.1 1.3 constant_dynamic-slice_fusion.4
  161.2 1.5 copy.41.cotangent_ref
  162.7 2.4 dynamic-slice_bitcast_fusion.refs_2_.refs_3_
  165.0 6.0 fusion
  171.0 1.1 fusion.11
  172.7 1.6 copy.49
  174.3 1.1 multiply_subtract_fusion
  175.5 1.1 fusion.2
  176.6 1.2 copy.51
  177.8 8.1 shard_map.229
  185.9 88.4 %shard_map.231 = (f32[256,2304]{1,0:T(8,128)}, f32[256,2304]{1,0:T(8,128)}, bf16[1024,2304]{1,0:T(8,128)(2,1)}) custom-call(bf16[1024,512]{1,0:T(8,128)(2,1)} %get-tuple-element.68.refs_0_, bf16[2304,512]{1,0:T(8,128)(2,1)} %shard_map.230.refs_1_, bf16[256,2304]{1,0:T(8,128)(2,1)} %dynamic-slice_bitcast_fusion.refs_2_.refs_3_, ...), custom_call_target="tpu_custom_call" | custom-call | tf_op jit(solution)/shard_map/pallas_call | solution.py:823
  274.3 3.1 copy.35
  277.4 1.9 copy.36
  279.2 2.0 copy.40.resid_ref
  281.2 65.1 %all-gather.5.cloned.1.call-done.gate_up_ref.refs_2_ = bf16[2304,4608]{1,0:T(8,128)(2,1)} async-done(((bf16[288,4608]{1,0:T(8,128)(2,1)}), bf16[2304,4608]{1,0:T(8,128)(2,1)}) %all-gather.5.cloned.1.call-update) | async-done | bytes 21233680 | tf_op jit(solution)/shard_map/all_gather | solution.py:1303
  346.3 139.0 %shard_map.232 = (bf16[256,2304]{1,0:T(8,128)(2,1)}, f32[8,2304]{1,0:T(8,128)}, bf16[3,256,768]{2,1,0:T(8,128)(2,1)}, bf16[1024,768]{1,0:T(8,128)(2,1)}, bf16[10...) custom-call(bf16[1024,2304]{1,0:T(8,128)(2,1)} %get-tuple-element.71., ...), custom_call_target="tpu_custom_call" | custom-call | tf_op jit(solution)/shard_map/pallas_call | solution.py:1158
  485.3 9.5 shard_map.233
  494.9 30.7 %shard_map.234 = (bf16[384,4608]{1,0:T(8,128)(2,1)}, bf16[1024,768]{1,0:T(8,128)(2,1)}, bf16[1024,768]{1,0:T(8,128)(2,1)}) custom-call(bf16[3,256,768]{2,1,0:T(8,128)(2,1)} %get-tuple-element.78.refs_0_, bf16[1024,2304]{1,0:T(8,128)(2,1)} %get-tuple-element.77.refs_1_), custom_call_target="tpu_custom_call" | custom-call | tf_op jit(solution)/shard_map/pallas_call | solution.py:964
  525.6 9.4 shard_map.235
  535.1 20.2 %shard_map.236 = (bf16[1024,2304]{1,0:T(8,128)(2,1)}, bf16[1024,2304]{1,0:T(8,128)(2,1)}) custom-call(bf16[1024,768]{1,0:T(8,128)(2,1)} %get-tuple-element.81.refs_0_, bf16[1024,768]{1,0:T(8,128)(2,1)} %get-tuple-element.82.refs_1_, bf16[1024,768]{1,0:T(8,128)(2,1)} %get-tuple-element.79.refs_0_.refs_2_, bf16[2304,2304]{1,0:T(8,128)(2,1)} %get-tuple-element.83.refs_3_, ...), custom_call_target="tpu_custom_call" | custom-call | tf_op jit(solution)/shard_map/pallas_call | solution.py:1208
  555.3 38.3 %shard_map.237 = bf16[1152,4608]{1,0:T(8,128)(2,1)} custom-call(bf16[1024,2304]{1,0:T(8,128)(2,1)} %get-tuple-element.71.normed_ref.refs_0_, bf16[1024,2304]{1,0:T(8,128)(2,1)} %get-tuple-element.89.refs_1_.refs_0_, bf16[1024,2304]{1,0:T(8,128)(2,1)} %get-tuple-element.88.refs_2_.refs_1_), custom_call_target="tpu_custom_call" | custom-call | tf_op jit(solution)/shard_map/pallas_call | solution.py:964
  593.6 8.0 reduce-scatter.9.cloned.1.call-done
  601.9 2.4 fusion.18.refs_5_
  604.2 100.1 %shard_map.238 = (f32[256,2304]{1,0:T(8,128)}, f32[8,2304]{1,0:T(8,128)}, f32[8,2304]{1,0:T(8,128)}, bf16[1024,2304]{1,0:T(8,128)(2,1)}) custom-call(bf16[1024,2304]{1,0:T(8,128)(2,1)} %get-tuple-element.89.refs_1_.refs_0_, bf16[1024,2304]{1,0:T(8,128)(2,1)} %get-tuple-element.88.refs_2_.refs_1_, ...), custom_call_target="tpu_custom_call" | custom-call | tf_op jit(solution)/shard_map/pallas_call | solution.py:823
  704.4 5.1 fusion.14
  709.5 1.0 dynamic-slice_convert_fusion.3
  710.4 1.0 pad_maximum_fusion.1.do_ref
  711.5 13.4 %shard_map.239 = (f32[1024,512]{1,0:T(8,128)}, bf16[4096,512]{1,0:T(8,128)(2,1)}) custom-call(bf16[1024,512]{1,0:T(8,128)(2,1)} %bitcast.48, bf16[1024,512]{1,0:T(8,128)(2,1)} %pad_maximum_fusion.1.do_ref, f32[1024,512]{1,0:T(8,128)} %get-tuple-element.92.of_ref, f32[4,1,512]{2,1,0:T(1,128)} %get-tuple-element.93.lse_ref, ...), custom_call_target="tpu_custom_call" | custom-call | tf_op jit(solution)/shard_map/pallas_call | solution.py:549
  724.9 3.1 broadcast_multiply_fusion
  728.0 2.7 mul.126
  730.7 1.4 subtract_convert_fusion
  732.2 1.1 pad_maximum_fusion.2
  733.3 1.2 copy.52
  734.5 8.9 shard_map.241.refs_2_
  743.5 1.0 pad_maximum_fusion.3.refs_1_
  744.5 8.9 shard_map.240
  753.4 30.9 %reduce-scatter.11.cloned.1.call-done = bf16[288,4608]{1,0:T(8,128)(2,1)} async-done(((bf16[1152,4608]{1,0:T(8,128)(2,1)}), bf16[288,4608]{1,0:T(8,128)(2,1)}) %reduce-scatter.11.cloned.1.call-update) | async-done | bytes 2654224 | tf_op jit(solution)/shard_map/reduce_scatter | solution.py:1369
  784.7 0.9 copy-done.14
  785.6 1.7 convert_bitcast_fusion
  787.3 1.0 copy-done.4
  788.3 2.8 slice_convert_fusion
  791.1 73.3 %reduce-scatter.13.cloned.1.call-done = bf16[1024,512]{1,0:T(8,128)(2,1)} async-done(((bf16[4096,512]{1,0:T(8,128)(2,1)}), bf16[1024,512]{1,0:T(8,128)(2,1)}) %reduce-scatter.13.cloned.1.call-update) | async-done | bytes 1048592 | tf_op jit(solution)/shard_map/reduce_scatter | solution.py:1369
  864.4 1.5 convert_element_type.38
  866.1 1.1 pad_maximum_fusion.4.refs_1_
  867.2 9.0 shard_map.242
  876.2 49.3 %shard_map.243 = (bf16[256,2304]{1,0:T(8,128)(2,1)}, f32[8,2304]{1,0:T(8,128)}) custom-call(bf16[1024,512]{1,0:T(8,128)(2,1)} %bitcast.41, bf16[1024,512]{1,0:T(8,128)(2,1)} %pad_maximum_fusion.4.refs_1_, bf16[2304,1024]{1,0:T(8,128)(2,1)} %get-tuple-element.65.refs_2_, bf16[256,2304]{1,0:T(8,128)(2,1)} %dynamic-slice_bitcast_fusion.refs_2_.refs_3_, ...), custom_call_target="tpu_custom_call" | custom-call | tf_op jit(solution)/shard_map/pallas_call | solution.py:823
  925.8 1.0 copy-done.7
  927.5 1.5 copy.47
  930.2 0.7 slice.101.kv_ref
  930.9 18.4 %shard_map.244 = (f32[8,384]{1,0:T(8,128)}, f32[288,1024]{1,0:T(8,128)}, f32[288,1024]{1,0:T(8,128)}) custom-call(f32[8,8,384]{2,1,0:T(8,128)} %pad.13.x_ref, bf16[288,512]{1,0:T(8,128)(2,1)} %slice.101.kv_ref), custom_call_target="tpu_custom_call" | custom-call | tf_op jit(solution)/shard_map/pallas_call | solution.py:140
  949.3 1.5 slice_reduce_fusion.1
  950.8 0.9 slice_convert_fusion.3
  951.7 6.0 reduce-scatter.17.cloned.1.call-done
  957.6 1.8 convert_bitcast_fusion.1
  959.5 1.0 copy.59
  960.5 1.0 copy.60
  961.5 1.0 copy.61
  (91 shorter events, 7.5 us)
Async XLA Ops:
  7.2 150.4 %all-gather.3.cloned.1.call-start = ((), (), s32[]{:S(2)}) async-start(), calls=%async_computation.6 | async-start | bytes 5242880 | tf_op jit(solution)/shard_map/all_gather | solution.py:1316
  10.3 0.6 copy-start.21
  64.5 79.3 %copy-start.5 = (bf16[288,2304]{1,0:T(8,128)(2,1)S(1)}, bf16[288,2304]{1,0:T(8,128)(2,1)}, u32[]{:S(2)}) copy-start(bf16[288,2304]{1,0:T(8,128)(2,1)} %param.23) | copy-start | bytes 3981316
  64.5 79.3 %copy-start.6 = (bf16[288,2304]{1,0:T(8,128)(2,1)S(1)}, bf16[288,2304]{1,0:T(8,128)(2,1)}, u32[]{:S(2)}) copy-start(bf16[288,2304]{1,0:T(8,128)(2,1)} %param.22) | copy-start | bytes 3981316
  64.6 281.7 %all-gather.5.cloned.1.call-start = ((), (), s32[]{:S(2)}) async-start(), calls=%async_computation.7 | async-start | bytes 23887872 | tf_op jit(solution)/shard_map/all_gather | solution.py:1303
  145.6 12.1 %copy-start.22 = (f32[8,2304]{1,0:T(8,128)S(1)}, f32[8,2304]{1,0:T(8,128)}, u32[]{:S(2)}) copy-start(f32[8,2304]{1,0:T(8,128)} %get-tuple-element.70) | copy-start | bytes 221188
  157.6 377.4 %reduce-scatter.7.cloned.1.call-start = ((), (), s32[]{:S(2)}) async-start(), calls=%async_computation.8 | async-start | bytes 2211840 | tf_op jit(solution)/shard_map/reduce_scatter | solution.py:1369
  172.1 2.2 copy-start.1
  172.1 2.2 copy-start.2
  494.8 106.8 %reduce-scatter.9.cloned.1.call-start = ((), (), s32[]{:S(2)}) async-start(), calls=%async_computation.9 | async-start | bytes 4423680 | tf_op jit(solution)/shard_map/reduce_scatter | solution.py:1369
  535.0 249.3 %reduce-scatter.11.cloned.1.call-start = ((), (), s32[]{:S(2)}) async-start(), calls=%async_computation.10 | async-start | bytes 13271040 | tf_op jit(solution)/shard_map/reduce_scatter | solution.py:1369
  601.6 262.7 %reduce-scatter.13.cloned.1.call-start = ((), (), s32[]{:S(2)}) async-start(), calls=%async_computation.11 | async-start | bytes 5242880 | tf_op jit(solution)/shard_map/reduce_scatter | solution.py:1369
  604.2 100.1 %copy-start = (bf16[2304,512]{1,0:T(8,128)(2,1)S(1)}, bf16[2304,512]{1,0:T(8,128)(2,1)}, u32[]{:S(2)}) copy-start(bf16[2304,512]{1,0:T(8,128)(2,1)} %shard_map.230.refs_1_) | copy-start | bytes 7077892
  704.4 5.1 copy-start.3
  734.5 8.9 copy-start.11
  734.5 8.9 copy-start.12
  734.5 8.9 copy-start.13
  784.4 1.2 copy-start.14
  784.4 1.3 copy-start.16
  784.4 141.2 %reduce-scatter.15.cloned.1.call-start = ((), (), s32[]{:S(2)}) async-start(), calls=%async_computation.12 | async-start | bytes 2949120 | tf_op jit(solution)/shard_map/reduce_scatter | solution.py:1369
  785.6 2.7 copy-start.4
  876.2 81.4 %reduce-scatter.17.cloned.1.call-start = ((), (), s32[]{:S(2)}) async-start(), calls=%async_computation.13 | async-start | bytes 1474560 | tf_op jit(solution)/shard_map/reduce_scatter | solution.py:1369
  876.2 49.4 %copy-start.17 = (f32[8,2304]{1,0:T(8,128)S(1)}, f32[8,2304]{1,0:T(8,128)}, u32[]{:S(2)}) copy-start(f32[8,2304]{1,0:T(8,128)} %get-tuple-element.105) | copy-start | bytes 221188
  925.5 1.3 copy-start.7
  927.4 1.7 copy-start.19
  927.4 1.8 copy-start.18
  927.4 1.9 copy-start.20
  927.4 2.7 copy-start.15
  929.1 30.4 %copy-start.8 = (bf16[256,2304]{1,0:T(8,128)(2,1)S(1)}, bf16[256,2304]{1,0:T(8,128)(2,1)}, u32[]{:S(2)}) copy-start(bf16[256,2304]{1,0:T(8,128)(2,1)} %get-tuple-element.101) | copy-start | bytes 3538948
  949.3 11.2 %copy-start.10 = (f32[288,1024]{1,0:T(8,128)S(1)}, f32[288,1024]{1,0:T(8,128)}, u32[]{:S(2)}) copy-start(f32[288,1024]{1,0:T(8,128)} %get-tuple-element.173) | copy-start | bytes 3538948
  959.5 2.0 copy-start.9
Sparse Core Ops, SparseCore 0:
  64.7 92.8 all-gather.2
  159.8 186.4 all-gather.4
  494.9 38.3 reduce-scatter.6
  535.6 65.9 reduce-scatter.8
  603.9 180.3 reduce-scatter.10
  786.5 77.7 reduce-scatter.12
  876.3 48.5 reduce-scatter.14
  927.3 30.2 reduce-scatter.16

commit v7 on v6

--- a/solution.py
+++ b/solution.py
@@ -2,6 +2,7 @@
 
 import jax
 import jax.numpy as jnp
+import numpy as np
 from jax import lax
 from jax.experimental import pallas as pl
 from jax.experimental.pallas import tpu as pltpu
@@ -125,8 +126,8 @@
         piece = (kv_from[k * rows : (k + 1) * rows, :] if k else kv_ref[...]).astype(F32)
         head = flipped(mp, k) * heads // (Q_HEADS // KV_HEADS)
         columns = pl.ds(pl.multiple_of(head * HEAD_DIM, HEAD_DIM), HEAD_DIM)
-        key_ref[:, columns] += piece[:, :HEAD_DIM]
-        value_ref[:, columns] += piece[:, HEAD_DIM:]
+        key_ref[:, columns] = (key_ref[:, columns].astype(F32) + piece[:, :HEAD_DIM]).astype(BF16)
+        value_ref[:, columns] = (value_ref[:, columns].astype(F32) + piece[:, HEAD_DIM:]).astype(BF16)
 
 
 def last_sums(grads, kv, kv_width, heads, sizes):
@@ -136,7 +137,7 @@
     width = -(-local // LANES) * LANES
     block = jnp.transpose(jnp.stack(grads).reshape(len(grads), count, local), (1, 0, 2))
     block = jnp.pad(block, ((0, 0), (0, 8 - len(grads)), (0, width - local)))
-    kv_out = jax.ShapeDtypeStruct((kv.shape[0], kv_width), F32)
+    kv_out = jax.ShapeDtypeStruct((kv.shape[0], kv_width), BF16)
     total, key, value = pl.pallas_call(
         functools.partial(last_kernel, sizes, heads),
         out_shape=(jax.ShapeDtypeStruct((8, width), F32), kv_out, kv_out),
@@ -340,10 +341,11 @@
     pieces = 3
     lanes = window_width(count, shard)
     offset = (lax.axis_index("dp") * seq_size + lax.axis_index("seq")) * shard % LANES
-    block = jnp.pad(jnp.stack([gain.astype(F32) for gain in gains]), ((0, 8 - len(gains)), (0, 0)))
+    block = jnp.concatenate(gains).reshape(len(gains), shard).astype(F32)
+    block = jnp.pad(block, ((0, 8 - len(gains)), (0, 0)))
     block = lax.dynamic_update_slice_in_dim(jnp.zeros((8, lanes), F32), block, offset, 1)
-    frequency = ROPE_BASE ** (-jnp.arange(half_dim, dtype=F32) * 2.0 / HEAD_DIM)
-    frequency = jnp.broadcast_to(frequency, (8, half_dim))
+    frequency = ROPE_BASE ** (-np.arange(half_dim) * 2.0 / HEAD_DIM)
+    frequency = jnp.asarray(np.tile(frequency.astype(np.float32), (8, 1)))
     plan = (dp_size, seq_size, heads, pieces, min(32, span))
     return pl.pallas_call(
         functools.partial(front_kernel, plan),
@@ -1447,6 +1449,8 @@
         heads,
         sizes,
     )
+    grad_key, grad_value = grad_key.astype(F32), grad_value.astype(F32)
+    grad_out_t = after(grad_out_t, grad_key, grad_value)
     return (
         output[None],
         tokens_grad[None],

time: 979 us -> 977 us (level)
  no operation moved by 1% of the time
where the time goes in v7:
time: 977 us; the launch traced here: 968 us
  Pallas kernels  684 us (70%)
  waiting for transfers between devices  193 us (20%)
  local copies, waits for them, and re-layouts  38.5 us (4%)
  other arithmetic  25.2 us (3%)
  between operations  15.1 us (2%)
  matrix products  11 us (1%)
    pallas_call x3, Pallas kernels, sum_rows(): pl.pallas_call(functools.partial(rows_kernel, plan, rows_fn), out_shape=o...  238 us
    pallas_call x1, Pallas kernels, ffw(): pl.pallas_call(functools.partial(ffw_kernel, plan), out_shape=(jax.ShapeD...  139 us
    reduce_scatter x6, waiting for transfers between devices, spread(): return lax.psum_scatter(x, 'seq', scatter_dimension=0, tiled=True)  116 us
    pallas_call x7, Pallas kernels, weight_grad(): pl.pallas_call(functools.partial(weight_grad_kernel, plan), out_shape=out...  115 us
    pallas_call x1, Pallas kernels, carry(): pl.pallas_call(functools.partial(carry_kernel, seq_size), out_shape=jax.S...  79.2 us
    all_gather x1, waiting for transfers between devices, gather_weight(): return lax.all_gather(x, both, axis=0, tiled=True)  65.1 us
    pallas_call x1, Pallas kernels, front(): pl.pallas_call(functools.partial(front_kernel, plan), out_shape=(jax.Shap...  53.6 us
    pallas_call x1, Pallas kernels, hidden_back(): pl.pallas_call(functools.partial(hidden_back_kernel, len(dmixed)), grid=(...  20.2 us
  transfers between devices with their start and end apart: 8, of which 6 were waited for; matrix products, arithmetic and copies ran while one was open for 6% of the time, Pallas kernels for 49%

profile of v7, /device:TPU:0, one launch (start us, length us, event | category | flops | bytes accessed | tf_op | source)
XLA Modules:
  0.0 967.9 jit_solution(8048289885156105766)
XLA Ops:
  7.2 2.8 concatenate.30
  11.1 53.6 %shard_map.237 = (f32[8,2304]{1,0:T(8,128)}, bf16[1024,512]{1,0:T(8,128)(2,1)}, f32[1024,128]{1,0:T(8,128)}, f32[1024,128]{1,0:T(8,128)}, bf16[1024,2304]{1,0:T(8,128)(2,1)}, /*index=5*/bf16[2304,1024]{1,0:T(8,128)(2,1)}) custom-call(bf16[1024,2304]{1,0:T(8,128)(2,1)} %bitcast.42, bf16[288,512]{1,0:T(8,128)(2,1)} %wq_ref.1, bf16[288,1024]{1,0:T(8,128)(2,1)} %wk_ref.1, ...), custom_call_target="tpu_custom_call" | custom-call | tf_op jit(solution)/shard_map/pallas_call | solution.py:350
  64.8 79.2 %shard_map.239.refs_1_ = bf16[2304,512]{1,0:T(8,128)(2,1)} custom-call(bf16[288,512]{1,0:T(8,128)(2,1)} %bitcast.54), custom_call_target="tpu_custom_call" | custom-call | tf_op jit(solution)/shard_map/pallas_call | solution.py:412
  144.0 1.7 pad_maximum_fusion
  145.7 12.0 %all-gather.3.cloned.1.call-done.kv_ref = bf16[4096,512]{1,0:T(8,128)(2,1)} async-done(((bf16[1024,512]{1,0:T(8,128)(2,1)}), bf16[4096,512]{1,0:T(8,128)(2,1)}) %all-gather.3.cloned.1.call-update) | async-done | bytes 4194320 | tf_op jit(solution)/shard_map/all_gather | solution.py:1318
  157.9 0.6 fusion.5
  158.6 0.7 reshape.88.gain_ref
  159.3 1.3 constant_dynamic-slice_fusion.4
  161.3 1.5 copy.42.cotangent_ref
  162.9 2.4 dynamic-slice_bitcast_fusion.refs_2_.refs_3_
  165.2 6.0 fusion
  171.2 1.1 fusion.3
  172.9 1.6 copy.50
  174.5 1.1 multiply_subtract_fusion
  175.6 1.1 fusion.2
  176.8 1.2 copy.52
  178.0 8.1 shard_map.238
  186.1 88.4 %shard_map.240 = (f32[256,2304]{1,0:T(8,128)}, f32[256,2304]{1,0:T(8,128)}, bf16[1024,2304]{1,0:T(8,128)(2,1)}) custom-call(bf16[1024,512]{1,0:T(8,128)(2,1)} %get-tuple-element.69.refs_0_, bf16[2304,512]{1,0:T(8,128)(2,1)} %shard_map.239.refs_1_, bf16[256,2304]{1,0:T(8,128)(2,1)} %dynamic-slice_bitcast_fusion.refs_2_.refs_3_, ...), custom_call_target="tpu_custom_call" | custom-call | tf_op jit(solution)/shard_map/pallas_call | solution.py:825
  274.5 3.1 copy.36
  277.5 1.9 copy.37
  279.4 2.0 copy.41.resid_ref
  281.3 65.1 %all-gather.5.cloned.1.call-done.gate_up_ref.refs_2_ = bf16[2304,4608]{1,0:T(8,128)(2,1)} async-done(((bf16[288,4608]{1,0:T(8,128)(2,1)}), bf16[2304,4608]{1,0:T(8,128)(2,1)}) %all-gather.5.cloned.1.call-update) | async-done | bytes 21233680 | tf_op jit(solution)/shard_map/all_gather | solution.py:1305
  346.5 139.0 %shard_map.241 = (bf16[256,2304]{1,0:T(8,128)(2,1)}, f32[8,2304]{1,0:T(8,128)}, bf16[3,256,768]{2,1,0:T(8,128)(2,1)}, bf16[1024,768]{1,0:T(8,128)(2,1)}, bf16[10...) custom-call(bf16[1024,2304]{1,0:T(8,128)(2,1)} %get-tuple-element.72., ...), custom_call_target="tpu_custom_call" | custom-call | tf_op jit(solution)/shard_map/pallas_call | solution.py:1160
  485.5 9.5 shard_map.242
  495.0 30.7 %shard_map.243 = (bf16[384,4608]{1,0:T(8,128)(2,1)}, bf16[1024,768]{1,0:T(8,128)(2,1)}, bf16[1024,768]{1,0:T(8,128)(2,1)}) custom-call(bf16[3,256,768]{2,1,0:T(8,128)(2,1)} %get-tuple-element.79.refs_0_, bf16[1024,2304]{1,0:T(8,128)(2,1)} %get-tuple-element.78.refs_1_), custom_call_target="tpu_custom_call" | custom-call | tf_op jit(solution)/shard_map/pallas_call | solution.py:966
  525.8 9.4 shard_map.244
  535.2 20.2 %shard_map.245 = (bf16[1024,2304]{1,0:T(8,128)(2,1)}, bf16[1024,2304]{1,0:T(8,128)(2,1)}) custom-call(bf16[1024,768]{1,0:T(8,128)(2,1)} %get-tuple-element.82.refs_0_, bf16[1024,768]{1,0:T(8,128)(2,1)} %get-tuple-element.83.refs_1_, bf16[1024,768]{1,0:T(8,128)(2,1)} %get-tuple-element.80.refs_0_.refs_2_, bf16[2304,2304]{1,0:T(8,128)(2,1)} %get-tuple-element.84.refs_3_, ...), custom_call_target="tpu_custom_call" | custom-call | tf_op jit(solution)/shard_map/pallas_call | solution.py:1210
  555.4 38.3 %shard_map.246 = bf16[1152,4608]{1,0:T(8,128)(2,1)} custom-call(bf16[1024,2304]{1,0:T(8,128)(2,1)} %get-tuple-element.72.normed_ref.refs_0_, bf16[1024,2304]{1,0:T(8,128)(2,1)} %get-tuple-element.90.refs_1_.refs_0_, bf16[1024,2304]{1,0:T(8,128)(2,1)} %get-tuple-element.89.refs_2_.refs_1_), custom_call_target="tpu_custom_call" | custom-call | tf_op jit(solution)/shard_map/pallas_call | solution.py:966
  593.7 8.0 reduce-scatter.9.cloned.1.call-done
  602.0 2.4 fusion.10.refs_5_
  604.4 100.0 %shard_map.247 = (f32[256,2304]{1,0:T(8,128)}, f32[8,2304]{1,0:T(8,128)}, f32[8,2304]{1,0:T(8,128)}, bf16[1024,2304]{1,0:T(8,128)(2,1)}) custom-call(bf16[1024,2304]{1,0:T(8,128)(2,1)} %get-tuple-element.90.refs_1_.refs_0_, bf16[1024,2304]{1,0:T(8,128)(2,1)} %get-tuple-element.89.refs_2_.refs_1_, ...), custom_call_target="tpu_custom_call" | custom-call | tf_op jit(solution)/shard_map/pallas_call | solution.py:825
  704.5 5.0 fusion.6
  709.5 1.0 dynamic-slice_convert_fusion.3
  710.5 1.0 pad_maximum_fusion.1.do_ref
  711.6 13.4 %shard_map.248 = (f32[1024,512]{1,0:T(8,128)}, bf16[4096,512]{1,0:T(8,128)(2,1)}) custom-call(bf16[1024,512]{1,0:T(8,128)(2,1)} %bitcast.48, bf16[1024,512]{1,0:T(8,128)(2,1)} %pad_maximum_fusion.1.do_ref, f32[1024,512]{1,0:T(8,128)} %get-tuple-element.93.of_ref, f32[4,1,512]{2,1,0:T(1,128)} %get-tuple-element.94.lse_ref, ...), custom_call_target="tpu_custom_call" | custom-call | tf_op jit(solution)/shard_map/pallas_call | solution.py:551
  725.0 3.1 broadcast_multiply_fusion
  728.1 2.7 mul.124
  730.8 1.4 subtract_convert_fusion
  732.3 1.1 pad_maximum_fusion.2
  733.4 1.2 copy.53
  734.6 8.9 shard_map.250.refs_2_
  743.6 1.0 pad_maximum_fusion.3.refs_1_
  744.6 8.9 shard_map.249
  753.5 31.0 %reduce-scatter.11.cloned.1.call-done = bf16[288,4608]{1,0:T(8,128)(2,1)} async-done(((bf16[1152,4608]{1,0:T(8,128)(2,1)}), bf16[288,4608]{1,0:T(8,128)(2,1)}) %reduce-scatter.11.cloned.1.call-update) | async-done | bytes 2654224 | tf_op jit(solution)/shard_map/reduce_scatter | solution.py:1371
  784.9 0.9 copy-done.12
  785.8 1.7 convert_bitcast_fusion
  787.5 1.0 copy-done.4
  788.5 2.8 slice_convert_fusion
  791.3 73.3 %reduce-scatter.13.cloned.1.call-done = bf16[1024,512]{1,0:T(8,128)(2,1)} async-done(((bf16[4096,512]{1,0:T(8,128)(2,1)}), bf16[1024,512]{1,0:T(8,128)(2,1)}) %reduce-scatter.13.cloned.1.call-update) | async-done | bytes 1048592 | tf_op jit(solution)/shard_map/reduce_scatter | solution.py:1371
  864.6 1.5 convert_element_type.45
  866.3 1.1 pad_maximum_fusion.4.refs_1_
  867.4 9.0 shard_map.251
  876.4 49.3 %shard_map.252 = (bf16[256,2304]{1,0:T(8,128)(2,1)}, f32[8,2304]{1,0:T(8,128)}) custom-call(bf16[1024,512]{1,0:T(8,128)(2,1)} %bitcast.41, bf16[1024,512]{1,0:T(8,128)(2,1)} %pad_maximum_fusion.4.refs_1_, bf16[2304,1024]{1,0:T(8,128)(2,1)} %get-tuple-element.66.refs_2_, bf16[256,2304]{1,0:T(8,128)(2,1)} %dynamic-slice_bitcast_fusion.refs_2_.refs_3_, ...), custom_call_target="tpu_custom_call" | custom-call | tf_op jit(solution)/shard_map/pallas_call | solution.py:825
  926.0 1.0 copy-done.7
  927.7 1.5 copy.48
  929.7 0.7 pad.13.x_ref
  930.4 0.7 slice.101.kv_ref
  931.1 18.1 %shard_map.253 = (f32[8,384]{1,0:T(8,128)}, bf16[288,1024]{1,0:T(8,128)(2,1)}, bf16[288,1024]{1,0:T(8,128)(2,1)}) custom-call(f32[8,8,384]{2,1,0:T(8,128)} %pad.13.x_ref, bf16[288,512]{1,0:T(8,128)(2,1)} %slice.101.kv_ref), custom_call_target="tpu_custom_call" | custom-call | tf_op jit(solution)/shard_map/pallas_call | solution.py:141
  949.2 2.3 convert_element_type.48
  951.5 1.1 convert_element_type.50
  953.3 0.9 slice_convert_fusion.3
  954.1 3.7 reduce-scatter.17.cloned.1.call-done
  957.8 1.8 convert_bitcast_fusion.1
  959.7 1.0 copy.58
  (87 shorter events, 5.5 us)
Async XLA Ops:
  7.2 150.6 %all-gather.3.cloned.1.call-start = ((), (), s32[]{:S(2)}) async-start(), calls=%async_computation.6 | async-start | bytes 5242880 | tf_op jit(solution)/shard_map/all_gather | solution.py:1318
  10.5 0.6 copy-start.20
  64.7 79.3 %copy-start.5 = (bf16[288,2304]{1,0:T(8,128)(2,1)S(1)}, bf16[288,2304]{1,0:T(8,128)(2,1)}, u32[]{:S(2)}) copy-start(bf16[288,2304]{1,0:T(8,128)(2,1)} %param.24) | copy-start | bytes 3981316
  64.7 79.3 %copy-start.6 = (bf16[288,2304]{1,0:T(8,128)(2,1)S(1)}, bf16[288,2304]{1,0:T(8,128)(2,1)}, u32[]{:S(2)}) copy-start(bf16[288,2304]{1,0:T(8,128)(2,1)} %param.23) | copy-start | bytes 3981316
  64.7 281.7 %all-gather.5.cloned.1.call-start = ((), (), s32[]{:S(2)}) async-start(), calls=%async_computation.7 | async-start | bytes 23887872 | tf_op jit(solution)/shard_map/all_gather | solution.py:1305
  145.7 12.1 %copy-start.21 = (f32[8,2304]{1,0:T(8,128)S(1)}, f32[8,2304]{1,0:T(8,128)}, u32[]{:S(2)}) copy-start(f32[8,2304]{1,0:T(8,128)} %get-tuple-element.71) | copy-start | bytes 221188
  157.8 377.3 %reduce-scatter.7.cloned.1.call-start = ((), (), s32[]{:S(2)}) async-start(), calls=%async_computation.8 | async-start | bytes 2211840 | tf_op jit(solution)/shard_map/reduce_scatter | solution.py:1371
  172.3 2.2 copy-start.1
  172.3 2.2 copy-start.2
  495.0 106.8 %reduce-scatter.9.cloned.1.call-start = ((), (), s32[]{:S(2)}) async-start(), calls=%async_computation.9 | async-start | bytes 4423680 | tf_op jit(solution)/shard_map/reduce_scatter | solution.py:1371
  535.2 249.4 %reduce-scatter.11.cloned.1.call-start = ((), (), s32[]{:S(2)}) async-start(), calls=%async_computation.10 | async-start | bytes 13271040 | tf_op jit(solution)/shard_map/reduce_scatter | solution.py:1371
  601.8 262.7 %reduce-scatter.13.cloned.1.call-start = ((), (), s32[]{:S(2)}) async-start(), calls=%async_computation.11 | async-start | bytes 5242880 | tf_op jit(solution)/shard_map/reduce_scatter | solution.py:1371
  604.4 100.1 %copy-start = (bf16[2304,512]{1,0:T(8,128)(2,1)S(1)}, bf16[2304,512]{1,0:T(8,128)(2,1)}, u32[]{:S(2)}) copy-start(bf16[2304,512]{1,0:T(8,128)(2,1)} %shard_map.239.refs_1_) | copy-start | bytes 7077892
  704.5 5.1 copy-start.3
  734.6 8.9 copy-start.9
  734.6 8.9 copy-start.10
  734.6 8.9 copy-start.11
  784.6 1.2 copy-start.12
  784.6 1.3 copy-start.15
  784.6 141.1 %reduce-scatter.15.cloned.1.call-start = ((), (), s32[]{:S(2)}) async-start(), calls=%async_computation.12 | async-start | bytes 2949120 | tf_op jit(solution)/shard_map/reduce_scatter | solution.py:1371
  785.8 2.7 copy-start.4
  876.4 81.4 %reduce-scatter.17.cloned.1.call-start = ((), (), s32[]{:S(2)}) async-start(), calls=%async_computation.13 | async-start | bytes 1474560 | tf_op jit(solution)/shard_map/reduce_scatter | solution.py:1371
  876.4 49.3 %copy-start.16 = (f32[8,2304]{1,0:T(8,128)S(1)}, f32[8,2304]{1,0:T(8,128)}, u32[]{:S(2)}) copy-start(f32[8,2304]{1,0:T(8,128)} %get-tuple-element.106) | copy-start | bytes 221188
  925.7 1.3 copy-start.7
  927.6 1.7 copy-start.18
  927.6 1.8 copy-start.17
  927.6 1.9 copy-start.19
  927.6 2.7 copy-start.14
  949.2 2.3 copy-start.13
  949.2 3.4 copy-start.22
  951.5 8.2 copy-start.8
Sparse Core Ops, SparseCore 0:
  64.9 92.8 all-gather.2
  160.0 186.4 all-gather.4
  495.1 38.3 reduce-scatter.6
  535.8 65.9 reduce-scatter.8
  604.1 180.4 reduce-scatter.10
  786.7 77.7 reduce-scatter.12
  876.5 48.5 reduce-scatter.14
  927.5 30.2 reduce-scatter.16
